TPU v7x, 32 devices: a whole 2x2x4 slice. The times are simulated.
32 devices in a mesh: seq: 4 (over y, x), dp: 8 (over z, core).
Axes of the slice: x: 2, y: 2, z: 4, core: 2. Of those that a mesh axis runs over, the one named last changes fastest.
Arguments:
- queries: bfloat16 [8, 512, 2048], P('dp', 'seq'), may hold values from -6 to 6
- key_rows: bfloat16 [8, 512, 2048], P('dp', 'seq'), may hold values from -6 to 6
- values: bfloat16 [8, 512, 2048], P('dp', 'seq'), may hold values from -6 to 6
- cotangent: bfloat16 [8, 512, 2048], P('dp', 'seq'), may hold values from -6 to 6
- slice_ids: int32 [8, 512], P('dp', 'seq'), may hold values from 0 to 1, never falling along the last dimension, each value on 1 to 400 neighbouring positions
- query_gain: float32 [128], replicated, may hold values from 0.1 to 1.9
- key_gain: float32 [128], replicated, may hold values from 0.1 to 1.9
Outputs:
- attended: bfloat16 [8, 512, 2048], P('dp', 'seq')
- query_grad: bfloat16 [8, 512, 2048], P('dp', 'seq')
- key_grad: bfloat16 [8, 512, 2048], P('dp', 'seq')
- value_grad: bfloat16 [8, 512, 2048], P('dp', 'seq')
- query_gain_grad: float32 [128], replicated
- key_gain_grad: float32 [128], replicated
Inputs may be any that keep to these rules, and one draw needn't show every extreme that they name: `slice_ids`: within each packed sequence the slice numbers never fall, and each slice holds 1 to 400 rows.
All inputs are finite; a program needn't handle non-finite values.
Results may differ from a plain program's by a relative error of at most 0.0086.
Values may be sent and summed in bfloat16 or wider, within the bound.
No kernel may reach another device: no remote copies, remote signals or barrier semaphores. Data moves between devices by JAX's collectives and lax.ppermute only.
A program may use at most 64 MiB of HBM per device.

v0:
```python
import math

import jax
import jax.numpy as jnp
from jax import lax
from jax.sharding import PartitionSpec as P

HEAD_DIM = 128


def normalize(rows, gain):
    floats = rows.astype(jnp.float32)
    inv_rms = lax.rsqrt(jnp.mean(floats * floats, axis=-1, keepdims=True) + 1e-06)
    normed = floats * inv_rms
    return (normed, inv_rms, (normed * gain).astype(jnp.bfloat16))


def norm_back(grad_out, normed, inv_rms, gain):
    grad_normed = grad_out * gain
    inner_mean = jnp.mean(grad_normed * normed, axis=-1, keepdims=True)
    grad_rows = (inv_rms * (grad_normed - normed * inner_mean)).astype(jnp.bfloat16)
    return (grad_rows, jnp.sum(grad_out * normed, axis=0))


def attend_head(queries, key_rows, values, cotangent, slice_ids, query_gain, key_gain):
    length = queries.shape[0]
    block_rows = math.gcd(length, 512)
    blocks_count = length // block_rows
    score_scale = HEAD_DIM ** (-0.5)
    q_normed, q_inv, q_ready = normalize(queries, query_gain)
    k_normed, k_inv, k_ready = normalize(key_rows, key_gain)

    def one_block(carry, inputs):
        value_acc, key_acc = carry
        q_block, grad_block, ids_block = inputs
        scores = jnp.dot(q_block, k_ready.T, preferred_element_type=jnp.float32) * score_scale
        same = ids_block[:, None] == slice_ids[None, :]
        weights = jnp.where(same, jnp.exp(scores), jnp.zeros_like(scores))
        probs = weights / jnp.sum(weights, axis=1, keepdims=True)
        probs_low = probs.astype(jnp.bfloat16)
        attended = jnp.dot(probs_low, values, preferred_element_type=jnp.float32).astype(
            jnp.bfloat16
        )
        row_inner = jnp.sum(
            grad_block.astype(jnp.float32) * attended.astype(jnp.float32), axis=1, keepdims=True
        )
        grad_probs = jnp.dot(grad_block, values.T, preferred_element_type=jnp.float32)
        grad_scores = (probs * (grad_probs - row_inner) * score_scale).astype(jnp.bfloat16)
        value_acc = value_acc + jnp.dot(probs_low.T, grad_block, preferred_element_type=jnp.float32)
        key_acc = key_acc + jnp.dot(grad_scores.T, q_block, preferred_element_type=jnp.float32)
        query_part = jnp.dot(grad_scores, k_ready, preferred_element_type=jnp.float32)
        return ((value_acc, key_acc), (attended, query_part))

    zeros = jnp.zeros((length, queries.shape[1]), jnp.float32)
    inputs = (
        q_ready.reshape(blocks_count, block_rows, -1),
        cotangent.reshape(blocks_count, block_rows, -1),
        slice_ids.reshape(blocks_count, block_rows),
    )
    (value_acc, key_acc), (attended, query_part) = lax.scan(one_block, (zeros, zeros), inputs)
    attended = attended.reshape(length, -1)
    query_part = query_part.reshape(length, -1)
    query_grad, q_gain_part = norm_back(query_part, q_normed, q_inv, query_gain)
    key_grad, k_gain_part = norm_back(key_acc, k_normed, k_inv, key_gain)
    return (
        attended,
        query_grad,
        key_grad,
        value_acc.astype(jnp.bfloat16),
        q_gain_part,
        k_gain_part,
    )


def per_device(queries, key_rows, values, cotangent, slice_ids, query_gain, key_gain):
    rows = queries.shape[1]
    width = queries.shape[2]
    groups = lax.axis_size("seq")
    local_heads = width // HEAD_DIM // groups
    all_ids = lax.all_gather(slice_ids, "seq", axis=1, tiled=True)[0]

    def to_blocks(tensor):
        return tensor[0].reshape(rows, groups, local_heads, HEAD_DIM)

    pieces = (
        lax.all_to_all(to_blocks(queries), "seq", split_axis=1, concat_axis=0, tiled=True),
        lax.all_to_all(to_blocks(key_rows), "seq", split_axis=1, concat_axis=0, tiled=True),
        lax.all_to_all(to_blocks(values), "seq", split_axis=1, concat_axis=0, tiled=True),
        lax.all_to_all(to_blocks(cotangent), "seq", split_axis=1, concat_axis=0, tiled=True),
    )
    count = pieces[0].shape[2]

    def flatten(tensor):
        return tensor[:, 0].transpose(1, 0, 2)

    def run(items):
        return attend_head(items[0], items[1], items[2], items[3], all_ids, query_gain, key_gain)

    results = lax.map(
        run, (flatten(pieces[0]), flatten(pieces[1]), flatten(pieces[2]), flatten(pieces[3]))
    )

    def unflatten(tensor):
        return tensor.transpose(1, 0, 2)[:, None]

    first = unflatten(results[0])
    second = unflatten(results[1])
    third = unflatten(results[2])
    fourth = unflatten(results[3])
    outcome = (
        first,
        second,
        third,
        fourth,
        results[4].reshape(1, 1, count, HEAD_DIM),
        results[5].reshape(1, 1, count, HEAD_DIM),
    )
    first, second, third, fourth = (outcome[0], outcome[1], outcome[2], outcome[3])
    first, second, third, fourth = (
        lax.all_to_all(first, "seq", split_axis=0, concat_axis=1, tiled=True),
        lax.all_to_all(second, "seq", split_axis=0, concat_axis=1, tiled=True),
        lax.all_to_all(third, "seq", split_axis=0, concat_axis=1, tiled=True),
        lax.all_to_all(fourth, "seq", split_axis=0, concat_axis=1, tiled=True),
    )
    query_part = jnp.sum(outcome[4], axis=(0, 1, 2))
    key_part = jnp.sum(outcome[5], axis=(0, 1, 2))
    query_total, key_total = lax.psum((query_part, key_part), ("seq", "dp"))

    def to_rows(tensor):
        return tensor.reshape(1, rows, width)

    return (
        to_rows(first),
        to_rows(second),
        to_rows(third),
        to_rows(fourth),
        query_total,
        key_total,
    )


def solution(mesh):
    return jax.shard_map(
        per_device,
        mesh=mesh,
        in_specs=(
            P("dp", "seq", None),
            P("dp", "seq", None),
            P("dp", "seq", None),
            P("dp", "seq", None),
            P("dp", "seq"),
            P(),
            P(),
        ),
        out_specs=(
            P("dp", "seq", None),
            P("dp", "seq", None),
            P("dp", "seq", None),
            P("dp", "seq", None),
            P(),
            P(),
        ),
        check_vma=False,
    )
```

profile of v0, /device:TPU:0, one launch (start us, length us, event | category | flops | bytes accessed | tf_op | source)
XLA Modules:
  0.0 156.0 jit_solution(5254197184067538955)
XLA Ops:
  0.6 1.3 copy.39
  1.9 1.0 copy.40
  3.0 5.3 %all-to-all-start = ((bf16[128,4,4,128]{3,0,2,1:T(8,128)(2,1)}), bf16[128,4,4,128]{3,0,2,1:T(8,128)(2,1)S(1)}, u32[]{:S(2)}, u32[]{:S(2)}) async-start(bf16[128,4,4,128]{3,0,2,1:T(8,128)(2,1)} %copy.40), calls=%async_computation | async-start | bytes 1048576 | tf_op jit(solution)/shard_map/all_to_all | solution.py:86
  8.5 1.0 copy.43
  9.6 6.7 %all-to-all-done = bf16[128,4,4,128]{3,0,2,1:T(8,128)(2,1)S(1)} async-done(((bf16[128,4,4,128]{3,0,2,1:T(8,128)(2,1)}), bf16[128,4,4,128]{3,0,2,1:T(8,128)(2,1)S(1)}, u32[]{:S(2)}, u32[]{:S(2)}) %all-to-all-start) | async-done | bytes 524320 | tf_op jit(solution)/shard_map/all_to_all | solution.py:86
  16.3 3.5 %all-to-all-start.1 = ((bf16[128,4,4,128]{3,0,2,1:T(8,128)(2,1)}), bf16[128,4,4,128]{3,0,2,1:T(8,128)(2,1)S(1)}, u32[]{:S(2)}, u32[]{:S(2)}) async-start(bf16[128,4,4,128]{3,0,2,1:T(8,128)(2,1)} %copy.43), calls=%async_computation.1 | async-start | bytes 1048576 | tf_op jit(solution)/shard_map/all_to_all | solution.py:87
  20.0 1.0 copy.46
  21.1 5.8 %all-to-all-done.1 = bf16[128,4,4,128]{3,0,2,1:T(8,128)(2,1)S(1)} async-done(((bf16[128,4,4,128]{3,0,2,1:T(8,128)(2,1)}), bf16[128,4,4,128]{3,0,2,1:T(8,128)(2,1)S(1)}, u32[]{:S(2)}, u32[]{:S(2)}) %all-to-all-start.1) | async-done | bytes 524320 | tf_op jit(solution)/shard_map/all_to_all | solution.py:87
  26.9 3.5 %all-to-all-start.2 = ((bf16[128,4,4,128]{3,0,2,1:T(8,128)(2,1)}), bf16[128,4,4,128]{3,0,2,1:T(8,128)(2,1)S(1)}, u32[]{:S(2)}, u32[]{:S(2)}) async-start(bf16[128,4,4,128]{3,0,2,1:T(8,128)(2,1)} %copy.46), calls=%async_computation.2 | async-start | bytes 1048576 | tf_op jit(solution)/shard_map/all_to_all | solution.py:88
  30.4 1.0 copy.48
  31.4 5.5 %all-to-all-done.2 = bf16[128,4,4,128]{3,0,2,1:T(8,128)(2,1)S(1)} async-done(((bf16[128,4,4,128]{3,0,2,1:T(8,128)(2,1)}), bf16[128,4,4,128]{3,0,2,1:T(8,128)(2,1)S(1)}, u32[]{:S(2)}, u32[]{:S(2)}) %all-to-all-start.2) | async-done | bytes 524320 | tf_op jit(solution)/shard_map/all_to_all | solution.py:88
  36.9 3.5 %all-to-all-start.3 = ((bf16[128,4,4,128]{0,3,2,1:T(8,128)(2,1)}), bf16[128,4,4,128]{0,3,2,1:T(8,128)(2,1)S(1)}, u32[]{:S(2)}, u32[]{:S(2)}) async-start(bf16[128,4,4,128]{0,3,2,1:T(8,128)(2,1)} %bitcast.28), calls=%async_computation.3 | async-start | bytes 1048576 | tf_op jit(solution)/shard_map/all_to_all | solution.py:89
  41.1 8.4 %all_gather.3 = s32[1,512]{1,0:T(1,128)S(1)} all-gather(s32[1,128]{1,0:T(1,128)S(1)} %copy-done.8), channel_id=1, replica_groups=mesh['seq'=4,'dp'=8] {'seq'}, dimensions={1}, use_global_device_ids=true | all-gather | bytes 2560 | tf_op jit(solution)/shard_map/all_gather | solution.py:80
  51.5 21.5 %while.18 = (s32[]{:T(128)}, bf16[4,512,128]{1,2,0:T(8,128)(2,1)}, bf16[4,512,128]{2,1,0:T(8,128)(2,1)}, bf16[4,512,128]{2,1,0:T(8,128)(2,1)}, bf16[4,512,128]{2...) while((s32[]{:T(128)}, bf16[4,512,128]{1,2,0:T(8,128)(2,1)}, ...), condition=%wide.region_9.10_spmd, body=%wide.region_0.9_spmd.sunk | while | flops 409730816 | bytes 10167477 | solution.py:99
  52.7 0.9 bitcast_dynamic-update-slice_fusion.2
  63.5 0.9 bitcast_dynamic-update-slice_fusion.2
  73.0 2.1 %copy.54 = bf16[4,512,128]{2,0,1:T(4,128)(2,1)} copy(bf16[4,512,128]{1,2,0:T(8,128)(2,1)} %get-tuple-element.113) | data formatting | bytes 1048576 | tf_op jit(solution)/shard_map/while | solution.py:99
  75.1 3.6 %all-to-all-start.4 = ((bf16[512,1,4,128]{3,2,1,0:T(4,128)(2,1)}), bf16[512,1,4,128]{3,2,1,0:T(4,128)(2,1)S(1)}, u32[]{:S(2)}, u32[]{:S(2)}) async-start(bf16[512,1,4,128]{3,2,1,0:T(4,128)(2,1)} %bitcast.34), calls=%async_computation.4 | async-start | bytes 1048576 | tf_op jit(solution)/shard_map/all_to_all | solution.py:120
  78.7 1.2 copy.69
  79.9 5.3 %all-to-all-done.4 = bf16[512,1,4,128]{3,2,1,0:T(4,128)(2,1)S(1)} async-done(((bf16[512,1,4,128]{3,2,1,0:T(4,128)(2,1)}), bf16[512,1,4,128]{3,2,1,0:T(4,128)(2,1)S(1)}, u32[]{:S(2)}, u32[]{:S(2)}) %all-to-all-start.4) | async-done | bytes 524320 | tf_op jit(solution)/shard_map/all_to_all | solution.py:120
  85.2 3.6 %all-to-all-start.5 = ((bf16[512,1,4,128]{3,2,1,0:T(4,128)(2,1)}), bf16[512,1,4,128]{3,2,1,0:T(4,128)(2,1)S(1)}, u32[]{:S(2)}, u32[]{:S(2)}) async-start(bf16[512,1,4,128]{3,2,1,0:T(4,128)(2,1)} %bitcast.183), calls=%async_computation.5 | async-start | bytes 1048576 | tf_op jit(solution)/shard_map/all_to_all | solution.py:121
  88.9 1.2 copy.68
  90.1 5.3 %all-to-all-done.5 = bf16[512,1,4,128]{3,2,1,0:T(4,128)(2,1)S(1)} async-done(((bf16[512,1,4,128]{3,2,1,0:T(4,128)(2,1)}), bf16[512,1,4,128]{3,2,1,0:T(4,128)(2,1)S(1)}, u32[]{:S(2)}, u32[]{:S(2)}) %all-to-all-start.5) | async-done | bytes 524320 | tf_op jit(solution)/shard_map/all_to_all | solution.py:121
  95.4 3.5 %all-to-all-start.6 = ((bf16[512,1,4,128]{3,2,1,0:T(4,128)(2,1)}), bf16[512,1,4,128]{3,2,1,0:T(4,128)(2,1)S(1)}, u32[]{:S(2)}, u32[]{:S(2)}) async-start(bf16[512,1,4,128]{3,2,1,0:T(4,128)(2,1)} %bitcast.182), calls=%async_computation.6 | async-start | bytes 1048576 | tf_op jit(solution)/shard_map/all_to_all | solution.py:122
  98.9 1.2 copy.67
  100.1 6.0 %all-to-all-done.6 = bf16[512,1,4,128]{3,2,1,0:T(4,128)(2,1)S(1)} async-done(((bf16[512,1,4,128]{3,2,1,0:T(4,128)(2,1)}), bf16[512,1,4,128]{3,2,1,0:T(4,128)(2,1)S(1)}, u32[]{:S(2)}, u32[]{:S(2)}) %all-to-all-start.6) | async-done | bytes 524320 | tf_op jit(solution)/shard_map/all_to_all | solution.py:122
  106.1 3.5 %all-to-all-start.7 = ((bf16[512,1,4,128]{3,2,1,0:T(4,128)(2,1)}), bf16[512,1,4,128]{3,2,1,0:T(4,128)(2,1)S(1)}, u32[]{:S(2)}, u32[]{:S(2)}) async-start(bf16[512,1,4,128]{3,2,1,0:T(4,128)(2,1)} %bitcast.181), calls=%async_computation.7 | async-start | bytes 1048576 | tf_op jit(solution)/shard_map/all_to_all | solution.py:123
  109.6 40.9 %all-reduce = (f32[128]{0:T(128)}, f32[128]{0:T(128)}) all-reduce(f32[128]{0:T(128)S(1)} %reduce_sum.92, f32[128]{0:T(128)S(1)} %reduce_sum.93), channel_id=1, replica_groups=mesh['seq'=4,'dp'=8] {'seq','dp'}, use_global_device_ids=true, to_apply=%region_11.12 | all-reduce | flops 256 | bytes 2048 | tf_op jit(solution)/shard_map/psum | solution.py:127
  150.7 1.2 reshape.105
  152.1 1.2 reshape.106
  153.5 1.2 reshape.107
  154.8 1.2 reshape.108
  (108 shorter events, 23.3 us)
Async XLA Ops:
  3.0 5.3 %copy-start = (bf16[1,128,2048]{2,1,0:T(8,128)(2,1)S(1)}, bf16[1,128,2048]{2,1,0:T(8,128)(2,1)}, u32[]{:S(2)}) copy-start(bf16[1,128,2048]{2,1,0:T(8,128)(2,1)} %param.10) | copy-start | bytes 1572868
  3.0 13.3 %all-to-all-start = ((bf16[128,4,4,128]{3,0,2,1:T(8,128)(2,1)}), bf16[128,4,4,128]{3,0,2,1:T(8,128)(2,1)S(1)}, u32[]{:S(2)}, u32[]{:S(2)}) async-start(bf16[128,4,4,128]{3,0,2,1:T(8,128)(2,1)} %copy.40), calls=%async_computation | async-start | bytes 1048576 | tf_op jit(solution)/shard_map/all_to_all | solution.py:86
  9.6 10.2 %copy-start.1 = (bf16[1,128,2048]{2,1,0:T(8,128)(2,1)S(1)}, bf16[1,128,2048]{2,1,0:T(8,128)(2,1)}, u32[]{:S(2)}) copy-start(bf16[1,128,2048]{2,1,0:T(8,128)(2,1)} %param.11) | copy-start | bytes 1572868
  16.3 10.6 %all-to-all-start.1 = ((bf16[128,4,4,128]{3,0,2,1:T(8,128)(2,1)}), bf16[128,4,4,128]{3,0,2,1:T(8,128)(2,1)S(1)}, u32[]{:S(2)}, u32[]{:S(2)}) async-start(bf16[128,4,4,128]{3,0,2,1:T(8,128)(2,1)} %copy.43), calls=%async_computation.1 | async-start | bytes 1048576 | tf_op jit(solution)/shard_map/all_to_all | solution.py:87
  21.1 9.3 %copy-start.2 = (bf16[1,128,2048]{2,1,0:T(8,128)(2,1)S(1)}, bf16[1,128,2048]{2,1,0:T(8,128)(2,1)}, u32[]{:S(2)}) copy-start(bf16[1,128,2048]{2,1,0:T(8,128)(2,1)} %param.12) | copy-start | bytes 1572868
  26.9 10.0 %all-to-all-start.2 = ((bf16[128,4,4,128]{3,0,2,1:T(8,128)(2,1)}), bf16[128,4,4,128]{3,0,2,1:T(8,128)(2,1)S(1)}, u32[]{:S(2)}, u32[]{:S(2)}) async-start(bf16[128,4,4,128]{3,0,2,1:T(8,128)(2,1)} %copy.46), calls=%async_computation.2 | async-start | bytes 1048576 | tf_op jit(solution)/shard_map/all_to_all | solution.py:88
  36.9 13.5 %all-to-all-start.3 = ((bf16[128,4,4,128]{0,3,2,1:T(8,128)(2,1)}), bf16[128,4,4,128]{0,3,2,1:T(8,128)(2,1)S(1)}, u32[]{:S(2)}, u32[]{:S(2)}) async-start(bf16[128,4,4,128]{0,3,2,1:T(8,128)(2,1)} %bitcast.28), calls=%async_computation.3 | async-start | bytes 1048576 | tf_op jit(solution)/shard_map/all_to_all | solution.py:89
  40.4 0.7 copy-start.8
  50.4 1.0 copy-start.3
  50.7 0.8 copy-start.6
  50.7 0.7 copy-start.7
  75.1 3.6 %copy-start.5 = (bf16[4,512,128]{2,1,0:T(8,128)(2,1)S(1)}, bf16[4,512,128]{2,1,0:T(8,128)(2,1)}, u32[]{:S(2)}) copy-start(bf16[4,512,128]{2,1,0:T(8,128)(2,1)} %get-tuple-element.114) | copy-start | bytes 1572868
  75.1 10.2 %all-to-all-start.4 = ((bf16[512,1,4,128]{3,2,1,0:T(4,128)(2,1)}), bf16[512,1,4,128]{3,2,1,0:T(4,128)(2,1)S(1)}, u32[]{:S(2)}, u32[]{:S(2)}) async-start(bf16[512,1,4,128]{3,2,1,0:T(4,128)(2,1)} %bitcast.34), calls=%async_computation.4 | async-start | bytes 1048576 | tf_op jit(solution)/shard_map/all_to_all | solution.py:120
  85.2 3.6 %copy-start.4 = (bf16[4,512,128]{2,1,0:T(8,128)(2,1)S(1)}, bf16[4,512,128]{2,1,0:T(8,128)(2,1)}, u32[]{:S(2)}) copy-start(bf16[4,512,128]{2,1,0:T(8,128)(2,1)} %get-tuple-element.115) | copy-start | bytes 1572868
  85.2 10.2 %all-to-all-start.5 = ((bf16[512,1,4,128]{3,2,1,0:T(4,128)(2,1)}), bf16[512,1,4,128]{3,2,1,0:T(4,128)(2,1)S(1)}, u32[]{:S(2)}, u32[]{:S(2)}) async-start(bf16[512,1,4,128]{3,2,1,0:T(4,128)(2,1)} %bitcast.183), calls=%async_computation.5 | async-start | bytes 1048576 | tf_op jit(solution)/shard_map/all_to_all | solution.py:121
  95.4 10.7 %all-to-all-start.6 = ((bf16[512,1,4,128]{3,2,1,0:T(4,128)(2,1)}), bf16[512,1,4,128]{3,2,1,0:T(4,128)(2,1)S(1)}, u32[]{:S(2)}, u32[]{:S(2)}) async-start(bf16[512,1,4,128]{3,2,1,0:T(4,128)(2,1)} %bitcast.182), calls=%async_computation.6 | async-start | bytes 1048576 | tf_op jit(solution)/shard_map/all_to_all | solution.py:122
  106.1 48.6 %all-to-all-start.7 = ((bf16[512,1,4,128]{3,2,1,0:T(4,128)(2,1)}), bf16[512,1,4,128]{3,2,1,0:T(4,128)(2,1)S(1)}, u32[]{:S(2)}, u32[]{:S(2)}) async-start(bf16[512,1,4,128]{3,2,1,0:T(4,128)(2,1)} %bitcast.181), calls=%async_computation.7 | async-start | bytes 1048576 | tf_op jit(solution)/shard_map/all_to_all | solution.py:123
where the time goes:
time: 157 us; the launch traced here: 156 us
  blocking collectives  49.3 us (31%)
  waiting for transfers between devices  34.8 us (22%)
  starting transfers between devices  29.9 us (19%)
  local copies, waits for them, and re-layouts  20.5 us (13%)
  matrix products  12.4 us (8%)
  other arithmetic  8.1 us (5%)
    psum x1, blocking collectives, per_device(): query_total, key_total = lax.psum((query_part, key_part), ('seq', 'dp'))  40.9 us
    all_gather x1, blocking collectives, per_device(): all_ids = lax.all_gather(slice_ids, 'seq', axis=1, tiled=True)[0]  8.39 us
    dynamic_update_slice x8, other arithmetic, per_device(): lax.map(run, (flatten(pieces[0]), flatten(pieces[1]), flatten(pieces[2]),...  6.9 us
    all_to_all x1, waiting for transfers between devices, per_device(): lax.all_to_all(to_blocks(queries), 'seq', split_axis=1, concat_axis=0, ti...  6.72 us
    all_to_all x1, waiting for transfers between devices, per_device(): lax.all_to_all(third, 'seq', split_axis=0, concat_axis=1, tiled=True)  6.02 us
    all_to_all x1, waiting for transfers between devices, per_device(): lax.all_to_all(to_blocks(key_rows), 'seq', split_axis=1, concat_axis=0, t...  5.81 us
    while x4, local copies, waits for them, and re-layouts, per_device(): lax.map(run, (flatten(pieces[0]), flatten(pieces[1]), flatten(pieces[2]),...  5.7 us
    all_to_all x1, waiting for transfers between devices, per_device(): lax.all_to_all(to_blocks(values), 'seq', split_axis=1, concat_axis=0, til...  5.54 us
  transfers between devices with their start and end apart: 8, of which 6 were waited for; matrix products, arithmetic and copies ran while one was open for 8% of the time, Pallas kernels for 0%

commit v1 on v0

v1 whole, which is shorter than its diff:
```python
import functools

import jax
import jax.numpy as jnp
from jax import lax
from jax.experimental import pallas as pl
from jax.experimental.pallas import tpu as pltpu
from jax.sharding import PartitionSpec as P

HEAD_DIM = 128
EPS = 1e-06
TENSORS = 4
ID_ROWS = 16
SCALE = HEAD_DIM ** (-0.5)
VMEM_BYTES = 56 * 1024 * 1024


def dot(a, b, contract):
    return lax.dot_general(
        a, b, ((contract[:1], contract[1:]), ((), ())), preferred_element_type=jnp.float32
    )


def normalize(rows, gain):
    floats = rows.astype(jnp.float32)
    inv_rms = lax.rsqrt(jnp.mean(floats * floats, axis=-1, keepdims=True) + EPS)
    normed = floats * inv_rms
    return normed, inv_rms, (normed * gain).astype(jnp.bfloat16)


def norm_back(grad_out, normed, inv_rms, gain):
    grad_normed = grad_out * gain
    inner_mean = jnp.mean(grad_normed * normed, axis=-1, keepdims=True)
    grad_rows = (inv_rms * (grad_normed - normed * inner_mean)).astype(jnp.bfloat16)
    return grad_rows, jnp.sum(grad_out * normed, axis=0, keepdims=True)


def pack_kernel(groups, local, chunk, width, with_ids, me_ref, *refs):
    tensors, rest = refs[:TENSORS], refs[TENSORS:]
    if with_ids:
        ids_ref, rest = rest[0], rest[1:]
    outs, sems = rest[:groups], rest[groups]
    rows = tensors[0].shape[1]
    copies = []
    for shift in range(groups):
        owner = jnp.bitwise_xor(me_ref[0], shift)
        start = pl.multiple_of(owner * local + chunk * width, HEAD_DIM)
        for t in range(TENSORS):
            copies.append((
                tensors[t].at[0, :, pl.ds(start, width)],
                outs[shift].at[pl.ds(t * rows, rows), :],
            ))
        if with_ids:
            copies.append((ids_ref, outs[shift].at[pl.ds(TENSORS * rows, ID_ROWS), :]))
    started = [
        pltpu.make_async_copy(source, target, sems.at[i])
        for i, (source, target) in enumerate(copies)
    ]
    for copy in started:
        copy.start()
    for copy in started:
        copy.wait()


def pack(me, arrays, ids_block, groups, local, chunk, width):
    rows = arrays[0].shape[1]
    with_ids = ids_block is not None
    height = TENSORS * rows + (ID_ROWS if with_ids else 0)
    count = groups * (TENSORS + (1 if with_ids else 0))
    any_spec = pl.BlockSpec(memory_space=pl.ANY)
    operands = (me,) + tuple(arrays) + ((ids_block,) if with_ids else ())
    return pl.pallas_call(
        functools.partial(pack_kernel, groups, local, chunk, width, with_ids),
        out_shape=[jax.ShapeDtypeStruct((height, width), jnp.bfloat16)] * groups,
        in_specs=[pl.BlockSpec(memory_space=pltpu.SMEM)] + [any_spec] * (len(operands) - 1),
        out_specs=[any_spec] * groups,
        scratch_shapes=[pltpu.SemaphoreType.DMA((count,))],
        name=f"pack{chunk}",
    )(*operands)


def unpack_kernel(groups, local, chunk, width, aliased, me_ref, *refs):
    pieces, rest = refs[:groups], refs[groups:]
    if aliased:
        rest = rest[TENSORS:]
    outs, sems = rest[:TENSORS], rest[TENSORS]
    rows = outs[0].shape[1]
    started = []
    for shift in range(groups):
        owner = jnp.bitwise_xor(me_ref[0], shift)
        start = pl.multiple_of(owner * local + chunk * width, HEAD_DIM)
        for t in range(TENSORS):
            started.append(
                pltpu.make_async_copy(
                    pieces[shift].at[pl.ds(t * rows, rows), :],
                    outs[t].at[0, :, pl.ds(start, width)],
                    sems.at[shift * TENSORS + t],
                )
            )
    for copy in started:
        copy.start()
    for copy in started:
        copy.wait()


def unpack(me, pieces, previous, shape, local, chunk, width):
    groups = len(pieces)
    aliased = previous is not None
    any_spec = pl.BlockSpec(memory_space=pl.ANY)
    operands = (me,) + tuple(pieces) + (tuple(previous) if aliased else ())
    aliases = {1 + groups + t: t for t in range(TENSORS)} if aliased else {}
    return pl.pallas_call(
        functools.partial(unpack_kernel, groups, local, chunk, width, aliased),
        out_shape=[jax.ShapeDtypeStruct(shape, jnp.bfloat16)] * TENSORS,
        in_specs=[pl.BlockSpec(memory_space=pltpu.SMEM)] + [any_spec] * (len(operands) - 1),
        out_specs=[any_spec] * TENSORS,
        scratch_shapes=[pltpu.SemaphoreType.DMA((groups * TENSORS,))],
        input_output_aliases=aliases,
        name=f"unpack{chunk}",
    )(*operands)


def attend_kernel(groups, rows, heads, block, *refs):
    pieces, ids, rest = refs[:groups], refs[groups : 2 * groups], refs[2 * groups :]
    gain_refs, outs, gain_out = rest[:2], rest[2 : 2 + groups], rest[2 + groups]
    length = groups * rows
    query_gain, key_gain = gain_refs[0][...], gain_refs[1][...]
    ids_row = jnp.concatenate([ref[0:1, 0:rows].astype(jnp.float32) for ref in ids], axis=1)
    ids_col = jnp.broadcast_to(ids_row, (HEAD_DIM, length)).T[:, 0:1]
    gain_parts = [jnp.zeros((1, HEAD_DIM), jnp.float32)] * 2
    for head in range(heads):
        cols = slice(head * HEAD_DIM, (head + 1) * HEAD_DIM)

        def gather(t):
            return jnp.concatenate(
                [ref[t * rows : (t + 1) * rows, cols] for ref in pieces], axis=0
            )

        q_normed, q_inv, q_ready = normalize(gather(0), query_gain)
        k_normed, k_inv, k_ready = normalize(gather(1), key_gain)
        values, cotangent = gather(2), gather(3)
        value_acc = key_acc = None
        attended_parts, query_parts = [], []
        for start in range(0, length, block):
            part = slice(start, start + block)
            q_block, grad_block = q_ready[part], cotangent[part]
            scores = dot(q_block, k_ready, (1, 1)) * SCALE
            weights = jnp.where(ids_col[part] == ids_row, jnp.exp(scores), 0.0)
            probs = weights * (1.0 / jnp.sum(weights, axis=1, keepdims=True))
            probs_low = probs.astype(jnp.bfloat16)
            attended = dot(probs_low, values, (1, 0)).astype(jnp.bfloat16)
            row_inner = jnp.sum(
                grad_block.astype(jnp.float32) * attended.astype(jnp.float32),
                axis=1,
                keepdims=True,
            )
            grad_probs = dot(grad_block, values, (1, 1))
            grad_scores = (probs * (grad_probs - row_inner) * SCALE).astype(jnp.bfloat16)
            value_part = dot(probs_low, grad_block, (0, 0))
            key_part = dot(grad_scores, q_block, (0, 0))
            value_acc = value_part if value_acc is None else value_acc + value_part
            key_acc = key_part if key_acc is None else key_acc + key_part
            attended_parts.append(attended)
            query_parts.append(dot(grad_scores, k_ready, (1, 0)))
        attended = jnp.concatenate(attended_parts, axis=0)
        query_acc = jnp.concatenate(query_parts, axis=0)
        query_grad, query_sum = norm_back(query_acc, q_normed, q_inv, query_gain)
        key_grad, key_sum = norm_back(key_acc, k_normed, k_inv, key_gain)
        gain_parts = [gain_parts[0] + query_sum, gain_parts[1] + key_sum]
        results = (attended, query_grad, key_grad, value_acc.astype(jnp.bfloat16))
        for i, out in enumerate(outs):
            for t in range(TENSORS):
                out[t * rows : (t + 1) * rows, cols] = results[t][i * rows : (i + 1) * rows]
    gain_out[0:1, :] = gain_parts[0]
    gain_out[1:2, :] = gain_parts[1]


def attend(pieces, id_holders, query_gain, key_gain, rows, heads, chunk):
    groups = len(pieces)
    width = heads * HEAD_DIM
    length = groups * rows
    height = TENSORS * rows
    block = min(length, 256)
    piece_spec = pl.BlockSpec((height, width), lambda i: (0, 0))
    ids_spec = pl.BlockSpec((ID_ROWS, HEAD_DIM), lambda i: (height // ID_ROWS, 0))
    gain_spec = pl.BlockSpec((1, HEAD_DIM), lambda i: (0, 0))
    area = length * length * heads
    outs = pl.pallas_call(
        functools.partial(attend_kernel, groups, rows, heads, block),
        grid=(1,),
        out_shape=[jax.ShapeDtypeStruct((height, width), jnp.bfloat16)] * groups
        + [jax.ShapeDtypeStruct((2, HEAD_DIM), jnp.float32)],
        in_specs=[piece_spec] * groups + [ids_spec] * groups + [gain_spec] * 2,
        out_specs=[piece_spec] * groups + [pl.BlockSpec((2, HEAD_DIM), lambda i: (0, 0))],
        compiler_params=pltpu.CompilerParams(vmem_limit_bytes=VMEM_BYTES),
        cost_estimate=pl.CostEstimate(
            flops=12 * area * HEAD_DIM,
            bytes_accessed=4 * groups * height * width,
            transcendentals=area,
        ),
        name=f"attend{chunk}",
    )(*pieces, *id_holders, query_gain, key_gain)
    return outs[:groups], outs[groups]


def permute(value, axis, size, shift):
    return lax.ppermute(value, axis, [(i, i ^ shift) for i in range(size)])


def total_over(value, axis, size):
    shift = 1
    while shift < size:
        value = value + permute(value, axis, size, shift)
        shift *= 2
    return value


def per_device(queries, key_rows, values, cotangent, slice_ids, query_gain, key_gain):
    rows, width = queries.shape[1], queries.shape[2]
    groups, batches = lax.axis_size("seq"), lax.axis_size("dp")
    local = width // groups
    chunks = 2 if local >= 2 * HEAD_DIM else 1
    chunk_width = local // chunks
    heads = chunk_width // HEAD_DIM
    me = lax.axis_index("seq").astype(jnp.int32).reshape(1)
    arrays = (queries, key_rows, values, cotangent)
    ids_block = jnp.pad(
        slice_ids.astype(jnp.bfloat16), ((0, ID_ROWS - 1), (0, chunk_width - rows))
    )
    gains = (query_gain.reshape(1, HEAD_DIM), key_gain.reshape(1, HEAD_DIM))

    received = []
    for chunk in range(chunks):
        payloads = pack(
            me, arrays, ids_block if chunk == 0 else None, groups, local, chunk, chunk_width
        )
        received.append(
            [payloads[0]]
            + [permute(payloads[shift], "seq", groups, shift) for shift in range(1, groups)]
        )
    returned, gain_total = [], None
    for chunk in range(chunks):
        results, gain_part = attend(
            received[chunk], received[0], gains[0], gains[1], rows, heads, chunk
        )
        gain_total = gain_part if gain_total is None else gain_total + gain_part
        returned.append(
            [results[0]]
            + [permute(results[shift], "seq", groups, shift) for shift in range(1, groups)]
        )
    gain_total = total_over(gain_total, "dp", batches)
    gain_total = total_over(gain_total, "seq", groups)
    outputs = None
    for chunk in range(chunks):
        outputs = unpack(me, returned[chunk], outputs, queries.shape, local, chunk, chunk_width)
    return (*outputs, gain_total[0], gain_total[1])


def solution(mesh):
    rows = P("dp", "seq", None)
    return jax.shard_map(
        per_device,
        mesh=mesh,
        in_specs=(rows, rows, rows, rows, P("dp", "seq"), P(), P()),
        out_specs=(rows, rows, rows, rows, P(), P()),
        check_vma=False,
    )
```

time: 157 us -> 198 us (1.26)
  Pallas kernels: 0 us -> 144 us
  blocking collectives: 49.3 us -> 0 us
  local copies, waits for them, and re-layouts: 20.5 us -> 5.64 us
  matrix products: 12.4 us -> 0 us
  waiting for transfers between devices: 34.8 us -> 25.2 us
  other arithmetic: 8.1 us -> 0.02 us
  starting transfers between devices: 29.9 us -> 22.1 us
    pallas_call x0 -> x6, Pallas kernels: none -> 144 us  [the longest x2 67 us: pack(): pl.pallas_call(functools.partial(pack_kernel, groups, local, chunk, width...]
    psum x1 -> x0, blocking collectives: 40.9 us -> none  [per_device(): query_total, key_total = lax.psum((query_part, key_part), ('seq', 'dp'))]
    all_to_all x8 -> x0, waiting for transfers between devices: 34.8 us -> none  [the longest x1 6.72 us: per_device(): lax.all_to_all(to_blocks(queries), 'seq', split_axis=1, concat_axis=0, ti...]
    all_to_all x8 -> x0, starting transfers between devices: 29.9 us -> none  [the longest x1 5.29 us: per_device(): lax.all_to_all(to_blocks(queries), 'seq', split_axis=1, concat_axis=0, ti...]
    ppermute x0 -> x17, waiting for transfers between devices: none -> 25.2 us  [permute(): return lax.ppermute(value, axis, [(i, i ^ shift) for i in range(size)])]
    ppermute x0 -> x17, starting transfers between devices: none -> 22.1 us  [permute(): return lax.ppermute(value, axis, [(i, i ^ shift) for i in range(size)])]
    dot_general x24 -> x0, matrix products: 12.4 us -> none  [the longest x4 3.78 us: one_block(): jnp.dot(probs_low, values, preferred_element_type=jnp.float32)]
    all_gather x1 -> x0, blocking collectives: 8.39 us -> none  [per_device(): all_ids = lax.all_gather(slice_ids, 'seq', axis=1, tiled=True)[0]]
  transfers between devices with their start and end apart: 8 -> 17, of which waited for: 6 -> 8; matrix products, arithmetic and copies ran while one was open for 8% -> 0% of each run, Pallas kernels for 0% -> 39%
where the time goes in v1:
time: 198 us
  Pallas kernels  144 us (73%)
  waiting for transfers between devices  25.2 us (13%)
  starting transfers between devices  22.1 us (11%)
  local copies, waits for them, and re-layouts  5.64 us (3%)
    pallas_call x2, Pallas kernels, pack(): pl.pallas_call(functools.partial(pack_kernel, groups, local, chunk, width...  67 us
    pallas_call x2, Pallas kernels, unpack(): pl.pallas_call(functools.partial(unpack_kernel, groups, local, chunk, wid...  66 us
    ppermute x17, waiting for transfers between devices, permute(): return lax.ppermute(value, axis, [(i, i ^ shift) for i in range(size)])  25.2 us
    ppermute x17, starting transfers between devices, permute(): return lax.ppermute(value, axis, [(i, i ^ shift) for i in range(size)])  22.1 us
    pallas_call x2, Pallas kernels, attend(): pl.pallas_call(functools.partial(attend_kernel, groups, rows, heads, bloc...  11.3 us
    unnamed x34, local copies, waits for them, and re-layouts  4.52 us
  transfers between devices with their start and end apart: 17, of which 8 were waited for; matrix products, arithmetic and copies ran while one was open for 0% of the time, Pallas kernels for 39%

profile of v1, /device:TPU:0, one launch (start us, length us, event | category | flops | bytes accessed | tf_op | source)
XLA Modules:
  0.0 198.2 jit_solution(8106192375415136306)
XLA Ops:
  0.6 0.6 copy-done.16
  1.3 0.6 pad.4.refs_4_
  1.9 34.0 %pack0.1 = (bf16[528,256]{1,0:T(8,128)(2,1)}, bf16[528,256]{1,0:T(8,128)(2,1)}, bf16[528,256]{1,0:T(8,128)(2,1)}, bf16[528,256]{1,0:T(8,128)(2,1)}) custom-call(s32[1]{0:T(128)} %bitcast.me_ref, bf16[1,128,2048]{2,1,0:T(8,128)(2,1)} %refs_0_.3, bf16[1,128,2048]{2,1,0:T(8,128)(2,1)} %refs_1_.3, bf16[1,128,2048]{2,1,0:T(8,128)(2,1)} %refs_2_.3, ...), custom_call_target="tpu_custom_call" | custom-call | tf_op jit(solution)/shard_map/pack0/pallas_call | solution.py:72
  35.9 3.0 %collective-permute-start.3 = (bf16[528,256]{1,0:T(8,128)(2,1)}, bf16[528,256]{1,0:T(8,128)(2,1)S(1)}, u32[]{:S(2)}, u32[]{:S(2)}) collective-permute-start(bf16[528,256]{1,0:T(8,128)(2,1)} %get-tuple-element.37), channel_id=1, source_target_pairs={{0,8},{8,0},{16,24},{24,16},{1,9},{9,1},{17,25},{25,17},{2,10},{10... | collective-permute-start | bytes 811016 | tf_op jit(solution)/shard_map/ppermute | solution.py:207
  38.9 1.5 collective-permute-start.4
  40.5 33.0 %pack1.1 = (bf16[512,256]{1,0:T(8,128)(2,1)}, bf16[512,256]{1,0:T(8,128)(2,1)}, bf16[512,256]{1,0:T(8,128)(2,1)}, bf16[512,256]{1,0:T(8,128)(2,1)}) custom-call(s32[1]{0:T(128)} %bitcast.me_ref, bf16[1,128,2048]{2,1,0:T(8,128)(2,1)} %refs_0_.3, bf16[1,128,2048]{2,1,0:T(8,128)(2,1)} %refs_1_.3, bf16[1,128,2048]{2,1,0:T(8,128)(2,1)} %refs_2_.3, ...), custom_call_target="tpu_custom_call" | custom-call | tf_op jit(solution)/shard_map/pack1/pallas_call | solution.py:72
  73.5 2.0 %collective-permute-start = (bf16[512,256]{1,0:T(8,128)(2,1)}, bf16[512,256]{1,0:T(8,128)(2,1)S(1)}, u32[]{:S(2)}, u32[]{:S(2)}) collective-permute-start(bf16[512,256]{1,0:T(8,128)(2,1)} %get-tuple-element.33), channel_id=1, source_target_pairs={{0,8},{8,0},{16,24},{24,16},{1,9},{9,1},{17,25},{25,17},{2,10},{10... | collective-permute-start | bytes 786440 | tf_op jit(solution)/shard_map/ppermute | solution.py:207
  75.5 1.5 collective-permute-start.1
  77.1 0.6 copy-done.8
  77.9 5.6 %attend0.1 = (bf16[512,256]{1,0:T(8,128)(2,1)}, bf16[512,256]{1,0:T(8,128)(2,1)}, bf16[512,256]{1,0:T(8,128)(2,1)}, bf16[512,256]{1,0:T(8,128)(2,1)}, f32[2,128]{1,0:T(2,128)}) custom-call(bf16[528,256]{1,0:T(8,128)(2,1)} %get-tuple-element.36.refs_4_.refs_0_, bf16[528,256]{1,0:T(8,128)(2,1)} %copy-done.8, bf16[528,256]{1,0:T(8,128)(2,1)} %copy-done.9, ...), custom_call_target="tpu_custom_call" | custom-call | flops 805306368 | bytes 2097152 | tf_op jit(solution)/shard_map/attend0/pallas_call | solution.py:188
  83.6 1.9 collective-permute-start.9
  85.5 1.4 collective-permute-done.1.refs_2_
  86.9 3.2 %collective-permute-done.2.refs_3_ = bf16[512,256]{1,0:T(8,128)(2,1)S(1)} collective-permute-done((bf16[512,256]{1,0:T(8,128)(2,1)}, bf16[512,256]{1,0:T(8,128)(2,1)S(1)}, u32[]{:S(2)}, u32[]{:S(2)}) %collective-permute-start.2) | collective-permute-done | bytes 262176 | tf_op jit(solution)/shard_map/ppermute | solution.py:207
  90.1 0.7 copy-done.15
  90.8 5.7 %attend1.1 = (bf16[512,256]{1,0:T(8,128)(2,1)}, bf16[512,256]{1,0:T(8,128)(2,1)}, bf16[512,256]{1,0:T(8,128)(2,1)}, bf16[512,256]{1,0:T(8,128)(2,1)}, f32[2,128]{1,0:T(2,128)}) custom-call(bf16[512,256]{1,0:T(8,128)(2,1)} %get-tuple-element.32.refs_0_, bf16[512,256]{1,0:T(8,128)(2,1)} %copy-done.13, bf16[512,256]{1,0:T(8,128)(2,1)} %copy-done.14, ...), custom_call_target="tpu_custom_call" | custom-call | flops 805306368 | bytes 2097152 | tf_op jit(solution)/shard_map/attend1/pallas_call | solution.py:188
  96.5 0.7 copy-done.7
  97.2 1.1 collective-permute-done.12
  98.4 1.6 collective-permute-start.13
  99.9 2.0 %collective-permute-done.13 = f32[2,128]{1,0:T(2,128)S(1)} collective-permute-done((f32[2,128]{1,0:T(2,128)S(1)}, f32[2,128]{1,0:T(2,128)S(1)}, u32[]{:S(2)}, u32[]{:S(2)}) %collective-permute-start.13) | collective-permute-done | bytes 1056 | tf_op jit(solution)/shard_map/ppermute | solution.py:207
  101.9 2.6 %collective-permute-start.14 = (f32[2,128]{1,0:T(2,128)S(1)}, f32[2,128]{1,0:T(2,128)S(1)}, u32[]{:S(2)}, u32[]{:S(2)}) collective-permute-start(f32[2,128]{1,0:T(2,128)S(1)} %add.22), channel_id=1, source_target_pairs={{0,4},{1,5},{2,6},{3,7},{4,0},{5,1},{6,2},{7,3},{8,12},{9,13},{10,... | collective-permute-start | bytes 3080 | tf_op jit(solution)/shard_map/ppermute | solution.py:207
  104.5 1.9 collective-permute-done.14
  106.4 1.4 collective-permute-start.15
  107.8 2.1 %collective-permute-done.15 = f32[2,128]{1,0:T(2,128)S(1)} collective-permute-done((f32[2,128]{1,0:T(2,128)S(1)}, f32[2,128]{1,0:T(2,128)S(1)}, u32[]{:S(2)}, u32[]{:S(2)}) %collective-permute-start.15) | collective-permute-done | bytes 1056 | tf_op jit(solution)/shard_map/ppermute | solution.py:207
  110.2 1.8 collective-permute-start.6
  112.0 1.5 collective-permute-start.10
  113.6 1.8 collective-permute-done.16
  115.5 2.7 %collective-permute-start.8 = (bf16[512,256]{1,0:T(8,128)(2,1)}, bf16[512,256]{1,0:T(8,128)(2,1)S(1)}, u32[]{:S(2)}, u32[]{:S(2)}) collective-permute-start(bf16[512,256]{1,0:T(8,128)(2,1)} %get-tuple-element.43), channel_id=1, source_target_pairs={{0,24},{8,16},{16,8},{24,0},{1,25},{9,17},{17,9},{25,1},{2,26},{10... | collective-permute-start | bytes 786440 | tf_op jit(solution)/shard_map/ppermute | solution.py:207
  118.8 11.6 %collective-permute-done.10.refs_2_ = bf16[512,256]{1,0:T(8,128)(2,1)S(1)} collective-permute-done((bf16[512,256]{1,0:T(8,128)(2,1)S(1)}, bf16[512,256]{1,0:T(8,128)(2,1)S(1)}, u32[]{:S(2)}, u32[]{:S(2)}) %collective-permute-start.10) | collective-permute-done | bytes 262176 | tf_op jit(solution)/shard_map/ppermute | solution.py:207
  130.4 0.7 copy-done.1
  131.2 33.0 %unpack0.1 = (bf16[1,128,2048]{2,1,0:T(8,128)(2,1)}, bf16[1,128,2048]{2,1,0:T(8,128)(2,1)}, bf16[1,128,2048]{2,1,0:T(8,128)(2,1)}, bf16[1,128,2048]{2,1,0:T(8,128)(2,1)}) custom-call(s32[1]{0:T(128)} %bitcast.me_ref, bf16[512,256]{1,0:T(8,128)(2,1)} %get-tuple-element.44.refs_0_, bf16[512,256]{1,0:T(8,128)(2,1)} %copy-done, bf16[512,256]{1,0:T(8,128)(2,1)} %copy-done.1, ...), custom_call_target="tpu_custom_call" | custom-call | tf_op jit(solution)/shard_map/unpack0/pallas_call | solution.py:112
  164.3 0.7 copy-done.3
  165.2 33.0 %unpack1.1 = (bf16[1,128,2048]{2,1,0:T(8,128)(2,1)}, bf16[1,128,2048]{2,1,0:T(8,128)(2,1)}, bf16[1,128,2048]{2,1,0:T(8,128)(2,1)}, bf16[1,128,2048]{2,1,0:T(8,128)(2,1)}) custom-call(s32[1]{0:T(128)} %bitcast.me_ref, bf16[512,256]{1,0:T(8,128)(2,1)} %get-tuple-element.40.refs_0_, ...), custom_call_target="tpu_custom_call", output_to_operand_aliasing={{0}: (5, {}), {1}: (6, {}), {2}: (7, {}), {3}: (8, {})} | custom-call | tf_op jit(solution)/shard_map/unpack1/pallas_call | solution.py:112
  (51 shorter events, 1.6 us)
Async XLA Ops:
  35.9 41.1 %collective-permute-start.3 = (bf16[528,256]{1,0:T(8,128)(2,1)}, bf16[528,256]{1,0:T(8,128)(2,1)S(1)}, u32[]{:S(2)}, u32[]{:S(2)}) collective-permute-start(bf16[528,256]{1,0:T(8,128)(2,1)} %get-tuple-element.37), channel_id=1, source_target_pairs={{0,8},{8,0},{16,24},{24,16},{1,9},{9,1},{17,25},{25,17},{2,10},{10... | collective-permute-start | bytes 811016 | tf_op jit(solution)/shard_map/ppermute | solution.py:207
  38.9 38.1 %collective-permute-start.4 = (bf16[528,256]{1,0:T(8,128)(2,1)}, bf16[528,256]{1,0:T(8,128)(2,1)S(1)}, u32[]{:S(2)}, u32[]{:S(2)}) collective-permute-start(bf16[528,256]{1,0:T(8,128)(2,1)} %get-tuple-element.38), channel_id=1, source_target_pairs={{0,16},{8,24},{16,0},{24,8},{1,17},{9,25},{17,1},{25,9},{2,18},{10... | collective-permute-start | bytes 811016 | tf_op jit(solution)/shard_map/ppermute | solution.py:207
  40.5 36.6 %collective-permute-start.5 = (bf16[528,256]{1,0:T(8,128)(2,1)}, bf16[528,256]{1,0:T(8,128)(2,1)S(1)}, u32[]{:S(2)}, u32[]{:S(2)}) collective-permute-start(bf16[528,256]{1,0:T(8,128)(2,1)} %get-tuple-element.39), channel_id=1, source_target_pairs={{0,24},{8,16},{16,8},{24,0},{1,25},{9,17},{17,9},{25,1},{2,26},{10... | collective-permute-start | bytes 811016 | tf_op jit(solution)/shard_map/ppermute | solution.py:207
  73.5 12.0 %collective-permute-start = (bf16[512,256]{1,0:T(8,128)(2,1)}, bf16[512,256]{1,0:T(8,128)(2,1)S(1)}, u32[]{:S(2)}, u32[]{:S(2)}) collective-permute-start(bf16[512,256]{1,0:T(8,128)(2,1)} %get-tuple-element.33), channel_id=1, source_target_pairs={{0,8},{8,0},{16,24},{24,16},{1,9},{9,1},{17,25},{25,17},{2,10},{10... | collective-permute-start | bytes 786440 | tf_op jit(solution)/shard_map/ppermute | solution.py:207
  75.5 11.4 %collective-permute-start.1 = (bf16[512,256]{1,0:T(8,128)(2,1)}, bf16[512,256]{1,0:T(8,128)(2,1)S(1)}, u32[]{:S(2)}, u32[]{:S(2)}) collective-permute-start(bf16[512,256]{1,0:T(8,128)(2,1)} %get-tuple-element.34), channel_id=1, source_target_pairs={{0,16},{8,24},{16,0},{24,8},{1,17},{9,25},{17,1},{25,9},{2,18},{10... | collective-permute-start | bytes 786440 | tf_op jit(solution)/shard_map/ppermute | solution.py:207
  77.0 0.7 copy-start.8
  77.0 13.1 %collective-permute-start.2 = (bf16[512,256]{1,0:T(8,128)(2,1)}, bf16[512,256]{1,0:T(8,128)(2,1)S(1)}, u32[]{:S(2)}, u32[]{:S(2)}) collective-permute-start(bf16[512,256]{1,0:T(8,128)(2,1)} %get-tuple-element.35), channel_id=1, source_target_pairs={{0,24},{8,16},{16,8},{24,0},{1,25},{9,17},{17,9},{25,1},{2,26},{10... | collective-permute-start | bytes 786440 | tf_op jit(solution)/shard_map/ppermute | solution.py:207
  77.1 0.7 copy-start.9
  77.1 0.8 copy-start.10
  83.6 32.0 %collective-permute-start.9 = (bf16[512,256]{1,0:T(8,128)(2,1)}, bf16[512,256]{1,0:T(8,128)(2,1)S(1)}, u32[]{:S(2)}, u32[]{:S(2)}) collective-permute-start(bf16[512,256]{1,0:T(8,128)(2,1)} %get-tuple-element.45), channel_id=1, source_target_pairs={{0,8},{8,0},{16,24},{24,16},{1,9},{9,1},{17,25},{25,17},{2,10},{10... | collective-permute-start | bytes 786440 | tf_op jit(solution)/shard_map/ppermute | solution.py:207
  85.5 4.6 %copy-start.13 = (bf16[512,256]{1,0:T(8,128)(2,1)}, bf16[512,256]{1,0:T(8,128)(2,1)S(1)}, u32[]{:S(2)}) copy-start(bf16[512,256]{1,0:T(8,128)(2,1)S(1)} %collective-permute-done.refs_1_) | copy-start | bytes 786436
  86.9 3.2 %copy-start.14 = (bf16[512,256]{1,0:T(8,128)(2,1)}, bf16[512,256]{1,0:T(8,128)(2,1)S(1)}, u32[]{:S(2)}) copy-start(bf16[512,256]{1,0:T(8,128)(2,1)S(1)} %collective-permute-done.1.refs_2_) | copy-start | bytes 786436
  90.1 0.7 copy-start.15
  90.8 21.2 %copy-start.12 = (bf16[512,256]{1,0:T(8,128)(2,1)S(1)}, bf16[512,256]{1,0:T(8,128)(2,1)}, u32[]{:S(2)}) copy-start(bf16[512,256]{1,0:T(8,128)(2,1)} %get-tuple-element.46) | copy-start | bytes 786436
  90.8 22.6 %copy-start.11 = (bf16[512,256]{1,0:T(8,128)(2,1)S(1)}, bf16[512,256]{1,0:T(8,128)(2,1)}, u32[]{:S(2)}) copy-start(bf16[512,256]{1,0:T(8,128)(2,1)} %get-tuple-element.47) | copy-start | bytes 786436
  96.5 0.7 copy-start.6
  97.2 1.1 collective-permute-start.12
  98.4 3.6 %collective-permute-start.13 = (f32[2,128]{1,0:T(2,128)S(1)}, f32[2,128]{1,0:T(2,128)S(1)}, u32[]{:S(2)}, u32[]{:S(2)}) collective-permute-start(f32[2,128]{1,0:T(2,128)S(1)} %add.21), channel_id=1, source_target_pairs={{0,2},{1,3},{2,0},{3,1},{4,6},{5,7},{6,4},{7,5},{8,10},{9,11},{10,... | collective-permute-start | bytes 3080 | tf_op jit(solution)/shard_map/ppermute | solution.py:207
  101.9 4.5 %collective-permute-start.14 = (f32[2,128]{1,0:T(2,128)S(1)}, f32[2,128]{1,0:T(2,128)S(1)}, u32[]{:S(2)}, u32[]{:S(2)}) collective-permute-start(f32[2,128]{1,0:T(2,128)S(1)} %add.22), channel_id=1, source_target_pairs={{0,4},{1,5},{2,6},{3,7},{4,0},{5,1},{6,2},{7,3},{8,12},{9,13},{10,... | collective-permute-start | bytes 3080 | tf_op jit(solution)/shard_map/ppermute | solution.py:207
  106.4 3.6 %collective-permute-start.15 = (f32[2,128]{1,0:T(2,128)S(1)}, f32[2,128]{1,0:T(2,128)S(1)}, u32[]{:S(2)}, u32[]{:S(2)}) collective-permute-start(f32[2,128]{1,0:T(2,128)S(1)} %add.23), channel_id=1, source_target_pairs={{0,8},{8,0},{16,24},{24,16},{1,9},{9,1},{17,25},{25,17},{2,10},{10... | collective-permute-start | bytes 3080 | tf_op jit(solution)/shard_map/ppermute | solution.py:207
  110.0 5.4 %collective-permute-start.16 = (f32[2,128]{1,0:T(2,128)S(1)}, f32[2,128]{1,0:T(2,128)S(1)}, u32[]{:S(2)}, u32[]{:S(2)}) collective-permute-start(f32[2,128]{1,0:T(2,128)S(1)} %add.24), channel_id=1, source_target_pairs={{0,16},{8,24},{16,0},{24,8},{1,17},{9,25},{17,1},{25,9},{2,18},{10... | collective-permute-start | bytes 3080 | tf_op jit(solution)/shard_map/ppermute | solution.py:207
  110.2 54.1 %collective-permute-start.6 = (bf16[512,256]{1,0:T(8,128)(2,1)}, bf16[512,256]{1,0:T(8,128)(2,1)S(1)}, u32[]{:S(2)}, u32[]{:S(2)}) collective-permute-start(bf16[512,256]{1,0:T(8,128)(2,1)} %get-tuple-element.41), channel_id=1, source_target_pairs={{0,8},{8,0},{16,24},{24,16},{1,9},{9,1},{17,25},{25,17},{2,10},{10... | collective-permute-start | bytes 786440 | tf_op jit(solution)/shard_map/ppermute | solution.py:207
  112.0 18.4 %collective-permute-start.10 = (bf16[512,256]{1,0:T(8,128)(2,1)S(1)}, bf16[512,256]{1,0:T(8,128)(2,1)S(1)}, u32[]{:S(2)}, u32[]{:S(2)}) collective-permute-start(bf16[512,256]{1,0:T(8,128)(2,1)S(1)} %copy-done.12), channel_id=1, source_target_pairs={{0,16},{8,24},{16,0},{24,8},{1,17},{9,25},{17,1},{25,9},{2,18},{10... | collective-permute-start | bytes 786440 | tf_op jit(solution)/shard_map/ppermute | solution.py:207
  113.5 17.0 %collective-permute-start.11 = (bf16[512,256]{1,0:T(8,128)(2,1)S(1)}, bf16[512,256]{1,0:T(8,128)(2,1)S(1)}, u32[]{:S(2)}, u32[]{:S(2)}) collective-permute-start(bf16[512,256]{1,0:T(8,128)(2,1)S(1)} %copy-done.11), channel_id=1, source_target_pairs={{0,24},{8,16},{16,8},{24,0},{1,25},{9,17},{17,9},{25,1},{2,26},{10... | collective-permute-start | bytes 786440 | tf_op jit(solution)/shard_map/ppermute | solution.py:207
  115.4 48.9 %collective-permute-start.7 = (bf16[512,256]{1,0:T(8,128)(2,1)}, bf16[512,256]{1,0:T(8,128)(2,1)S(1)}, u32[]{:S(2)}, u32[]{:S(2)}) collective-permute-start(bf16[512,256]{1,0:T(8,128)(2,1)} %get-tuple-element.42), channel_id=1, source_target_pairs={{0,16},{8,24},{16,0},{24,8},{1,17},{9,25},{17,1},{25,9},{2,18},{10... | collective-permute-start | bytes 786440 | tf_op jit(solution)/shard_map/ppermute | solution.py:207
  115.5 14.9 %copy-start = (bf16[512,256]{1,0:T(8,128)(2,1)}, bf16[512,256]{1,0:T(8,128)(2,1)S(1)}, u32[]{:S(2)}) copy-start(bf16[512,256]{1,0:T(8,128)(2,1)S(1)} %collective-permute-done.9.refs_1_) | copy-start | bytes 786436
  115.5 48.8 %collective-permute-start.8 = (bf16[512,256]{1,0:T(8,128)(2,1)}, bf16[512,256]{1,0:T(8,128)(2,1)S(1)}, u32[]{:S(2)}, u32[]{:S(2)}) collective-permute-start(bf16[512,256]{1,0:T(8,128)(2,1)} %get-tuple-element.43), channel_id=1, source_target_pairs={{0,24},{8,16},{16,8},{24,0},{1,25},{9,17},{17,9},{25,1},{2,26},{10... | collective-permute-start | bytes 786440 | tf_op jit(solution)/shard_map/ppermute | solution.py:207
  130.4 0.7 copy-start.1
  130.4 0.8 copy-start.2
  164.3 0.7 copy-start.3
  164.3 0.8 copy-start.4
  164.3 0.9 copy-start.5
  (2 other events, 1.3 us)

commit v2 on v1

--- a/solution.py
+++ b/solution.py
@@ -12,7 +12,7 @@
 TENSORS = 4
 ID_ROWS = 16
 SCALE = HEAD_DIM ** (-0.5)
-VMEM_BYTES = 56 * 1024 * 1024
+MIB = 1024 * 1024
 
 
 def dot(a, b, contract):
@@ -35,59 +35,65 @@
     return grad_rows, jnp.sum(grad_out * normed, axis=0, keepdims=True)
 
 
-def pack_kernel(groups, local, chunk, width, with_ids, me_ref, *refs):
+def pack_kernel(groups, local, chunk, width, with_ids, *refs):
     tensors, rest = refs[:TENSORS], refs[TENSORS:]
     if with_ids:
         ids_ref, rest = rest[0], rest[1:]
     outs, sems = rest[:groups], rest[groups]
     rows = tensors[0].shape[1]
-    copies = []
+    started = []
     for shift in range(groups):
-        owner = jnp.bitwise_xor(me_ref[0], shift)
+        owner = jnp.bitwise_xor(lax.axis_index("seq"), shift)
         start = pl.multiple_of(owner * local + chunk * width, HEAD_DIM)
         for t in range(TENSORS):
-            copies.append((
-                tensors[t].at[0, :, pl.ds(start, width)],
-                outs[shift].at[pl.ds(t * rows, rows), :],
-            ))
-        if with_ids:
-            copies.append((ids_ref, outs[shift].at[pl.ds(TENSORS * rows, ID_ROWS), :]))
-    started = [
-        pltpu.make_async_copy(source, target, sems.at[i])
-        for i, (source, target) in enumerate(copies)
-    ]
+            started.append(
+                pltpu.make_async_copy(
+                    tensors[t].at[0, :, pl.ds(start, width)],
+                    outs[shift].at[pl.ds(t * rows, rows), :],
+                    sems.at[shift * TENSORS + t],
+                )
+            )
     for copy in started:
         copy.start()
+    if with_ids:
+        ids = jnp.broadcast_to(ids_ref[...].astype(jnp.float32), (ID_ROWS, rows))
+        for out in outs:
+            for first in range(0, width, rows):
+                out[TENSORS * rows :, first : first + rows] = ids.astype(jnp.bfloat16)
     for copy in started:
         copy.wait()
 
 
-def pack(me, arrays, ids_block, groups, local, chunk, width):
+def pack(arrays, slice_ids, groups, local, chunk, width):
     rows = arrays[0].shape[1]
-    with_ids = ids_block is not None
+    with_ids = slice_ids is not None
     height = TENSORS * rows + (ID_ROWS if with_ids else 0)
-    count = groups * (TENSORS + (1 if with_ids else 0))
-    any_spec = pl.BlockSpec(memory_space=pl.ANY)
-    operands = (me,) + tuple(arrays) + ((ids_block,) if with_ids else ())
+    vmem_spec = pl.BlockSpec(memory_space=pltpu.VMEM)
+    operands = tuple(arrays) + ((slice_ids,) if with_ids else ())
     return pl.pallas_call(
         functools.partial(pack_kernel, groups, local, chunk, width, with_ids),
         out_shape=[jax.ShapeDtypeStruct((height, width), jnp.bfloat16)] * groups,
-        in_specs=[pl.BlockSpec(memory_space=pltpu.SMEM)] + [any_spec] * (len(operands) - 1),
-        out_specs=[any_spec] * groups,
-        scratch_shapes=[pltpu.SemaphoreType.DMA((count,))],
+        in_specs=[pl.BlockSpec(memory_space=pltpu.HBM)] * TENSORS
+        + [vmem_spec] * (len(operands) - TENSORS),
+        out_specs=[vmem_spec] * groups,
+        scratch_shapes=[pltpu.SemaphoreType.DMA((TENSORS * groups,))],
+        compiler_params=pltpu.CompilerParams(vmem_limit_bytes=8 * MIB),
         name=f"pack{chunk}",
     )(*operands)
 
 
-def unpack_kernel(groups, local, chunk, width, aliased, me_ref, *refs):
+def unpack_kernel(groups, local, chunk, width, aliased, carries, *refs):
     pieces, rest = refs[:groups], refs[groups:]
     if aliased:
         rest = rest[TENSORS:]
+    if carries:
+        rest[TENSORS + 1][...] = rest[0][...]
+        rest = rest[1 : TENSORS + 1] + rest[TENSORS + 2 :]
     outs, sems = rest[:TENSORS], rest[TENSORS]
     rows = outs[0].shape[1]
     started = []
     for shift in range(groups):
-        owner = jnp.bitwise_xor(me_ref[0], shift)
+        owner = jnp.bitwise_xor(lax.axis_index("seq"), shift)
         start = pl.multiple_of(owner * local + chunk * width, HEAD_DIM)
         for t in range(TENSORS):
             started.append(
@@ -103,21 +109,25 @@
         copy.wait()
 
 
-def unpack(me, pieces, previous, shape, local, chunk, width):
+def unpack(pieces, previous, carried, shape, local, chunk, width):
     groups = len(pieces)
-    aliased = previous is not None
-    any_spec = pl.BlockSpec(memory_space=pl.ANY)
-    operands = (me,) + tuple(pieces) + (tuple(previous) if aliased else ())
-    aliases = {1 + groups + t: t for t in range(TENSORS)} if aliased else {}
+    aliased, carries = previous is not None, carried is not None
+    any_spec = pl.BlockSpec(memory_space=pltpu.HBM)
+    vmem_spec = pl.BlockSpec(memory_space=pltpu.VMEM)
+    operands = tuple(pieces) + (tuple(previous) if aliased else ())
+    aliases = {groups + t: t for t in range(TENSORS)} if aliased else {}
+    extra = ([carried], [vmem_spec]) if carries else ([], [])
     return pl.pallas_call(
-        functools.partial(unpack_kernel, groups, local, chunk, width, aliased),
-        out_shape=[jax.ShapeDtypeStruct(shape, jnp.bfloat16)] * TENSORS,
-        in_specs=[pl.BlockSpec(memory_space=pltpu.SMEM)] + [any_spec] * (len(operands) - 1),
-        out_specs=[any_spec] * TENSORS,
+        functools.partial(unpack_kernel, groups, local, chunk, width, aliased, carries),
+        out_shape=[jax.ShapeDtypeStruct(shape, jnp.bfloat16)] * TENSORS
+        + [jax.ShapeDtypeStruct(value.shape, value.dtype) for value in extra[0]],
+        in_specs=[vmem_spec] * groups + [any_spec] * (len(operands) - groups) + extra[1],
+        out_specs=[any_spec] * TENSORS + extra[1],
         scratch_shapes=[pltpu.SemaphoreType.DMA((groups * TENSORS,))],
         input_output_aliases=aliases,
+        compiler_params=pltpu.CompilerParams(vmem_limit_bytes=8 * MIB),
         name=f"unpack{chunk}",
-    )(*operands)
+    )(*operands, *extra[0])
 
 
 def attend_kernel(groups, rows, heads, block, *refs):
@@ -192,7 +202,7 @@
         + [jax.ShapeDtypeStruct((2, HEAD_DIM), jnp.float32)],
         in_specs=[piece_spec] * groups + [ids_spec] * groups + [gain_spec] * 2,
         out_specs=[piece_spec] * groups + [pl.BlockSpec((2, HEAD_DIM), lambda i: (0, 0))],
-        compiler_params=pltpu.CompilerParams(vmem_limit_bytes=VMEM_BYTES),
+        compiler_params=pltpu.CompilerParams(vmem_limit_bytes=(24 if length <= 512 else 48) * MIB),
         cost_estimate=pl.CostEstimate(
             flops=12 * area * HEAD_DIM,
             bytes_accessed=4 * groups * height * width,
@@ -222,17 +232,13 @@
     chunks = 2 if local >= 2 * HEAD_DIM else 1
     chunk_width = local // chunks
     heads = chunk_width // HEAD_DIM
-    me = lax.axis_index("seq").astype(jnp.int32).reshape(1)
     arrays = (queries, key_rows, values, cotangent)
-    ids_block = jnp.pad(
-        slice_ids.astype(jnp.bfloat16), ((0, ID_ROWS - 1), (0, chunk_width - rows))
-    )
     gains = (query_gain.reshape(1, HEAD_DIM), key_gain.reshape(1, HEAD_DIM))
 
     received = []
     for chunk in range(chunks):
         payloads = pack(
-            me, arrays, ids_block if chunk == 0 else None, groups, local, chunk, chunk_width
+            arrays, slice_ids if chunk == 0 else None, groups, local, chunk, chunk_width
         )
         received.append(
             [payloads[0]]
@@ -248,11 +254,16 @@
             [results[0]]
             + [permute(results[shift], "seq", groups, shift) for shift in range(1, groups)]
         )
+    outputs = None
+    for chunk in range(chunks):
+        carried = gain_total if chunk == 0 else None
+        outputs = unpack(
+            returned[chunk], outputs, carried, queries.shape, local, chunk, chunk_width
+        )
+        if chunk == 0:
+            *outputs, gain_total = outputs
     gain_total = total_over(gain_total, "dp", batches)
     gain_total = total_over(gain_total, "seq", groups)
-    outputs = None
-    for chunk in range(chunks):
-        outputs = unpack(me, returned[chunk], outputs, queries.shape, local, chunk, chunk_width)
     return (*outputs, gain_total[0], gain_total[1])
 
 

time: 198 us -> 64.4 us (0.33)
  Pallas kernels: 144 us -> 9.9 us
  starting transfers between devices: 22.1 us -> 25.8 us
  waiting for transfers between devices: 25.2 us -> 21.7 us
    pallas_call x2, Pallas kernels: 67 us -> 0.67 us  [pack(): pl.pallas_call(functools.partial(pack_kernel, groups, local, chunk, width...]
    pallas_call x2, Pallas kernels: 66 us -> 2.19 us  [unpack(): pl.pallas_call(functools.partial(unpack_kernel, groups, local, chunk, wid...]
    pallas_call x2, Pallas kernels: 11.3 us -> 7.04 us  [attend(): pl.pallas_call(functools.partial(attend_kernel, groups, rows, heads, bloc...]
    ppermute x17, starting transfers between devices: 22.1 us -> 25.8 us  [permute(): return lax.ppermute(value, axis, [(i, i ^ shift) for i in range(size)])]
    ppermute x17, waiting for transfers between devices: 25.2 us -> 21.7 us  [permute(): return lax.ppermute(value, axis, [(i, i ^ shift) for i in range(size)])]
    unnamed x34 -> x14, local copies, waits for them, and re-layouts: 4.52 us -> 5.48 us
  transfers between devices with their start and end apart: 17 -> 17, of which waited for: 8 -> 11; matrix products, arithmetic and copies ran while one was open for 0% -> 0% of each run, Pallas kernels for 39% -> 15%
where the time goes in v2:
time: 64.4 us; the launch traced here: 64.1 us
  starting transfers between devices  25.8 us (40%)
  waiting for transfers between devices  21.7 us (34%)
  Pallas kernels  9.9 us (15%)
  local copies, waits for them, and re-layouts  6 us (9%)
  between operations  0.72 us (1%)
    ppermute x17, starting transfers between devices, permute(): return lax.ppermute(value, axis, [(i, i ^ shift) for i in range(size)])  25.8 us
    ppermute x17, waiting for transfers between devices, permute(): return lax.ppermute(value, axis, [(i, i ^ shift) for i in range(size)])  21.7 us
    pallas_call x2, Pallas kernels, attend(): pl.pallas_call(functools.partial(attend_kernel, groups, rows, heads, bloc...  7.04 us
    unnamed x14, local copies, waits for them, and re-layouts  5.48 us
    pallas_call x2, Pallas kernels, unpack(): pl.pallas_call(functools.partial(unpack_kernel, groups, local, chunk, wid...  2.19 us
  transfers between devices with their start and end apart: 17, of which 11 were waited for; matrix products, arithmetic and copies ran while one was open for 0% of the time, Pallas kernels for 15%

profile of v2, /device:TPU:0, one launch (start us, length us, event | category | flops | bytes accessed | tf_op | source)
XLA Modules:
  0.0 64.1 jit_solution(14644997218582275186)
XLA Ops:
  0.6 1.0 %copy-done = bf16[1,128,2048]{2,1,0:T(8,128)(2,1)S(1)} copy-done((bf16[1,128,2048]{2,1,0:T(8,128)(2,1)S(1)}, bf16[1,128,2048]{2,1,0:T(8,128)(2,1)}, u32[]{:S(2)}) %copy-start) | copy-done | bytes 524312
  1.7 1.0 %copy-done.1 = bf16[1,128,2048]{2,1,0:T(8,128)(2,1)S(1)} copy-done((bf16[1,128,2048]{2,1,0:T(8,128)(2,1)S(1)}, bf16[1,128,2048]{2,1,0:T(8,128)(2,1)}, u32[]{:S(2)}) %copy-start.1) | copy-done | bytes 524312
  2.7 1.0 %copy-done.2 = bf16[1,128,2048]{2,1,0:T(8,128)(2,1)S(1)} copy-done((bf16[1,128,2048]{2,1,0:T(8,128)(2,1)S(1)}, bf16[1,128,2048]{2,1,0:T(8,128)(2,1)}, u32[]{:S(2)}) %copy-start.2) | copy-done | bytes 524312
  3.8 1.0 %copy-done.3 = bf16[1,128,2048]{2,1,0:T(8,128)(2,1)S(1)} copy-done((bf16[1,128,2048]{2,1,0:T(8,128)(2,1)S(1)}, bf16[1,128,2048]{2,1,0:T(8,128)(2,1)}, u32[]{:S(2)}) %copy-start.3) | copy-done | bytes 524312
  4.8 0.7 %copy-done.4 = s32[1,128]{1,0:T(1,128)S(1)} copy-done((s32[1,128]{1,0:T(1,128)S(1)}, s32[1,128]{1,0:T(1,128)}, u32[]{:S(2)}) %copy-start.4) | copy-done | bytes 536
  5.8 3.0 %collective-permute-start.3 = (bf16[528,256]{1,0:T(8,128)(2,1)S(1)}, bf16[528,256]{1,0:T(8,128)(2,1)S(1)}, u32[]{:S(2)}, u32[]{:S(2)}) collective-permute-start(bf16[528,256]{1,0:T(8,128)(2,1)S(1)} %get-tuple-element.38), channel_id=1, source_target_pairs={{0,8},{8,0},{16,24},{24,16},{1,9},{9,1},{17,25},{25,17},{2,10},{10... | collective-permute-start | bytes 811016 | tf_op jit(solution)/shard_map/ppermute | solution.py:217
  8.8 1.5 %collective-permute-start.4 = (bf16[528,256]{1,0:T(8,128)(2,1)S(1)}, bf16[528,256]{1,0:T(8,128)(2,1)S(1)}, u32[]{:S(2)}, u32[]{:S(2)}) collective-permute-start(bf16[528,256]{1,0:T(8,128)(2,1)S(1)} %get-tuple-element.39), channel_id=1, source_target_pairs={{0,16},{8,24},{16,0},{24,8},{1,17},{9,25},{17,1},{25,9},{2,18},{10... | collective-permute-start | bytes 811016 | tf_op jit(solution)/shard_map/ppermute | solution.py:217
  10.7 2.0 %collective-permute-start = (bf16[512,256]{1,0:T(8,128)(2,1)S(1)}, bf16[512,256]{1,0:T(8,128)(2,1)S(1)}, u32[]{:S(2)}, u32[]{:S(2)}) collective-permute-start(bf16[512,256]{1,0:T(8,128)(2,1)S(1)} %get-tuple-element.34), channel_id=1, source_target_pairs={{0,8},{8,0},{16,24},{24,16},{1,9},{9,1},{17,25},{25,17},{2,10},{10... | collective-permute-start | bytes 786440 | tf_op jit(solution)/shard_map/ppermute | solution.py:217
  12.7 1.5 %collective-permute-start.1 = (bf16[512,256]{1,0:T(8,128)(2,1)S(1)}, bf16[512,256]{1,0:T(8,128)(2,1)S(1)}, u32[]{:S(2)}, u32[]{:S(2)}) collective-permute-start(bf16[512,256]{1,0:T(8,128)(2,1)S(1)} %get-tuple-element.35), channel_id=1, source_target_pairs={{0,16},{8,24},{16,0},{24,8},{1,17},{9,25},{17,1},{25,9},{2,18},{10... | collective-permute-start | bytes 786440 | tf_op jit(solution)/shard_map/ppermute | solution.py:217
  14.2 1.9 %collective-permute-done.3.refs_5_.refs_1_ = bf16[528,256]{1,0:T(8,128)(2,1)S(1)} collective-permute-done((bf16[528,256]{1,0:T(8,128)(2,1)S(1)}, bf16[528,256]{1,0:T(8,128)(2,1)S(1)}, u32[]{:S(2)}, u32[]{:S(2)}) %collective-permute-start.3) | collective-permute-done | bytes 270368 | tf_op jit(solution)/shard_map/ppermute | solution.py:217
  16.1 3.0 %collective-permute-start.2 = (bf16[512,256]{1,0:T(8,128)(2,1)S(1)}, bf16[512,256]{1,0:T(8,128)(2,1)S(1)}, u32[]{:S(2)}, u32[]{:S(2)}) collective-permute-start(bf16[512,256]{1,0:T(8,128)(2,1)S(1)} %get-tuple-element.36), channel_id=1, source_target_pairs={{0,24},{8,16},{16,8},{24,0},{1,25},{9,17},{17,9},{25,1},{2,26},{10... | collective-permute-start | bytes 786440 | tf_op jit(solution)/shard_map/ppermute | solution.py:217
  19.1 4.9 %collective-permute-done.4.refs_6_.refs_2_ = bf16[528,256]{1,0:T(8,128)(2,1)S(1)} collective-permute-done((bf16[528,256]{1,0:T(8,128)(2,1)S(1)}, bf16[528,256]{1,0:T(8,128)(2,1)S(1)}, u32[]{:S(2)}, u32[]{:S(2)}) %collective-permute-start.4) | collective-permute-done | bytes 270368 | tf_op jit(solution)/shard_map/ppermute | solution.py:217
  24.7 3.5 %attend0.1 = (bf16[512,256]{1,0:T(8,128)(2,1)S(1)}, bf16[512,256]{1,0:T(8,128)(2,1)S(1)}, bf16[512,256]{1,0:T(8,128)(2,1)S(1)}, bf16[512,256]{1,0:T(8,128)(2,1)S(1)}, f32[2,128]{1,0:T(2,128)S(1)}) custom-call(bf16[528,256]{1,0:T(8,128)(2,1)S(1)} %get-tuple-element.37.refs_4_.refs_0_, bf16[528,256]{1,0:T(8,128)(2,1)S(1)} %collective-permute-done.3.refs_5_.refs_1_, ...), custom_call_target="tpu_custom_call" | custom-call | flops 805306368 | bytes 2097152 | tf_op jit(solution)/shard_map/attend0/pallas_call | solution.py:198
  28.2 1.0 %collective-permute-start.9 = (bf16[512,256]{1,0:T(8,128)(2,1)S(1)}, bf16[512,256]{1,0:T(8,128)(2,1)S(1)}, u32[]{:S(2)}, u32[]{:S(2)}) collective-permute-start(bf16[512,256]{1,0:T(8,128)(2,1)S(1)} %get-tuple-element.46), channel_id=1, source_target_pairs={{0,8},{8,0},{16,24},{24,16},{1,9},{9,1},{17,25},{25,17},{2,10},{10... | collective-permute-start | bytes 786440 | tf_op jit(solution)/shard_map/ppermute | solution.py:217
  29.2 1.1 %collective-permute-start.10 = (bf16[512,256]{1,0:T(8,128)(2,1)S(1)}, bf16[512,256]{1,0:T(8,128)(2,1)S(1)}, u32[]{:S(2)}, u32[]{:S(2)}) collective-permute-start(bf16[512,256]{1,0:T(8,128)(2,1)S(1)} %get-tuple-element.47), channel_id=1, source_target_pairs={{0,16},{8,24},{16,0},{24,8},{1,17},{9,25},{17,1},{25,9},{2,18},{10... | collective-permute-start | bytes 786440 | tf_op jit(solution)/shard_map/ppermute | solution.py:217
  30.3 1.4 %collective-permute-start.11 = (bf16[512,256]{1,0:T(8,128)(2,1)S(1)}, bf16[512,256]{1,0:T(8,128)(2,1)S(1)}, u32[]{:S(2)}, u32[]{:S(2)}) collective-permute-start(bf16[512,256]{1,0:T(8,128)(2,1)S(1)} %get-tuple-element.48), channel_id=1, source_target_pairs={{0,24},{8,16},{16,8},{24,0},{1,25},{9,17},{17,9},{25,1},{2,26},{10... | collective-permute-start | bytes 786440 | tf_op jit(solution)/shard_map/ppermute | solution.py:217
  31.8 2.4 %collective-permute-done.1.refs_2_ = bf16[512,256]{1,0:T(8,128)(2,1)S(1)} collective-permute-done((bf16[512,256]{1,0:T(8,128)(2,1)S(1)}, bf16[512,256]{1,0:T(8,128)(2,1)S(1)}, u32[]{:S(2)}, u32[]{:S(2)}) %collective-permute-start.1) | collective-permute-done | bytes 262176 | tf_op jit(solution)/shard_map/ppermute | solution.py:217
  34.8 3.5 %attend1.1 = (bf16[512,256]{1,0:T(8,128)(2,1)S(1)}, bf16[512,256]{1,0:T(8,128)(2,1)S(1)}, bf16[512,256]{1,0:T(8,128)(2,1)S(1)}, bf16[512,256]{1,0:T(8,128)(2,1)S(1)}, f32[2,128]{1,0:T(2,128)S(1)}) custom-call(bf16[512,256]{1,0:T(8,128)(2,1)S(1)} %get-tuple-element.33.refs_0_, bf16[512,256]{1,0:T(8,128)(2,1)S(1)} %collective-permute-done.refs_1_, ...), custom_call_target="tpu_custom_call" | custom-call | flops 805306368 | bytes 2097152 | tf_op jit(solution)/shard_map/attend1/pallas_call | solution.py:198
  38.3 1.5 %collective-permute-start.6 = (bf16[512,256]{1,0:T(8,128)(2,1)S(1)}, bf16[512,256]{1,0:T(8,128)(2,1)S(1)}, u32[]{:S(2)}, u32[]{:S(2)}) collective-permute-start(bf16[512,256]{1,0:T(8,128)(2,1)S(1)} %get-tuple-element.42), channel_id=1, source_target_pairs={{0,8},{8,0},{16,24},{24,16},{1,9},{9,1},{17,25},{25,17},{2,10},{10... | collective-permute-start | bytes 786440 | tf_op jit(solution)/shard_map/ppermute | solution.py:217
  40.3 1.5 %collective-permute-start.8 = (bf16[512,256]{1,0:T(8,128)(2,1)S(1)}, bf16[512,256]{1,0:T(8,128)(2,1)S(1)}, u32[]{:S(2)}, u32[]{:S(2)}) collective-permute-start(bf16[512,256]{1,0:T(8,128)(2,1)S(1)} %get-tuple-element.44), channel_id=1, source_target_pairs={{0,24},{8,16},{16,8},{24,0},{1,25},{9,17},{17,9},{25,1},{2,26},{10... | collective-permute-start | bytes 786440 | tf_op jit(solution)/shard_map/ppermute | solution.py:217
  41.9 3.5 %collective-permute-done.10.refs_2_ = bf16[512,256]{1,0:T(8,128)(2,1)S(1)} collective-permute-done((bf16[512,256]{1,0:T(8,128)(2,1)S(1)}, bf16[512,256]{1,0:T(8,128)(2,1)S(1)}, u32[]{:S(2)}, u32[]{:S(2)}) %collective-permute-start.10) | collective-permute-done | bytes 262176 | tf_op jit(solution)/shard_map/ppermute | solution.py:217
  45.4 0.7 %collective-permute-done.11.refs_3_ = bf16[512,256]{1,0:T(8,128)(2,1)S(1)} collective-permute-done((bf16[512,256]{1,0:T(8,128)(2,1)S(1)}, bf16[512,256]{1,0:T(8,128)(2,1)S(1)}, u32[]{:S(2)}, u32[]{:S(2)}) %collective-permute-start.11) | collective-permute-done | bytes 262176 | tf_op jit(solution)/shard_map/ppermute | solution.py:217
  46.0 1.1 %unpack0.1 = (bf16[1,128,2048]{2,1,0:T(8,128)(2,1)}, bf16[1,128,2048]{2,1,0:T(8,128)(2,1)}, bf16[1,128,2048]{2,1,0:T(8,128)(2,1)}, bf16[1,128,2048]{2,1,0:T(8,128)(2,1)}, f32[2,128]{1,0:T(2,128)S(1)}) custom-call(bf16[512,256]{1,0:T(8,128)(2,1)S(1)} %get-tuple-element.45.refs_0_, bf16[512,256]{1,0:T(8,128)(2,1)S(1)} %collective-permute-done.9.refs_1_, ...), custom_call_target="tpu_custom_call" | custom-call | tf_op jit(solution)/shard_map/unpack0/pallas_call | solution.py:120
  47.2 1.1 %collective-permute-done.12 = f32[2,128]{1,0:T(2,128)S(1)} collective-permute-done((f32[2,128]{1,0:T(2,128)S(1)}, f32[2,128]{1,0:T(2,128)S(1)}, u32[]{:S(2)}, u32[]{:S(2)}) %collective-permute-start.12) | collective-permute-done | bytes 1056 | tf_op jit(solution)/shard_map/ppermute | solution.py:217
  48.3 1.6 %collective-permute-start.13 = (f32[2,128]{1,0:T(2,128)S(1)}, f32[2,128]{1,0:T(2,128)S(1)}, u32[]{:S(2)}, u32[]{:S(2)}) collective-permute-start(f32[2,128]{1,0:T(2,128)S(1)} %add.19), channel_id=1, source_target_pairs={{0,2},{1,3},{2,0},{3,1},{4,6},{5,7},{6,4},{7,5},{8,10},{9,11},{10,... | collective-permute-start | bytes 3080 | tf_op jit(solution)/shard_map/ppermute | solution.py:217
  49.9 2.0 %collective-permute-done.13 = f32[2,128]{1,0:T(2,128)S(1)} collective-permute-done((f32[2,128]{1,0:T(2,128)S(1)}, f32[2,128]{1,0:T(2,128)S(1)}, u32[]{:S(2)}, u32[]{:S(2)}) %collective-permute-start.13) | collective-permute-done | bytes 1056 | tf_op jit(solution)/shard_map/ppermute | solution.py:217
  51.9 2.6 %collective-permute-start.14 = (f32[2,128]{1,0:T(2,128)S(1)}, f32[2,128]{1,0:T(2,128)S(1)}, u32[]{:S(2)}, u32[]{:S(2)}) collective-permute-start(f32[2,128]{1,0:T(2,128)S(1)} %add.20), channel_id=1, source_target_pairs={{0,4},{1,5},{2,6},{3,7},{4,0},{5,1},{6,2},{7,3},{8,12},{9,13},{10,... | collective-permute-start | bytes 3080 | tf_op jit(solution)/shard_map/ppermute | solution.py:217
  54.5 1.9 %collective-permute-done.14 = f32[2,128]{1,0:T(2,128)S(1)} collective-permute-done((f32[2,128]{1,0:T(2,128)S(1)}, f32[2,128]{1,0:T(2,128)S(1)}, u32[]{:S(2)}, u32[]{:S(2)}) %collective-permute-start.14) | collective-permute-done | bytes 1056 | tf_op jit(solution)/shard_map/ppermute | solution.py:217
  56.4 1.5 %collective-permute-start.15 = (f32[2,128]{1,0:T(2,128)S(1)}, f32[2,128]{1,0:T(2,128)S(1)}, u32[]{:S(2)}, u32[]{:S(2)}) collective-permute-start(f32[2,128]{1,0:T(2,128)S(1)} %add.21), channel_id=1, source_target_pairs={{0,8},{8,0},{16,24},{24,16},{1,9},{9,1},{17,25},{25,17},{2,10},{10... | collective-permute-start | bytes 3080 | tf_op jit(solution)/shard_map/ppermute | solution.py:217
  57.9 2.1 %collective-permute-done.15 = f32[2,128]{1,0:T(2,128)S(1)} collective-permute-done((f32[2,128]{1,0:T(2,128)S(1)}, f32[2,128]{1,0:T(2,128)S(1)}, u32[]{:S(2)}, u32[]{:S(2)}) %collective-permute-start.15) | collective-permute-done | bytes 1056 | tf_op jit(solution)/shard_map/ppermute | solution.py:217
  60.0 1.8 %collective-permute-start.16 = (f32[2,128]{1,0:T(2,128)S(1)}, f32[2,128]{1,0:T(2,128)S(1)}, u32[]{:S(2)}, u32[]{:S(2)}) collective-permute-start(f32[2,128]{1,0:T(2,128)S(1)} %add.22), channel_id=1, source_target_pairs={{0,16},{8,24},{16,0},{24,8},{1,17},{9,25},{17,1},{25,9},{2,18},{10... | collective-permute-start | bytes 3080 | tf_op jit(solution)/shard_map/ppermute | solution.py:217
  61.8 1.1 %unpack1.1 = (bf16[1,128,2048]{2,1,0:T(8,128)(2,1)}, bf16[1,128,2048]{2,1,0:T(8,128)(2,1)}, bf16[1,128,2048]{2,1,0:T(8,128)(2,1)}, bf16[1,128,2048]{2,1,0:T(8,128)(2,1)}) custom-call(bf16[512,256]{1,0:T(8,128)(2,1)S(1)} %get-tuple-element.41.refs_0_, ...), custom_call_target="tpu_custom_call", output_to_operand_aliasing={{0}: (4, {}), {1}: (5, {}), {2}: (6, {}), {3}: (7, {})} | custom-call | tf_op jit(solution)/shard_map/unpack1/pallas_call | solution.py:120
  (29 shorter events, 3.8 us)
Async XLA Ops:
  0.6 1.0 %copy-start = (bf16[1,128,2048]{2,1,0:T(8,128)(2,1)S(1)}, bf16[1,128,2048]{2,1,0:T(8,128)(2,1)}, u32[]{:S(2)}) copy-start(bf16[1,128,2048]{2,1,0:T(8,128)(2,1)} %refs_0_.3) | copy-start | bytes 1572868
  1.7 1.0 %copy-start.1 = (bf16[1,128,2048]{2,1,0:T(8,128)(2,1)S(1)}, bf16[1,128,2048]{2,1,0:T(8,128)(2,1)}, u32[]{:S(2)}) copy-start(bf16[1,128,2048]{2,1,0:T(8,128)(2,1)} %refs_1_.3) | copy-start | bytes 1572868
  2.7 1.0 %copy-start.2 = (bf16[1,128,2048]{2,1,0:T(8,128)(2,1)S(1)}, bf16[1,128,2048]{2,1,0:T(8,128)(2,1)}, u32[]{:S(2)}) copy-start(bf16[1,128,2048]{2,1,0:T(8,128)(2,1)} %refs_2_.3) | copy-start | bytes 1572868
  3.8 1.0 %copy-start.3 = (bf16[1,128,2048]{2,1,0:T(8,128)(2,1)S(1)}, bf16[1,128,2048]{2,1,0:T(8,128)(2,1)}, u32[]{:S(2)}) copy-start(bf16[1,128,2048]{2,1,0:T(8,128)(2,1)} %refs_3_.3) | copy-start | bytes 1572868
  4.8 0.7 %copy-start.4 = (s32[1,128]{1,0:T(1,128)S(1)}, s32[1,128]{1,0:T(1,128)}, u32[]{:S(2)}) copy-start(s32[1,128]{1,0:T(1,128)} %refs_4_.1) | copy-start | bytes 1540
  5.8 10.3 %collective-permute-start.3 = (bf16[528,256]{1,0:T(8,128)(2,1)S(1)}, bf16[528,256]{1,0:T(8,128)(2,1)S(1)}, u32[]{:S(2)}, u32[]{:S(2)}) collective-permute-start(bf16[528,256]{1,0:T(8,128)(2,1)S(1)} %get-tuple-element.38), channel_id=1, source_target_pairs={{0,8},{8,0},{16,24},{24,16},{1,9},{9,1},{17,25},{25,17},{2,10},{10... | collective-permute-start | bytes 811016 | tf_op jit(solution)/shard_map/ppermute | solution.py:217
  8.8 15.2 %collective-permute-start.4 = (bf16[528,256]{1,0:T(8,128)(2,1)S(1)}, bf16[528,256]{1,0:T(8,128)(2,1)S(1)}, u32[]{:S(2)}, u32[]{:S(2)}) collective-permute-start(bf16[528,256]{1,0:T(8,128)(2,1)S(1)} %get-tuple-element.39), channel_id=1, source_target_pairs={{0,16},{8,24},{16,0},{24,8},{1,17},{9,25},{17,1},{25,9},{2,18},{10... | collective-permute-start | bytes 811016 | tf_op jit(solution)/shard_map/ppermute | solution.py:217
  10.3 13.7 %collective-permute-start.5 = (bf16[528,256]{1,0:T(8,128)(2,1)S(1)}, bf16[528,256]{1,0:T(8,128)(2,1)S(1)}, u32[]{:S(2)}, u32[]{:S(2)}) collective-permute-start(bf16[528,256]{1,0:T(8,128)(2,1)S(1)} %get-tuple-element.40), channel_id=1, source_target_pairs={{0,24},{8,16},{16,8},{24,0},{1,25},{9,17},{17,9},{25,1},{2,26},{10... | collective-permute-start | bytes 811016 | tf_op jit(solution)/shard_map/ppermute | solution.py:217
  10.7 19.6 %collective-permute-start = (bf16[512,256]{1,0:T(8,128)(2,1)S(1)}, bf16[512,256]{1,0:T(8,128)(2,1)S(1)}, u32[]{:S(2)}, u32[]{:S(2)}) collective-permute-start(bf16[512,256]{1,0:T(8,128)(2,1)S(1)} %get-tuple-element.34), channel_id=1, source_target_pairs={{0,8},{8,0},{16,24},{24,16},{1,9},{9,1},{17,25},{25,17},{2,10},{10... | collective-permute-start | bytes 786440 | tf_op jit(solution)/shard_map/ppermute | solution.py:217
  12.7 21.4 %collective-permute-start.1 = (bf16[512,256]{1,0:T(8,128)(2,1)S(1)}, bf16[512,256]{1,0:T(8,128)(2,1)S(1)}, u32[]{:S(2)}, u32[]{:S(2)}) collective-permute-start(bf16[512,256]{1,0:T(8,128)(2,1)S(1)} %get-tuple-element.35), channel_id=1, source_target_pairs={{0,16},{8,24},{16,0},{24,8},{1,17},{9,25},{17,1},{25,9},{2,18},{10... | collective-permute-start | bytes 786440 | tf_op jit(solution)/shard_map/ppermute | solution.py:217
  16.1 18.6 %collective-permute-start.2 = (bf16[512,256]{1,0:T(8,128)(2,1)S(1)}, bf16[512,256]{1,0:T(8,128)(2,1)S(1)}, u32[]{:S(2)}, u32[]{:S(2)}) collective-permute-start(bf16[512,256]{1,0:T(8,128)(2,1)S(1)} %get-tuple-element.36), channel_id=1, source_target_pairs={{0,24},{8,16},{16,8},{24,0},{1,25},{9,17},{17,9},{25,1},{2,26},{10... | collective-permute-start | bytes 786440 | tf_op jit(solution)/shard_map/ppermute | solution.py:217
  24.0 0.7 %copy-start.5 = (f32[128]{0:T(128)S(1)}, f32[128]{0:T(128)}, u32[]{:S(2)}) copy-start(f32[128]{0:T(128)} %param.12) | copy-start | bytes 1540
  24.0 0.7 %copy-start.6 = (f32[128]{0:T(128)S(1)}, f32[128]{0:T(128)}, u32[]{:S(2)}) copy-start(f32[128]{0:T(128)} %param.13) | copy-start | bytes 1540
  28.2 12.1 %collective-permute-start.9 = (bf16[512,256]{1,0:T(8,128)(2,1)S(1)}, bf16[512,256]{1,0:T(8,128)(2,1)S(1)}, u32[]{:S(2)}, u32[]{:S(2)}) collective-permute-start(bf16[512,256]{1,0:T(8,128)(2,1)S(1)} %get-tuple-element.46), channel_id=1, source_target_pairs={{0,8},{8,0},{16,24},{24,16},{1,9},{9,1},{17,25},{25,17},{2,10},{10... | collective-permute-start | bytes 786440 | tf_op jit(solution)/shard_map/ppermute | solution.py:217
  29.2 16.1 %collective-permute-start.10 = (bf16[512,256]{1,0:T(8,128)(2,1)S(1)}, bf16[512,256]{1,0:T(8,128)(2,1)S(1)}, u32[]{:S(2)}, u32[]{:S(2)}) collective-permute-start(bf16[512,256]{1,0:T(8,128)(2,1)S(1)} %get-tuple-element.47), channel_id=1, source_target_pairs={{0,16},{8,24},{16,0},{24,8},{1,17},{9,25},{17,1},{25,9},{2,18},{10... | collective-permute-start | bytes 786440 | tf_op jit(solution)/shard_map/ppermute | solution.py:217
  30.3 15.7 %collective-permute-start.11 = (bf16[512,256]{1,0:T(8,128)(2,1)S(1)}, bf16[512,256]{1,0:T(8,128)(2,1)S(1)}, u32[]{:S(2)}, u32[]{:S(2)}) collective-permute-start(bf16[512,256]{1,0:T(8,128)(2,1)S(1)} %get-tuple-element.48), channel_id=1, source_target_pairs={{0,24},{8,16},{16,8},{24,0},{1,25},{9,17},{17,9},{25,1},{2,26},{10... | collective-permute-start | bytes 786440 | tf_op jit(solution)/shard_map/ppermute | solution.py:217
  38.3 23.5 %collective-permute-start.6 = (bf16[512,256]{1,0:T(8,128)(2,1)S(1)}, bf16[512,256]{1,0:T(8,128)(2,1)S(1)}, u32[]{:S(2)}, u32[]{:S(2)}) collective-permute-start(bf16[512,256]{1,0:T(8,128)(2,1)S(1)} %get-tuple-element.42), channel_id=1, source_target_pairs={{0,8},{8,0},{16,24},{24,16},{1,9},{9,1},{17,25},{25,17},{2,10},{10... | collective-permute-start | bytes 786440 | tf_op jit(solution)/shard_map/ppermute | solution.py:217
  39.8 21.9 %collective-permute-start.7 = (bf16[512,256]{1,0:T(8,128)(2,1)S(1)}, bf16[512,256]{1,0:T(8,128)(2,1)S(1)}, u32[]{:S(2)}, u32[]{:S(2)}) collective-permute-start(bf16[512,256]{1,0:T(8,128)(2,1)S(1)} %get-tuple-element.43), channel_id=1, source_target_pairs={{0,16},{8,24},{16,0},{24,8},{1,17},{9,25},{17,1},{25,9},{2,18},{10... | collective-permute-start | bytes 786440 | tf_op jit(solution)/shard_map/ppermute | solution.py:217
  40.3 21.4 %collective-permute-start.8 = (bf16[512,256]{1,0:T(8,128)(2,1)S(1)}, bf16[512,256]{1,0:T(8,128)(2,1)S(1)}, u32[]{:S(2)}, u32[]{:S(2)}) collective-permute-start(bf16[512,256]{1,0:T(8,128)(2,1)S(1)} %get-tuple-element.44), channel_id=1, source_target_pairs={{0,24},{8,16},{16,8},{24,0},{1,25},{9,17},{17,9},{25,1},{2,26},{10... | collective-permute-start | bytes 786440 | tf_op jit(solution)/shard_map/ppermute | solution.py:217
  47.1 1.2 %collective-permute-start.12 = (f32[2,128]{1,0:T(2,128)S(1)}, f32[2,128]{1,0:T(2,128)S(1)}, u32[]{:S(2)}, u32[]{:S(2)}) collective-permute-start(f32[2,128]{1,0:T(2,128)S(1)} %get-tuple-element.59), channel_id=1, source_target_pairs={{0,1},{1,0},{2,3},{3,2},{4,5},{5,4},{6,7},{7,6},{8,9},{9,8},{10,11... | collective-permute-start | bytes 3080 | tf_op jit(solution)/shard_map/ppermute | solution.py:217
  48.3 3.6 %collective-permute-start.13 = (f32[2,128]{1,0:T(2,128)S(1)}, f32[2,128]{1,0:T(2,128)S(1)}, u32[]{:S(2)}, u32[]{:S(2)}) collective-permute-start(f32[2,128]{1,0:T(2,128)S(1)} %add.19), channel_id=1, source_target_pairs={{0,2},{1,3},{2,0},{3,1},{4,6},{5,7},{6,4},{7,5},{8,10},{9,11},{10,... | collective-permute-start | bytes 3080 | tf_op jit(solution)/shard_map/ppermute | solution.py:217
  51.9 4.5 %collective-permute-start.14 = (f32[2,128]{1,0:T(2,128)S(1)}, f32[2,128]{1,0:T(2,128)S(1)}, u32[]{:S(2)}, u32[]{:S(2)}) collective-permute-start(f32[2,128]{1,0:T(2,128)S(1)} %add.20), channel_id=1, source_target_pairs={{0,4},{1,5},{2,6},{3,7},{4,0},{5,1},{6,2},{7,3},{8,12},{9,13},{10,... | collective-permute-start | bytes 3080 | tf_op jit(solution)/shard_map/ppermute | solution.py:217
  56.4 3.6 %collective-permute-start.15 = (f32[2,128]{1,0:T(2,128)S(1)}, f32[2,128]{1,0:T(2,128)S(1)}, u32[]{:S(2)}, u32[]{:S(2)}) collective-permute-start(f32[2,128]{1,0:T(2,128)S(1)} %add.21), channel_id=1, source_target_pairs={{0,8},{8,0},{16,24},{24,16},{1,9},{9,1},{17,25},{25,17},{2,10},{10... | collective-permute-start | bytes 3080 | tf_op jit(solution)/shard_map/ppermute | solution.py:217
  60.0 3.6 %collective-permute-start.16 = (f32[2,128]{1,0:T(2,128)S(1)}, f32[2,128]{1,0:T(2,128)S(1)}, u32[]{:S(2)}, u32[]{:S(2)}) collective-permute-start(f32[2,128]{1,0:T(2,128)S(1)} %add.22), channel_id=1, source_target_pairs={{0,16},{8,24},{16,0},{24,8},{1,17},{9,25},{17,1},{25,9},{2,18},{10... | collective-permute-start | bytes 3080 | tf_op jit(solution)/shard_map/ppermute | solution.py:217

commit v3 on v1

--- a/solution.py
+++ b/solution.py
@@ -12,7 +12,8 @@
 TENSORS = 4
 ID_ROWS = 16
 SCALE = HEAD_DIM ** (-0.5)
-VMEM_BYTES = 56 * 1024 * 1024
+MIB = 1024 * 1024
+PACK_MIB = 58
 
 
 def dot(a, b, contract):
@@ -35,51 +36,65 @@
     return grad_rows, jnp.sum(grad_out * normed, axis=0, keepdims=True)
 
 
-def pack_kernel(groups, local, chunk, width, with_ids, me_ref, *refs):
+def pack_kernel(groups, local, chunk, width, first, *refs):
     tensors, rest = refs[:TENSORS], refs[TENSORS:]
-    if with_ids:
-        ids_ref, rest = rest[0], rest[1:]
-    outs, sems = rest[:groups], rest[groups]
+    if first:
+        (ids_ref, *gain_refs), rest = rest[:3], rest[3:]
+    outs, rest = rest[:groups], rest[groups:]
+    if first:
+        gain_outs, rest = rest[:2], rest[2:]
+    sems = rest[0]
     rows = tensors[0].shape[1]
-    copies = []
+    pairs = []
+    if first:
+        pairs.append((ids_ref, rest[1]))
+        pairs.extend(zip(gain_refs, gain_outs))
     for shift in range(groups):
-        owner = jnp.bitwise_xor(me_ref[0], shift)
+        owner = jnp.bitwise_xor(lax.axis_index("seq"), shift)
         start = pl.multiple_of(owner * local + chunk * width, HEAD_DIM)
         for t in range(TENSORS):
-            copies.append((
+            pairs.append((
                 tensors[t].at[0, :, pl.ds(start, width)],
                 outs[shift].at[pl.ds(t * rows, rows), :],
             ))
-        if with_ids:
-            copies.append((ids_ref, outs[shift].at[pl.ds(TENSORS * rows, ID_ROWS), :]))
     started = [
         pltpu.make_async_copy(source, target, sems.at[i])
-        for i, (source, target) in enumerate(copies)
+        for i, (source, target) in enumerate(pairs)
     ]
     for copy in started:
         copy.start()
-    for copy in started:
+    if first:
+        started[0].wait()
+        ids = jnp.broadcast_to(rest[1][...].astype(jnp.float32), (ID_ROWS, rows))
+        for out in outs:
+            for column in range(0, width, rows):
+                out[TENSORS * rows :, column : column + rows] = ids.astype(jnp.bfloat16)
+    for copy in started[1 if first else 0 :]:
         copy.wait()
 
 
-def pack(me, arrays, ids_block, groups, local, chunk, width):
+def pack(arrays, slice_ids, gains, groups, local, chunk, width):
     rows = arrays[0].shape[1]
-    with_ids = ids_block is not None
-    height = TENSORS * rows + (ID_ROWS if with_ids else 0)
-    count = groups * (TENSORS + (1 if with_ids else 0))
-    any_spec = pl.BlockSpec(memory_space=pl.ANY)
-    operands = (me,) + tuple(arrays) + ((ids_block,) if with_ids else ())
-    return pl.pallas_call(
-        functools.partial(pack_kernel, groups, local, chunk, width, with_ids),
-        out_shape=[jax.ShapeDtypeStruct((height, width), jnp.bfloat16)] * groups,
-        in_specs=[pl.BlockSpec(memory_space=pltpu.SMEM)] + [any_spec] * (len(operands) - 1),
-        out_specs=[any_spec] * groups,
-        scratch_shapes=[pltpu.SemaphoreType.DMA((count,))],
+    first = chunk == 0
+    height = TENSORS * rows + (ID_ROWS if first else 0)
+    vmem_spec = pl.BlockSpec(memory_space=pltpu.VMEM)
+    operands = tuple(arrays) + ((slice_ids, *gains) if first else ())
+    count = TENSORS * groups + (3 if first else 0)
+    gain_shapes = [jax.ShapeDtypeStruct((1, HEAD_DIM), jnp.float32)] * (2 if first else 0)
+    outs = pl.pallas_call(
+        functools.partial(pack_kernel, groups, local, chunk, width, first),
+        out_shape=[jax.ShapeDtypeStruct((height, width), jnp.bfloat16)] * groups + gain_shapes,
+        in_specs=[pl.BlockSpec(memory_space=pltpu.HBM)] * len(operands),
+        out_specs=[vmem_spec] * (groups + len(gain_shapes)),
+        scratch_shapes=[pltpu.SemaphoreType.DMA((count,))]
+        + ([pltpu.VMEM((1, rows), jnp.int32)] if first else []),
+        compiler_params=pltpu.CompilerParams(vmem_limit_bytes=PACK_MIB * MIB),
         name=f"pack{chunk}",
     )(*operands)
-
-
-def unpack_kernel(groups, local, chunk, width, aliased, me_ref, *refs):
+    return outs[:groups], outs[groups:]
+
+
+def unpack_kernel(groups, local, chunk, width, aliased, *refs):
     pieces, rest = refs[:groups], refs[groups:]
     if aliased:
         rest = rest[TENSORS:]
@@ -87,7 +102,7 @@
     rows = outs[0].shape[1]
     started = []
     for shift in range(groups):
-        owner = jnp.bitwise_xor(me_ref[0], shift)
+        owner = jnp.bitwise_xor(lax.axis_index("seq"), shift)
         start = pl.multiple_of(owner * local + chunk * width, HEAD_DIM)
         for t in range(TENSORS):
             started.append(
@@ -103,19 +118,21 @@
         copy.wait()
 
 
-def unpack(me, pieces, previous, shape, local, chunk, width):
+def unpack(pieces, previous, shape, local, chunk, width):
     groups = len(pieces)
     aliased = previous is not None
-    any_spec = pl.BlockSpec(memory_space=pl.ANY)
-    operands = (me,) + tuple(pieces) + (tuple(previous) if aliased else ())
-    aliases = {1 + groups + t: t for t in range(TENSORS)} if aliased else {}
+    any_spec = pl.BlockSpec(memory_space=pltpu.HBM)
+    vmem_spec = pl.BlockSpec(memory_space=pltpu.VMEM)
+    operands = tuple(pieces) + (tuple(previous) if aliased else ())
+    aliases = {groups + t: t for t in range(TENSORS)} if aliased else {}
     return pl.pallas_call(
         functools.partial(unpack_kernel, groups, local, chunk, width, aliased),
         out_shape=[jax.ShapeDtypeStruct(shape, jnp.bfloat16)] * TENSORS,
-        in_specs=[pl.BlockSpec(memory_space=pltpu.SMEM)] + [any_spec] * (len(operands) - 1),
+        in_specs=[vmem_spec] * groups + [any_spec] * (len(operands) - groups),
         out_specs=[any_spec] * TENSORS,
         scratch_shapes=[pltpu.SemaphoreType.DMA((groups * TENSORS,))],
         input_output_aliases=aliases,
+        compiler_params=pltpu.CompilerParams(vmem_limit_bytes=8 * MIB),
         name=f"unpack{chunk}",
     )(*operands)
 
@@ -192,7 +209,7 @@
         + [jax.ShapeDtypeStruct((2, HEAD_DIM), jnp.float32)],
         in_specs=[piece_spec] * groups + [ids_spec] * groups + [gain_spec] * 2,
         out_specs=[piece_spec] * groups + [pl.BlockSpec((2, HEAD_DIM), lambda i: (0, 0))],
-        compiler_params=pltpu.CompilerParams(vmem_limit_bytes=VMEM_BYTES),
+        compiler_params=pltpu.CompilerParams(vmem_limit_bytes=(24 if length <= 512 else 48) * MIB),
         cost_estimate=pl.CostEstimate(
             flops=12 * area * HEAD_DIM,
             bytes_accessed=4 * groups * height * width,
@@ -200,19 +217,31 @@
         ),
         name=f"attend{chunk}",
     )(*pieces, *id_holders, query_gain, key_gain)
-    return outs[:groups], outs[groups]
+    return list(outs[:groups]), outs[groups]
 
 
 def permute(value, axis, size, shift):
     return lax.ppermute(value, axis, [(i, i ^ shift) for i in range(size)])
 
 
-def total_over(value, axis, size):
-    shift = 1
-    while shift < size:
-        value = value + permute(value, axis, size, shift)
-        shift *= 2
-    return value
+def add_parts_kernel(count, *refs):
+    parts, out = refs[:count], refs[-1]
+    total = parts[0][...]
+    for part in parts[1:]:
+        total = total + part[...]
+    out[...] = total
+
+
+def add_parts(parts, after):
+    vmem_spec = pl.BlockSpec(memory_space=pltpu.VMEM)
+    return pl.pallas_call(
+        functools.partial(add_parts_kernel, len(parts)),
+        out_shape=jax.ShapeDtypeStruct(parts[0].shape, jnp.float32),
+        in_specs=[vmem_spec] * len(parts) + [pl.BlockSpec(memory_space=pl.ANY)] * len(after),
+        out_specs=vmem_spec,
+        compiler_params=pltpu.CompilerParams(vmem_limit_bytes=4 * MIB),
+        name="add_parts",
+    )(*parts, *after)
 
 
 def per_device(queries, key_rows, values, cotangent, slice_ids, query_gain, key_gain):
@@ -222,37 +251,35 @@
     chunks = 2 if local >= 2 * HEAD_DIM else 1
     chunk_width = local // chunks
     heads = chunk_width // HEAD_DIM
-    me = lax.axis_index("seq").astype(jnp.int32).reshape(1)
     arrays = (queries, key_rows, values, cotangent)
-    ids_block = jnp.pad(
-        slice_ids.astype(jnp.bfloat16), ((0, ID_ROWS - 1), (0, chunk_width - rows))
-    )
     gains = (query_gain.reshape(1, HEAD_DIM), key_gain.reshape(1, HEAD_DIM))
 
     received = []
     for chunk in range(chunks):
-        payloads = pack(
-            me, arrays, ids_block if chunk == 0 else None, groups, local, chunk, chunk_width
-        )
+        payloads, staged = pack(arrays, slice_ids, gains, groups, local, chunk, chunk_width)
+        if chunk == 0:
+            gains = staged
         received.append(
             [payloads[0]]
             + [permute(payloads[shift], "seq", groups, shift) for shift in range(1, groups)]
         )
-    returned, gain_total = [], None
+    returned, gain_parts = [], []
     for chunk in range(chunks):
         results, gain_part = attend(
             received[chunk], received[0], gains[0], gains[1], rows, heads, chunk
         )
-        gain_total = gain_part if gain_total is None else gain_total + gain_part
+        gain_parts.append(gain_part)
         returned.append(
             [results[0]]
             + [permute(results[shift], "seq", groups, shift) for shift in range(1, groups)]
         )
-    gain_total = total_over(gain_total, "dp", batches)
-    gain_total = total_over(gain_total, "seq", groups)
+    gain_total = add_parts(gain_parts, [returned[0][1], returned[0][2]])
+    for axis, size in (("dp", batches), ("seq", groups)):
+        for step in range(size.bit_length() - 1):
+            gain_total = gain_total + permute(gain_total, axis, size, 1 << step)
     outputs = None
     for chunk in range(chunks):
-        outputs = unpack(me, returned[chunk], outputs, queries.shape, local, chunk, chunk_width)
+        outputs = unpack(returned[chunk], outputs, queries.shape, local, chunk, chunk_width)
     return (*outputs, gain_total[0], gain_total[1])
 
 

time: 198 us -> 58.1 us (0.29)
  Pallas kernels: 144 us -> 14.1 us
  waiting for transfers between devices: 25.2 us -> 16 us
  local copies, waits for them, and re-layouts: 5.64 us -> 1.19 us
  starting transfers between devices: 22.1 us -> 25.7 us
    pallas_call x2, Pallas kernels: 66 us -> 2.19 us  [unpack(): pl.pallas_call(functools.partial(unpack_kernel, groups, local, chunk, wid...]
    pallas_call x2, Pallas kernels: 67 us -> 4.87 us  [pack(): pl.pallas_call(functools.partial(pack_kernel, groups, local, chunk, width...]
    ppermute x17, waiting for transfers between devices: 25.2 us -> 16 us  [permute(): return lax.ppermute(value, axis, [(i, i ^ shift) for i in range(size)])]
    pallas_call x2, Pallas kernels: 11.3 us -> 7.03 us  [attend(): pl.pallas_call(functools.partial(attend_kernel, groups, rows, heads, bloc...]
    unnamed x34 -> x8, local copies, waits for them, and re-layouts: 4.52 us -> 0.67 us
    ppermute x17, starting transfers between devices: 22.1 us -> 25.7 us  [permute(): return lax.ppermute(value, axis, [(i, i ^ shift) for i in range(size)])]
  transfers between devices with their start and end apart: 17 -> 17, of which waited for: 8 -> 7; matrix products, arithmetic and copies ran while one was open for 0% -> 0% of each run, Pallas kernels for 39% -> 20%
where the time goes in v3:
time: 58.1 us; the launch traced here: 57.8 us
  starting transfers between devices  25.7 us (44%)
  waiting for transfers between devices  16 us (28%)
  Pallas kernels  14.1 us (24%)
  local copies, waits for them, and re-layouts  1.19 us (2%)
  between operations  0.74 us (1%)
    ppermute x17, starting transfers between devices, permute(): return lax.ppermute(value, axis, [(i, i ^ shift) for i in range(size)])  25.7 us
    ppermute x17, waiting for transfers between devices, permute(): return lax.ppermute(value, axis, [(i, i ^ shift) for i in range(size)])  16 us
    pallas_call x2, Pallas kernels, attend(): pl.pallas_call(functools.partial(attend_kernel, groups, rows, heads, bloc...  7.03 us
    pallas_call x2, Pallas kernels, pack(): pl.pallas_call(functools.partial(pack_kernel, groups, local, chunk, width...  4.87 us
    pallas_call x2, Pallas kernels, unpack(): pl.pallas_call(functools.partial(unpack_kernel, groups, local, chunk, wid...  2.19 us
  transfers between devices with their start and end apart: 17, of which 7 were waited for; matrix products, arithmetic and copies ran while one was open for 0% of the time, Pallas kernels for 20%

profile of v3, /device:TPU:0, one launch (start us, length us, event | category | flops | bytes accessed | tf_op | source)
XLA Modules:
  0.0 57.8 jit_solution(2072507568271805269)
XLA Ops:
  0.6 2.4 %pack0.1 = (bf16[528,256]{1,0:T(8,128)(2,1)}, bf16[528,256]{1,0:T(8,128)(2,1)}, bf16[528,256]{1,0:T(8,128)(2,1)}, bf16[528,256]{1,0:T(8,128)(2,1)}, f32[1,128]{1,0:T(1,128)}, /*index=5*/f32[1,128]{1,0:T(1,128)}) custom-call(bf16[1,128,2048]{2,1,0:T(8,128)(2,1)} %refs_0_.3, bf16[1,128,2048]{2,1,0:T(8,128)(2,1)} %refs_1_.3, bf16[1,128,2048]{2,1,0:T(8,128)(2,1)} %refs_2_.3, ...), custom_call_target="tpu_custom_call" | custom-call | tf_op jit(solution)/shard_map/pack0/pallas_call | solution.py:84
  3.1 3.0 %collective-permute-start.3 = (bf16[528,256]{1,0:T(8,128)(2,1)}, bf16[528,256]{1,0:T(8,128)(2,1)S(1)}, u32[]{:S(2)}, u32[]{:S(2)}) collective-permute-start(bf16[528,256]{1,0:T(8,128)(2,1)} %get-tuple-element.39), channel_id=1, source_target_pairs={{0,8},{8,0},{16,24},{24,16},{1,9},{9,1},{17,25},{25,17},{2,10},{10... | collective-permute-start | bytes 811016 | tf_op jit(solution)/shard_map/ppermute | solution.py:224
  6.1 1.5 %collective-permute-start.4 = (bf16[528,256]{1,0:T(8,128)(2,1)}, bf16[528,256]{1,0:T(8,128)(2,1)S(1)}, u32[]{:S(2)}, u32[]{:S(2)}) collective-permute-start(bf16[528,256]{1,0:T(8,128)(2,1)} %get-tuple-element.40), channel_id=1, source_target_pairs={{0,16},{8,24},{16,0},{24,8},{1,17},{9,25},{17,1},{25,9},{2,18},{10... | collective-permute-start | bytes 811016 | tf_op jit(solution)/shard_map/ppermute | solution.py:224
  7.6 0.0 collective-permute-start.5
  7.6 2.4 %pack1.1 = (bf16[512,256]{1,0:T(8,128)(2,1)}, bf16[512,256]{1,0:T(8,128)(2,1)}, bf16[512,256]{1,0:T(8,128)(2,1)}, bf16[512,256]{1,0:T(8,128)(2,1)}) custom-call(bf16[1,128,2048]{2,1,0:T(8,128)(2,1)} %refs_0_.3, bf16[1,128,2048]{2,1,0:T(8,128)(2,1)} %refs_1_.3, bf16[1,128,2048]{2,1,0:T(8,128)(2,1)} %refs_2_.3, bf16[1,128,2048]{2,1,0:T(8,128)(2,1)} %refs_3_.3), custom_call_target="tpu_custom_call" | custom-call | tf_op jit(solution)/shard_map/pack1/pallas_call | solution.py:84
  10.1 2.0 %collective-permute-start = (bf16[512,256]{1,0:T(8,128)(2,1)}, bf16[512,256]{1,0:T(8,128)(2,1)S(1)}, u32[]{:S(2)}, u32[]{:S(2)}) collective-permute-start(bf16[512,256]{1,0:T(8,128)(2,1)} %get-tuple-element.35), channel_id=1, source_target_pairs={{0,8},{8,0},{16,24},{24,16},{1,9},{9,1},{17,25},{25,17},{2,10},{10... | collective-permute-start | bytes 786440 | tf_op jit(solution)/shard_map/ppermute | solution.py:224
  12.0 1.5 %collective-permute-start.1 = (bf16[512,256]{1,0:T(8,128)(2,1)}, bf16[512,256]{1,0:T(8,128)(2,1)S(1)}, u32[]{:S(2)}, u32[]{:S(2)}) collective-permute-start(bf16[512,256]{1,0:T(8,128)(2,1)} %get-tuple-element.36), channel_id=1, source_target_pairs={{0,16},{8,24},{16,0},{24,8},{1,17},{9,25},{17,1},{25,9},{2,18},{10... | collective-permute-start | bytes 786440 | tf_op jit(solution)/shard_map/ppermute | solution.py:224
  13.6 0.0 collective-permute-done.3.refs_5_.refs_1_
  13.6 3.0 %collective-permute-start.2 = (bf16[512,256]{1,0:T(8,128)(2,1)}, bf16[512,256]{1,0:T(8,128)(2,1)S(1)}, u32[]{:S(2)}, u32[]{:S(2)}) collective-permute-start(bf16[512,256]{1,0:T(8,128)(2,1)} %get-tuple-element.37), channel_id=1, source_target_pairs={{0,24},{8,16},{16,8},{24,0},{1,25},{9,17},{17,9},{25,1},{2,26},{10... | collective-permute-start | bytes 786440 | tf_op jit(solution)/shard_map/ppermute | solution.py:224
  16.6 4.4 %collective-permute-done.4.refs_6_.refs_2_ = bf16[528,256]{1,0:T(8,128)(2,1)S(1)} collective-permute-done((bf16[528,256]{1,0:T(8,128)(2,1)}, bf16[528,256]{1,0:T(8,128)(2,1)S(1)}, u32[]{:S(2)}, u32[]{:S(2)}) %collective-permute-start.4) | collective-permute-done | bytes 270368 | tf_op jit(solution)/shard_map/ppermute | solution.py:224
  21.0 0.6 %copy-done.2 = f32[1,128]{1,0:T(1,128)S(1)} copy-done((f32[1,128]{1,0:T(1,128)S(1)}, f32[1,128]{1,0:T(1,128)}, u32[]{:S(2)}) %copy-start.2) | copy-done | bytes 536
  21.7 3.5 %attend0.1 = (bf16[512,256]{1,0:T(8,128)(2,1)S(1)}, bf16[512,256]{1,0:T(8,128)(2,1)S(1)}, bf16[512,256]{1,0:T(8,128)(2,1)S(1)}, bf16[512,256]{1,0:T(8,128)(2,1)S(1)}, f32[2,128]{1,0:T(2,128)S(1)}) custom-call(bf16[528,256]{1,0:T(8,128)(2,1)S(1)} %copy-done, bf16[528,256]{1,0:T(8,128)(2,1)S(1)} %collective-permute-done.3.refs_5_.refs_1_, ...), custom_call_target="tpu_custom_call" | custom-call | flops 805306368 | bytes 2097152 | tf_op jit(solution)/shard_map/attend0/pallas_call | solution.py:205
  25.2 1.5 %collective-permute-start.9 = (bf16[512,256]{1,0:T(8,128)(2,1)S(1)}, bf16[512,256]{1,0:T(8,128)(2,1)S(1)}, u32[]{:S(2)}, u32[]{:S(2)}) collective-permute-start(bf16[512,256]{1,0:T(8,128)(2,1)S(1)} %get-tuple-element.49), channel_id=1, source_target_pairs={{0,8},{8,0},{16,24},{24,16},{1,9},{9,1},{17,25},{25,17},{2,10},{10... | collective-permute-start | bytes 786440 | tf_op jit(solution)/shard_map/ppermute | solution.py:224
  26.7 0.6 %collective-permute-start.10 = (bf16[512,256]{1,0:T(8,128)(2,1)S(1)}, bf16[512,256]{1,0:T(8,128)(2,1)S(1)}, u32[]{:S(2)}, u32[]{:S(2)}) collective-permute-start(bf16[512,256]{1,0:T(8,128)(2,1)S(1)} %get-tuple-element.50), channel_id=1, source_target_pairs={{0,16},{8,24},{16,0},{24,8},{1,17},{9,25},{17,1},{25,9},{2,18},{10... | collective-permute-start | bytes 786440 | tf_op jit(solution)/shard_map/ppermute | solution.py:224
  27.4 4.3 %collective-permute-done.1.refs_2_ = bf16[512,256]{1,0:T(8,128)(2,1)S(1)} collective-permute-done((bf16[512,256]{1,0:T(8,128)(2,1)}, bf16[512,256]{1,0:T(8,128)(2,1)S(1)}, u32[]{:S(2)}, u32[]{:S(2)}) %collective-permute-start.1) | collective-permute-done | bytes 262176 | tf_op jit(solution)/shard_map/ppermute | solution.py:224
  31.7 0.5 collective-permute-done.2.refs_3_
  32.2 3.5 %attend1.1 = (bf16[512,256]{1,0:T(8,128)(2,1)S(1)}, bf16[512,256]{1,0:T(8,128)(2,1)S(1)}, bf16[512,256]{1,0:T(8,128)(2,1)S(1)}, bf16[512,256]{1,0:T(8,128)(2,1)S(1)}, f32[2,128]{1,0:T(2,128)S(1)}) custom-call(bf16[512,256]{1,0:T(8,128)(2,1)S(1)} %copy-done.1, bf16[512,256]{1,0:T(8,128)(2,1)S(1)} %collective-permute-done.refs_1_, ...), custom_call_target="tpu_custom_call" | custom-call | flops 805306368 | bytes 2097152 | tf_op jit(solution)/shard_map/attend1/pallas_call | solution.py:205
  35.8 1.6 %collective-permute-start.6 = (bf16[512,256]{1,0:T(8,128)(2,1)S(1)}, bf16[512,256]{1,0:T(8,128)(2,1)S(1)}, u32[]{:S(2)}, u32[]{:S(2)}) collective-permute-start(bf16[512,256]{1,0:T(8,128)(2,1)S(1)} %get-tuple-element.45), channel_id=1, source_target_pairs={{0,8},{8,0},{16,24},{24,16},{1,9},{9,1},{17,25},{25,17},{2,10},{10... | collective-permute-start | bytes 786440 | tf_op jit(solution)/shard_map/ppermute | solution.py:224
  37.3 1.8 %collective-permute-start.11 = (bf16[512,256]{1,0:T(8,128)(2,1)S(1)}, bf16[512,256]{1,0:T(8,128)(2,1)S(1)}, u32[]{:S(2)}, u32[]{:S(2)}) collective-permute-start(bf16[512,256]{1,0:T(8,128)(2,1)S(1)} %get-tuple-element.51), channel_id=1, source_target_pairs={{0,24},{8,16},{16,8},{24,0},{1,25},{9,17},{17,9},{25,1},{2,26},{10... | collective-permute-start | bytes 786440 | tf_op jit(solution)/shard_map/ppermute | solution.py:224
  39.1 0.2 collective-permute-start.7
  39.3 1.4 %collective-permute-start.8 = (bf16[512,256]{1,0:T(8,128)(2,1)S(1)}, bf16[512,256]{1,0:T(8,128)(2,1)S(1)}, u32[]{:S(2)}, u32[]{:S(2)}) collective-permute-start(bf16[512,256]{1,0:T(8,128)(2,1)S(1)} %get-tuple-element.47), channel_id=1, source_target_pairs={{0,24},{8,16},{16,8},{24,0},{1,25},{9,17},{17,9},{25,1},{2,26},{10... | collective-permute-start | bytes 786440 | tf_op jit(solution)/shard_map/ppermute | solution.py:224
  40.8 1.1 %collective-permute-done.12 = f32[2,128]{1,0:T(2,128)S(1)} collective-permute-done((f32[2,128]{1,0:T(2,128)S(1)}, f32[2,128]{1,0:T(2,128)S(1)}, u32[]{:S(2)}, u32[]{:S(2)}) %collective-permute-start.12) | collective-permute-done | bytes 1056 | tf_op jit(solution)/shard_map/ppermute | solution.py:224
  41.9 1.6 %collective-permute-start.13 = (f32[2,128]{1,0:T(2,128)S(1)}, f32[2,128]{1,0:T(2,128)S(1)}, u32[]{:S(2)}, u32[]{:S(2)}) collective-permute-start(f32[2,128]{1,0:T(2,128)S(1)} %add.15), channel_id=1, source_target_pairs={{0,2},{1,3},{2,0},{3,1},{4,6},{5,7},{6,4},{7,5},{8,10},{9,11},{10,... | collective-permute-start | bytes 3080 | tf_op jit(solution)/shard_map/ppermute | solution.py:224
  43.5 2.0 %collective-permute-done.13 = f32[2,128]{1,0:T(2,128)S(1)} collective-permute-done((f32[2,128]{1,0:T(2,128)S(1)}, f32[2,128]{1,0:T(2,128)S(1)}, u32[]{:S(2)}, u32[]{:S(2)}) %collective-permute-start.13) | collective-permute-done | bytes 1056 | tf_op jit(solution)/shard_map/ppermute | solution.py:224
  45.5 2.6 %collective-permute-start.14 = (f32[2,128]{1,0:T(2,128)S(1)}, f32[2,128]{1,0:T(2,128)S(1)}, u32[]{:S(2)}, u32[]{:S(2)}) collective-permute-start(f32[2,128]{1,0:T(2,128)S(1)} %add.16), channel_id=1, source_target_pairs={{0,4},{1,5},{2,6},{3,7},{4,0},{5,1},{6,2},{7,3},{8,12},{9,13},{10,... | collective-permute-start | bytes 3080 | tf_op jit(solution)/shard_map/ppermute | solution.py:224
  48.1 1.9 %collective-permute-done.14 = f32[2,128]{1,0:T(2,128)S(1)} collective-permute-done((f32[2,128]{1,0:T(2,128)S(1)}, f32[2,128]{1,0:T(2,128)S(1)}, u32[]{:S(2)}, u32[]{:S(2)}) %collective-permute-start.14) | collective-permute-done | bytes 1056 | tf_op jit(solution)/shard_map/ppermute | solution.py:224
  50.0 1.9 %collective-permute-start.15 = (f32[2,128]{1,0:T(2,128)S(1)}, f32[2,128]{1,0:T(2,128)S(1)}, u32[]{:S(2)}, u32[]{:S(2)}) collective-permute-start(f32[2,128]{1,0:T(2,128)S(1)} %add.17), channel_id=1, source_target_pairs={{0,8},{8,0},{16,24},{24,16},{1,9},{9,1},{17,25},{25,17},{2,10},{10... | collective-permute-start | bytes 3080 | tf_op jit(solution)/shard_map/ppermute | solution.py:224
  51.8 1.7 %collective-permute-done.15 = f32[2,128]{1,0:T(2,128)S(1)} collective-permute-done((f32[2,128]{1,0:T(2,128)S(1)}, f32[2,128]{1,0:T(2,128)S(1)}, u32[]{:S(2)}, u32[]{:S(2)}) %collective-permute-start.15) | collective-permute-done | bytes 1056 | tf_op jit(solution)/shard_map/ppermute | solution.py:224
  53.5 1.5 %collective-permute-start.16 = (f32[2,128]{1,0:T(2,128)S(1)}, f32[2,128]{1,0:T(2,128)S(1)}, u32[]{:S(2)}, u32[]{:S(2)}) collective-permute-start(f32[2,128]{1,0:T(2,128)S(1)} %add.18), channel_id=1, source_target_pairs={{0,16},{8,24},{16,0},{24,8},{1,17},{9,25},{17,1},{25,9},{2,18},{10... | collective-permute-start | bytes 3080 | tf_op jit(solution)/shard_map/ppermute | solution.py:224
  55.1 1.1 %unpack0.1 = (bf16[1,128,2048]{2,1,0:T(8,128)(2,1)}, bf16[1,128,2048]{2,1,0:T(8,128)(2,1)}, bf16[1,128,2048]{2,1,0:T(8,128)(2,1)}, bf16[1,128,2048]{2,1,0:T(8,128)(2,1)}) custom-call(bf16[512,256]{1,0:T(8,128)(2,1)S(1)} %get-tuple-element.48.refs_0_, bf16[512,256]{1,0:T(8,128)(2,1)S(1)} %collective-permute-done.9.refs_1_.refs_2_, ...), custom_call_target="tpu_custom_call" | custom-call | tf_op jit(solution)/shard_map/unpack0/pallas_call | solution.py:128
  56.2 1.1 %unpack1.1 = (bf16[1,128,2048]{2,1,0:T(8,128)(2,1)}, bf16[1,128,2048]{2,1,0:T(8,128)(2,1)}, bf16[1,128,2048]{2,1,0:T(8,128)(2,1)}, bf16[1,128,2048]{2,1,0:T(8,128)(2,1)}) custom-call(bf16[512,256]{1,0:T(8,128)(2,1)S(1)} %get-tuple-element.44.refs_0_, ...), custom_call_target="tpu_custom_call", output_to_operand_aliasing={{0}: (4, {}), {1}: (5, {}), {2}: (6, {}), {3}: (7, {})} | custom-call | tf_op jit(solution)/shard_map/unpack1/pallas_call | solution.py:128
  57.3 0.5 slice_bitcast_fusion
  (23 shorter events, 0.1 us)
Async XLA Ops:
  3.1 10.5 %collective-permute-start.3 = (bf16[528,256]{1,0:T(8,128)(2,1)}, bf16[528,256]{1,0:T(8,128)(2,1)S(1)}, u32[]{:S(2)}, u32[]{:S(2)}) collective-permute-start(bf16[528,256]{1,0:T(8,128)(2,1)} %get-tuple-element.39), channel_id=1, source_target_pairs={{0,8},{8,0},{16,24},{24,16},{1,9},{9,1},{17,25},{25,17},{2,10},{10... | collective-permute-start | bytes 811016 | tf_op jit(solution)/shard_map/ppermute | solution.py:224
  6.1 14.9 %collective-permute-start.4 = (bf16[528,256]{1,0:T(8,128)(2,1)}, bf16[528,256]{1,0:T(8,128)(2,1)S(1)}, u32[]{:S(2)}, u32[]{:S(2)}) collective-permute-start(bf16[528,256]{1,0:T(8,128)(2,1)} %get-tuple-element.40), channel_id=1, source_target_pairs={{0,16},{8,24},{16,0},{24,8},{1,17},{9,25},{17,1},{25,9},{2,18},{10... | collective-permute-start | bytes 811016 | tf_op jit(solution)/shard_map/ppermute | solution.py:224
  7.6 13.4 %copy-start = (bf16[528,256]{1,0:T(8,128)(2,1)S(1)}, bf16[528,256]{1,0:T(8,128)(2,1)}, u32[]{:S(2)}) copy-start(bf16[528,256]{1,0:T(8,128)(2,1)} %get-tuple-element.38.refs_4_.refs_0_) | copy-start | bytes 811012
  7.6 13.4 %collective-permute-start.5 = (bf16[528,256]{1,0:T(8,128)(2,1)}, bf16[528,256]{1,0:T(8,128)(2,1)S(1)}, u32[]{:S(2)}, u32[]{:S(2)}) collective-permute-start(bf16[528,256]{1,0:T(8,128)(2,1)} %get-tuple-element.41), channel_id=1, source_target_pairs={{0,24},{8,16},{16,8},{24,0},{1,25},{9,17},{17,9},{25,1},{2,26},{10... | collective-permute-start | bytes 811016 | tf_op jit(solution)/shard_map/ppermute | solution.py:224
  10.1 17.3 %collective-permute-start = (bf16[512,256]{1,0:T(8,128)(2,1)}, bf16[512,256]{1,0:T(8,128)(2,1)S(1)}, u32[]{:S(2)}, u32[]{:S(2)}) collective-permute-start(bf16[512,256]{1,0:T(8,128)(2,1)} %get-tuple-element.35), channel_id=1, source_target_pairs={{0,8},{8,0},{16,24},{24,16},{1,9},{9,1},{17,25},{25,17},{2,10},{10... | collective-permute-start | bytes 786440 | tf_op jit(solution)/shard_map/ppermute | solution.py:224
  12.0 19.7 %collective-permute-start.1 = (bf16[512,256]{1,0:T(8,128)(2,1)}, bf16[512,256]{1,0:T(8,128)(2,1)S(1)}, u32[]{:S(2)}, u32[]{:S(2)}) collective-permute-start(bf16[512,256]{1,0:T(8,128)(2,1)} %get-tuple-element.36), channel_id=1, source_target_pairs={{0,16},{8,24},{16,0},{24,8},{1,17},{9,25},{17,1},{25,9},{2,18},{10... | collective-permute-start | bytes 786440 | tf_op jit(solution)/shard_map/ppermute | solution.py:224
  13.6 18.6 %collective-permute-start.2 = (bf16[512,256]{1,0:T(8,128)(2,1)}, bf16[512,256]{1,0:T(8,128)(2,1)S(1)}, u32[]{:S(2)}, u32[]{:S(2)}) collective-permute-start(bf16[512,256]{1,0:T(8,128)(2,1)} %get-tuple-element.37), channel_id=1, source_target_pairs={{0,24},{8,16},{16,8},{24,0},{1,25},{9,17},{17,9},{25,1},{2,26},{10... | collective-permute-start | bytes 786440 | tf_op jit(solution)/shard_map/ppermute | solution.py:224
  21.0 0.7 %copy-start.2 = (f32[1,128]{1,0:T(1,128)S(1)}, f32[1,128]{1,0:T(1,128)}, u32[]{:S(2)}) copy-start(f32[1,128]{1,0:T(1,128)} %get-tuple-element.42.refs_8_) | copy-start | bytes 1540
  21.0 0.7 %copy-start.3 = (f32[1,128]{1,0:T(1,128)S(1)}, f32[1,128]{1,0:T(1,128)}, u32[]{:S(2)}) copy-start(f32[1,128]{1,0:T(1,128)} %get-tuple-element.43.refs_9_) | copy-start | bytes 1540
  21.7 10.6 %copy-start.1 = (bf16[512,256]{1,0:T(8,128)(2,1)S(1)}, bf16[512,256]{1,0:T(8,128)(2,1)}, u32[]{:S(2)}) copy-start(bf16[512,256]{1,0:T(8,128)(2,1)} %get-tuple-element.34.refs_0_) | copy-start | bytes 786436
  25.2 14.1 %collective-permute-start.9 = (bf16[512,256]{1,0:T(8,128)(2,1)S(1)}, bf16[512,256]{1,0:T(8,128)(2,1)S(1)}, u32[]{:S(2)}, u32[]{:S(2)}) collective-permute-start(bf16[512,256]{1,0:T(8,128)(2,1)S(1)} %get-tuple-element.49), channel_id=1, source_target_pairs={{0,8},{8,0},{16,24},{24,16},{1,9},{9,1},{17,25},{25,17},{2,10},{10... | collective-permute-start | bytes 786440 | tf_op jit(solution)/shard_map/ppermute | solution.py:224
  26.7 14.0 %collective-permute-start.10 = (bf16[512,256]{1,0:T(8,128)(2,1)S(1)}, bf16[512,256]{1,0:T(8,128)(2,1)S(1)}, u32[]{:S(2)}, u32[]{:S(2)}) collective-permute-start(bf16[512,256]{1,0:T(8,128)(2,1)S(1)} %get-tuple-element.50), channel_id=1, source_target_pairs={{0,16},{8,24},{16,0},{24,8},{1,17},{9,25},{17,1},{25,9},{2,18},{10... | collective-permute-start | bytes 786440 | tf_op jit(solution)/shard_map/ppermute | solution.py:224
  35.8 20.4 %collective-permute-start.6 = (bf16[512,256]{1,0:T(8,128)(2,1)S(1)}, bf16[512,256]{1,0:T(8,128)(2,1)S(1)}, u32[]{:S(2)}, u32[]{:S(2)}) collective-permute-start(bf16[512,256]{1,0:T(8,128)(2,1)S(1)} %get-tuple-element.45), channel_id=1, source_target_pairs={{0,8},{8,0},{16,24},{24,16},{1,9},{9,1},{17,25},{25,17},{2,10},{10... | collective-permute-start | bytes 786440 | tf_op jit(solution)/shard_map/ppermute | solution.py:224
  37.3 17.7 %collective-permute-start.11 = (bf16[512,256]{1,0:T(8,128)(2,1)S(1)}, bf16[512,256]{1,0:T(8,128)(2,1)S(1)}, u32[]{:S(2)}, u32[]{:S(2)}) collective-permute-start(bf16[512,256]{1,0:T(8,128)(2,1)S(1)} %get-tuple-element.51), channel_id=1, source_target_pairs={{0,24},{8,16},{16,8},{24,0},{1,25},{9,17},{17,9},{25,1},{2,26},{10... | collective-permute-start | bytes 786440 | tf_op jit(solution)/shard_map/ppermute | solution.py:224
  39.1 17.0 %collective-permute-start.7 = (bf16[512,256]{1,0:T(8,128)(2,1)S(1)}, bf16[512,256]{1,0:T(8,128)(2,1)S(1)}, u32[]{:S(2)}, u32[]{:S(2)}) collective-permute-start(bf16[512,256]{1,0:T(8,128)(2,1)S(1)} %get-tuple-element.46), channel_id=1, source_target_pairs={{0,16},{8,24},{16,0},{24,8},{1,17},{9,25},{17,1},{25,9},{2,18},{10... | collective-permute-start | bytes 786440 | tf_op jit(solution)/shard_map/ppermute | solution.py:224
  39.3 16.9 %collective-permute-start.8 = (bf16[512,256]{1,0:T(8,128)(2,1)S(1)}, bf16[512,256]{1,0:T(8,128)(2,1)S(1)}, u32[]{:S(2)}, u32[]{:S(2)}) collective-permute-start(bf16[512,256]{1,0:T(8,128)(2,1)S(1)} %get-tuple-element.47), channel_id=1, source_target_pairs={{0,24},{8,16},{16,8},{24,0},{1,25},{9,17},{17,9},{25,1},{2,26},{10... | collective-permute-start | bytes 786440 | tf_op jit(solution)/shard_map/ppermute | solution.py:224
  40.8 1.1 %collective-permute-start.12 = (f32[2,128]{1,0:T(2,128)S(1)}, f32[2,128]{1,0:T(2,128)S(1)}, u32[]{:S(2)}, u32[]{:S(2)}) collective-permute-start(f32[2,128]{1,0:T(2,128)S(1)} %add_parts.1), channel_id=1, source_target_pairs={{0,1},{1,0},{2,3},{3,2},{4,5},{5,4},{6,7},{7,6},{8,9},{9,8},{10,11... | collective-permute-start | bytes 3080 | tf_op jit(solution)/shard_map/ppermute | solution.py:224
  41.9 3.6 %collective-permute-start.13 = (f32[2,128]{1,0:T(2,128)S(1)}, f32[2,128]{1,0:T(2,128)S(1)}, u32[]{:S(2)}, u32[]{:S(2)}) collective-permute-start(f32[2,128]{1,0:T(2,128)S(1)} %add.15), channel_id=1, source_target_pairs={{0,2},{1,3},{2,0},{3,1},{4,6},{5,7},{6,4},{7,5},{8,10},{9,11},{10,... | collective-permute-start | bytes 3080 | tf_op jit(solution)/shard_map/ppermute | solution.py:224
  45.5 4.5 %collective-permute-start.14 = (f32[2,128]{1,0:T(2,128)S(1)}, f32[2,128]{1,0:T(2,128)S(1)}, u32[]{:S(2)}, u32[]{:S(2)}) collective-permute-start(f32[2,128]{1,0:T(2,128)S(1)} %add.16), channel_id=1, source_target_pairs={{0,4},{1,5},{2,6},{3,7},{4,0},{5,1},{6,2},{7,3},{8,12},{9,13},{10,... | collective-permute-start | bytes 3080 | tf_op jit(solution)/shard_map/ppermute | solution.py:224
  50.0 3.6 %collective-permute-start.15 = (f32[2,128]{1,0:T(2,128)S(1)}, f32[2,128]{1,0:T(2,128)S(1)}, u32[]{:S(2)}, u32[]{:S(2)}) collective-permute-start(f32[2,128]{1,0:T(2,128)S(1)} %add.17), channel_id=1, source_target_pairs={{0,8},{8,0},{16,24},{24,16},{1,9},{9,1},{17,25},{25,17},{2,10},{10... | collective-permute-start | bytes 3080 | tf_op jit(solution)/shard_map/ppermute | solution.py:224
  53.5 3.8 %collective-permute-start.16 = (f32[2,128]{1,0:T(2,128)S(1)}, f32[2,128]{1,0:T(2,128)S(1)}, u32[]{:S(2)}, u32[]{:S(2)}) collective-permute-start(f32[2,128]{1,0:T(2,128)S(1)} %add.18), channel_id=1, source_target_pairs={{0,16},{8,24},{16,0},{24,8},{1,17},{9,25},{17,1},{25,9},{2,18},{10... | collective-permute-start | bytes 3080 | tf_op jit(solution)/shard_map/ppermute | solution.py:224

commit v4 on v3

--- a/solution.py
+++ b/solution.py
@@ -13,7 +13,6 @@
 ID_ROWS = 16
 SCALE = HEAD_DIM ** (-0.5)
 MIB = 1024 * 1024
-PACK_MIB = 58
 
 
 def dot(a, b, contract):
@@ -78,7 +77,10 @@
     first = chunk == 0
     height = TENSORS * rows + (ID_ROWS if first else 0)
     vmem_spec = pl.BlockSpec(memory_space=pltpu.VMEM)
-    operands = tuple(arrays) + ((slice_ids, *gains) if first else ())
+    operands = tuple(
+        pltpu.with_memory_space_constraint(x, pltpu.HBM)
+        for x in tuple(arrays) + ((slice_ids, *gains) if first else ())
+    )
     count = TENSORS * groups + (3 if first else 0)
     gain_shapes = [jax.ShapeDtypeStruct((1, HEAD_DIM), jnp.float32)] * (2 if first else 0)
     outs = pl.pallas_call(
@@ -88,7 +90,7 @@
         out_specs=[vmem_spec] * (groups + len(gain_shapes)),
         scratch_shapes=[pltpu.SemaphoreType.DMA((count,))]
         + ([pltpu.VMEM((1, rows), jnp.int32)] if first else []),
-        compiler_params=pltpu.CompilerParams(vmem_limit_bytes=PACK_MIB * MIB),
+        compiler_params=pltpu.CompilerParams(vmem_limit_bytes=8 * MIB),
         name=f"pack{chunk}",
     )(*operands)
     return outs[:groups], outs[groups:]
@@ -229,14 +231,14 @@
     total = parts[0][...]
     for part in parts[1:]:
         total = total + part[...]
-    out[...] = total
-
-
-def add_parts(parts, after):
+    out[...] = jnp.broadcast_to(total[None], out.shape)
+
+
+def add_parts(parts, after, copies):
     vmem_spec = pl.BlockSpec(memory_space=pltpu.VMEM)
     return pl.pallas_call(
         functools.partial(add_parts_kernel, len(parts)),
-        out_shape=jax.ShapeDtypeStruct(parts[0].shape, jnp.float32),
+        out_shape=jax.ShapeDtypeStruct((copies, *parts[0].shape), jnp.float32),
         in_specs=[vmem_spec] * len(parts) + [pl.BlockSpec(memory_space=pl.ANY)] * len(after),
         out_specs=vmem_spec,
         compiler_params=pltpu.CompilerParams(vmem_limit_bytes=4 * MIB),
@@ -273,10 +275,10 @@
             [results[0]]
             + [permute(results[shift], "seq", groups, shift) for shift in range(1, groups)]
         )
-    gain_total = add_parts(gain_parts, [returned[0][1], returned[0][2]])
-    for axis, size in (("dp", batches), ("seq", groups)):
-        for step in range(size.bit_length() - 1):
-            gain_total = gain_total + permute(gain_total, axis, size, 1 << step)
+    copies = add_parts(gain_parts, [returned[0][1], returned[0][2]], batches * groups)
+    gain_total = lax.all_to_all(
+        copies, ("dp", "seq"), split_axis=0, concat_axis=0, tiled=True
+    ).sum(0)
     outputs = None
     for chunk in range(chunks):
         outputs = unpack(returned[chunk], outputs, queries.shape, local, chunk, chunk_width)

time: 58.1 us -> 55.7 us (0.959)
  starting transfers between devices: 25.7 us -> 23.5 us
  waiting for transfers between devices: 16 us -> 17.9 us
  Pallas kernels: 14.1 us -> 12.7 us
  local copies, waits for them, and re-layouts: 1.19 us -> 0.52 us
    ppermute x17 -> x12, starting transfers between devices: 25.7 us -> 18.2 us  [permute(): return lax.ppermute(value, axis, [(i, i ^ shift) for i in range(size)])]
    all_to_all x0 -> x1, starting transfers between devices: none -> 5.33 us  [per_device(): lax.all_to_all(copies, ('dp', 'seq'), split_axis=0, concat_axis=0, tiled=...]
    pallas_call x2, Pallas kernels: 4.87 us -> 2.85 us  [pack(): pl.pallas_call(functools.partial(pack_kernel, groups, local, chunk, width...]
    ppermute x17 -> x12, waiting for transfers between devices: 16 us -> 17.9 us  [permute(): return lax.ppermute(value, axis, [(i, i ^ shift) for i in range(size)])]
    unnamed x8 -> x0, local copies, waits for them, and re-layouts: 0.67 us -> none
    pallas_call x1, Pallas kernels: 0.01 us -> 0.63 us  [add_parts(): pl.pallas_call(functools.partial(add_parts_kernel, len(parts)), out_shape...]
  transfers between devices with their start and end apart: 17 -> 13, of which waited for: 7 -> 6; matrix products, arithmetic and copies ran while one was open for 0% -> 0% of each run, Pallas kernels for 20% -> 20%
where the time goes in v4:
time: 55.7 us; the launch traced here: 55.4 us
  starting transfers between devices  23.5 us (42%)
  waiting for transfers between devices  17.9 us (32%)
  Pallas kernels  12.7 us (23%)
  between operations  0.71 us (1%)
    ppermute x12, starting transfers between devices, permute(): return lax.ppermute(value, axis, [(i, i ^ shift) for i in range(size)])  18.2 us
    ppermute x12, waiting for transfers between devices, permute(): return lax.ppermute(value, axis, [(i, i ^ shift) for i in range(size)])  17.9 us
    pallas_call x2, Pallas kernels, attend(): pl.pallas_call(functools.partial(attend_kernel, groups, rows, heads, bloc...  7.02 us
    all_to_all x1, starting transfers between devices, per_device(): lax.all_to_all(copies, ('dp', 'seq'), split_axis=0, concat_axis=0, tiled=...  5.33 us
    pallas_call x2, Pallas kernels, pack(): pl.pallas_call(functools.partial(pack_kernel, groups, local, chunk, width...  2.85 us
    pallas_call x2, Pallas kernels, unpack(): pl.pallas_call(functools.partial(unpack_kernel, groups, local, chunk, wid...  2.17 us
  transfers between devices with their start and end apart: 13, of which 6 were waited for; matrix products, arithmetic and copies ran while one was open for 0% of the time, Pallas kernels for 20%

profile of v4, /device:TPU:0, one launch (start us, length us, event | category | flops | bytes accessed | tf_op | source)
XLA Modules:
  0.0 55.4 jit_solution(5255616592039137312)
XLA Ops:
  0.6 1.5 %pack0.1 = (bf16[528,256]{1,0:T(8,128)(2,1)S(1)}, bf16[528,256]{1,0:T(8,128)(2,1)S(1)}, bf16[528,256]{1,0:T(8,128)(2,1)S(1)}, bf16[528,256]{1,0:T(8,128)(2,1)S(1...) custom-call(bf16[1,128,2048]{2,1,0:T(8,128)(2,1)} %refs_0_.3, bf16[1,128,2048]{2,1,0:T(8,128)(2,1)} %refs_1_.3, ...), custom_call_target="tpu_custom_call" | custom-call | tf_op jit(solution)/shard_map/pack0/pallas_call | solution.py:86
  2.1 3.0 %collective-permute-start.3 = (bf16[528,256]{1,0:T(8,128)(2,1)S(1)}, bf16[528,256]{1,0:T(8,128)(2,1)S(1)}, u32[]{:S(2)}, u32[]{:S(2)}) collective-permute-start(bf16[528,256]{1,0:T(8,128)(2,1)S(1)} %get-tuple-element.39), channel_id=1, source_target_pairs={{0,8},{8,0},{16,24},{24,16},{1,9},{9,1},{17,25},{25,17},{2,10},{10... | collective-permute-start | bytes 811016 | tf_op jit(solution)/shard_map/ppermute | solution.py:226
  5.1 1.5 %collective-permute-start.4 = (bf16[528,256]{1,0:T(8,128)(2,1)S(1)}, bf16[528,256]{1,0:T(8,128)(2,1)S(1)}, u32[]{:S(2)}, u32[]{:S(2)}) collective-permute-start(bf16[528,256]{1,0:T(8,128)(2,1)S(1)} %get-tuple-element.40), channel_id=1, source_target_pairs={{0,16},{8,24},{16,0},{24,8},{1,17},{9,25},{17,1},{25,9},{2,18},{10... | collective-permute-start | bytes 811016 | tf_op jit(solution)/shard_map/ppermute | solution.py:226
  6.6 0.0 collective-permute-start.5
  6.6 1.4 %pack1.1 = (bf16[512,256]{1,0:T(8,128)(2,1)S(1)}, bf16[512,256]{1,0:T(8,128)(2,1)S(1)}, bf16[512,256]{1,0:T(8,128)(2,1)S(1)}, bf16[512,256]{1,0:T(8,128)(2,1)S(1)}) custom-call(bf16[1,128,2048]{2,1,0:T(8,128)(2,1)} %refs_0_.3, bf16[1,128,2048]{2,1,0:T(8,128)(2,1)} %refs_1_.3, bf16[1,128,2048]{2,1,0:T(8,128)(2,1)} %refs_2_.3, bf16[1,128,2048]{2,1,0:T(8,128)(2,1)} %refs_3_.3), custom_call_target="tpu_custom_call" | custom-call | tf_op jit(solution)/shard_map/pack1/pallas_call | solution.py:86
  8.0 2.0 %collective-permute-start = (bf16[512,256]{1,0:T(8,128)(2,1)S(1)}, bf16[512,256]{1,0:T(8,128)(2,1)S(1)}, u32[]{:S(2)}, u32[]{:S(2)}) collective-permute-start(bf16[512,256]{1,0:T(8,128)(2,1)S(1)} %get-tuple-element.35), channel_id=1, source_target_pairs={{0,8},{8,0},{16,24},{24,16},{1,9},{9,1},{17,25},{25,17},{2,10},{10... | collective-permute-start | bytes 786440 | tf_op jit(solution)/shard_map/ppermute | solution.py:226
  10.1 1.5 %collective-permute-start.1 = (bf16[512,256]{1,0:T(8,128)(2,1)S(1)}, bf16[512,256]{1,0:T(8,128)(2,1)S(1)}, u32[]{:S(2)}, u32[]{:S(2)}) collective-permute-start(bf16[512,256]{1,0:T(8,128)(2,1)S(1)} %get-tuple-element.36), channel_id=1, source_target_pairs={{0,16},{8,24},{16,0},{24,8},{1,17},{9,25},{17,1},{25,9},{2,18},{10... | collective-permute-start | bytes 786440 | tf_op jit(solution)/shard_map/ppermute | solution.py:226
  11.6 0.8 %collective-permute-done.3.refs_5_.refs_1_ = bf16[528,256]{1,0:T(8,128)(2,1)S(1)} collective-permute-done((bf16[528,256]{1,0:T(8,128)(2,1)S(1)}, bf16[528,256]{1,0:T(8,128)(2,1)S(1)}, u32[]{:S(2)}, u32[]{:S(2)}) %collective-permute-start.3) | collective-permute-done | bytes 270368 | tf_op jit(solution)/shard_map/ppermute | solution.py:226
  12.4 3.0 %collective-permute-start.2 = (bf16[512,256]{1,0:T(8,128)(2,1)S(1)}, bf16[512,256]{1,0:T(8,128)(2,1)S(1)}, u32[]{:S(2)}, u32[]{:S(2)}) collective-permute-start(bf16[512,256]{1,0:T(8,128)(2,1)S(1)} %get-tuple-element.37), channel_id=1, source_target_pairs={{0,24},{8,16},{16,8},{24,0},{1,25},{9,17},{17,9},{25,1},{2,26},{10... | collective-permute-start | bytes 786440 | tf_op jit(solution)/shard_map/ppermute | solution.py:226
  15.4 4.9 %collective-permute-done.4.refs_6_.refs_2_ = bf16[528,256]{1,0:T(8,128)(2,1)S(1)} collective-permute-done((bf16[528,256]{1,0:T(8,128)(2,1)S(1)}, bf16[528,256]{1,0:T(8,128)(2,1)S(1)}, u32[]{:S(2)}, u32[]{:S(2)}) %collective-permute-start.4) | collective-permute-done | bytes 270368 | tf_op jit(solution)/shard_map/ppermute | solution.py:226
  20.3 0.0 collective-permute-done.5.refs_7_.refs_3_
  20.3 3.5 %attend0.1 = (bf16[512,256]{1,0:T(8,128)(2,1)S(1)}, bf16[512,256]{1,0:T(8,128)(2,1)S(1)}, bf16[512,256]{1,0:T(8,128)(2,1)S(1)}, bf16[512,256]{1,0:T(8,128)(2,1)S(1)}, f32[2,128]{1,0:T(2,128)S(1)}) custom-call(bf16[528,256]{1,0:T(8,128)(2,1)S(1)} %get-tuple-element.38.refs_4_.refs_0_, bf16[528,256]{1,0:T(8,128)(2,1)S(1)} %collective-permute-done.3.refs_5_.refs_1_, ...), custom_call_target="tpu_custom_call" | custom-call | flops 805306368 | bytes 2097152 | tf_op jit(solution)/shard_map/attend0/pallas_call | solution.py:207
  23.8 1.0 %collective-permute-start.9 = (bf16[512,256]{1,0:T(8,128)(2,1)S(1)}, bf16[512,256]{1,0:T(8,128)(2,1)S(1)}, u32[]{:S(2)}, u32[]{:S(2)}) collective-permute-start(bf16[512,256]{1,0:T(8,128)(2,1)S(1)} %get-tuple-element.49), channel_id=1, source_target_pairs={{0,8},{8,0},{16,24},{24,16},{1,9},{9,1},{17,25},{25,17},{2,10},{10... | collective-permute-start | bytes 786440 | tf_op jit(solution)/shard_map/ppermute | solution.py:226
  24.9 1.1 %collective-permute-start.10 = (bf16[512,256]{1,0:T(8,128)(2,1)S(1)}, bf16[512,256]{1,0:T(8,128)(2,1)S(1)}, u32[]{:S(2)}, u32[]{:S(2)}) collective-permute-start(bf16[512,256]{1,0:T(8,128)(2,1)S(1)} %get-tuple-element.50), channel_id=1, source_target_pairs={{0,16},{8,24},{16,0},{24,8},{1,17},{9,25},{17,1},{25,9},{2,18},{10... | collective-permute-start | bytes 786440 | tf_op jit(solution)/shard_map/ppermute | solution.py:226
  25.9 0.0 collective-permute-done.refs_1_
  26.0 4.5 %collective-permute-done.1.refs_2_ = bf16[512,256]{1,0:T(8,128)(2,1)S(1)} collective-permute-done((bf16[512,256]{1,0:T(8,128)(2,1)S(1)}, bf16[512,256]{1,0:T(8,128)(2,1)S(1)}, u32[]{:S(2)}, u32[]{:S(2)}) %collective-permute-start.1) | collective-permute-done | bytes 262176 | tf_op jit(solution)/shard_map/ppermute | solution.py:226
  30.4 0.6 %collective-permute-done.2.refs_3_ = bf16[512,256]{1,0:T(8,128)(2,1)S(1)} collective-permute-done((bf16[512,256]{1,0:T(8,128)(2,1)S(1)}, bf16[512,256]{1,0:T(8,128)(2,1)S(1)}, u32[]{:S(2)}, u32[]{:S(2)}) %collective-permute-start.2) | collective-permute-done | bytes 262176 | tf_op jit(solution)/shard_map/ppermute | solution.py:226
  31.1 3.5 %attend1.1 = (bf16[512,256]{1,0:T(8,128)(2,1)S(1)}, bf16[512,256]{1,0:T(8,128)(2,1)S(1)}, bf16[512,256]{1,0:T(8,128)(2,1)S(1)}, bf16[512,256]{1,0:T(8,128)(2,1)S(1)}, f32[2,128]{1,0:T(2,128)S(1)}) custom-call(bf16[512,256]{1,0:T(8,128)(2,1)S(1)} %get-tuple-element.34.refs_0_, bf16[512,256]{1,0:T(8,128)(2,1)S(1)} %collective-permute-done.refs_1_, ...), custom_call_target="tpu_custom_call" | custom-call | flops 805306368 | bytes 2097152 | tf_op jit(solution)/shard_map/attend1/pallas_call | solution.py:207
  34.6 1.6 %collective-permute-start.6 = (bf16[512,256]{1,0:T(8,128)(2,1)S(1)}, bf16[512,256]{1,0:T(8,128)(2,1)S(1)}, u32[]{:S(2)}, u32[]{:S(2)}) collective-permute-start(bf16[512,256]{1,0:T(8,128)(2,1)S(1)} %get-tuple-element.45), channel_id=1, source_target_pairs={{0,8},{8,0},{16,24},{24,16},{1,9},{9,1},{17,25},{25,17},{2,10},{10... | collective-permute-start | bytes 786440 | tf_op jit(solution)/shard_map/ppermute | solution.py:226
  36.1 1.8 %collective-permute-start.11 = (bf16[512,256]{1,0:T(8,128)(2,1)S(1)}, bf16[512,256]{1,0:T(8,128)(2,1)S(1)}, u32[]{:S(2)}, u32[]{:S(2)}) collective-permute-start(bf16[512,256]{1,0:T(8,128)(2,1)S(1)} %get-tuple-element.51), channel_id=1, source_target_pairs={{0,24},{8,16},{16,8},{24,0},{1,25},{9,17},{17,9},{25,1},{2,26},{10... | collective-permute-start | bytes 786440 | tf_op jit(solution)/shard_map/ppermute | solution.py:226
  37.9 0.2 collective-permute-start.7
  38.1 0.0 collective-permute-done.9.refs_1_.refs_2_
  38.1 1.4 %collective-permute-start.8 = (bf16[512,256]{1,0:T(8,128)(2,1)S(1)}, bf16[512,256]{1,0:T(8,128)(2,1)S(1)}, u32[]{:S(2)}, u32[]{:S(2)}) collective-permute-start(bf16[512,256]{1,0:T(8,128)(2,1)S(1)} %get-tuple-element.47), channel_id=1, source_target_pairs={{0,24},{8,16},{16,8},{24,0},{1,25},{9,17},{17,9},{25,1},{2,26},{10... | collective-permute-start | bytes 786440 | tf_op jit(solution)/shard_map/ppermute | solution.py:226
  39.6 0.0 collective-permute-done.10.refs_2_.refs_3_
  39.6 0.6 %add_parts.1 = f32[32,2,128]{2,1,0:T(2,128)} custom-call(f32[2,128]{1,0:T(2,128)S(1)} %get-tuple-element.60.refs_0_, f32[2,128]{1,0:T(2,128)S(1)} %get-tuple-element.61.refs_1_, bf16[512,256]{1,0:T(8,128)(2,1)S(1)} %collective-permute-done.9.refs_1_.refs_2_, bf16[512,256]{1,0:T(8,128)(2,1)S(1)} %collective-permute-done.10.refs_2_.refs_3_), custom_call_target="tpu_custom_call" | custom-call | tf_op jit(solution)/shard_map/add_parts/pallas_call | solution.py:239
  40.2 5.3 %all-to-all-start = ((f32[32,2,128]{2,1,0:T(2,128)}), f32[32,2,128]{2,1,0:T(2,128)S(1)}, u32[]{:S(2)}, u32[]{:S(2)}) async-start(f32[32,2,128]{2,1,0:T(2,128)} %add_parts.1), calls=%async_computation | async-start | bytes 65536 | tf_op jit(solution)/shard_map/all_to_all | solution.py:279
  45.5 4.2 %collective-permute-done.11.refs_3_ = bf16[512,256]{1,0:T(8,128)(2,1)S(1)} collective-permute-done((bf16[512,256]{1,0:T(8,128)(2,1)S(1)}, bf16[512,256]{1,0:T(8,128)(2,1)S(1)}, u32[]{:S(2)}, u32[]{:S(2)}) %collective-permute-start.11) | collective-permute-done | bytes 262176 | tf_op jit(solution)/shard_map/ppermute | solution.py:226
  49.7 1.1 %unpack0.1 = (bf16[1,128,2048]{2,1,0:T(8,128)(2,1)}, bf16[1,128,2048]{2,1,0:T(8,128)(2,1)}, bf16[1,128,2048]{2,1,0:T(8,128)(2,1)}, bf16[1,128,2048]{2,1,0:T(8,128)(2,1)}) custom-call(bf16[512,256]{1,0:T(8,128)(2,1)S(1)} %get-tuple-element.48.refs_0_, bf16[512,256]{1,0:T(8,128)(2,1)S(1)} %collective-permute-done.9.refs_1_.refs_2_, ...), custom_call_target="tpu_custom_call" | custom-call | tf_op jit(solution)/shard_map/unpack0/pallas_call | solution.py:130
  50.8 0.0 collective-permute-done.6.refs_1_
  50.8 2.9 %collective-permute-done.7.refs_2_ = bf16[512,256]{1,0:T(8,128)(2,1)S(1)} collective-permute-done((bf16[512,256]{1,0:T(8,128)(2,1)S(1)}, bf16[512,256]{1,0:T(8,128)(2,1)S(1)}, u32[]{:S(2)}, u32[]{:S(2)}) %collective-permute-start.7) | collective-permute-done | bytes 262176 | tf_op jit(solution)/shard_map/ppermute | solution.py:226
  53.7 1.1 %unpack1.1 = (bf16[1,128,2048]{2,1,0:T(8,128)(2,1)}, bf16[1,128,2048]{2,1,0:T(8,128)(2,1)}, bf16[1,128,2048]{2,1,0:T(8,128)(2,1)}, bf16[1,128,2048]{2,1,0:T(8,128)(2,1)}) custom-call(bf16[512,256]{1,0:T(8,128)(2,1)S(1)} %get-tuple-element.44.refs_0_, ...), custom_call_target="tpu_custom_call", output_to_operand_aliasing={{0}: (4, {}), {1}: (5, {}), {2}: (6, {}), {3}: (7, {})} | custom-call | tf_op jit(solution)/shard_map/unpack1/pallas_call | solution.py:130
  54.9 0.5 slice_bitcast_fusion
  (3 shorter events, 0.0 us)
Async XLA Ops:
  2.1 10.3 %collective-permute-start.3 = (bf16[528,256]{1,0:T(8,128)(2,1)S(1)}, bf16[528,256]{1,0:T(8,128)(2,1)S(1)}, u32[]{:S(2)}, u32[]{:S(2)}) collective-permute-start(bf16[528,256]{1,0:T(8,128)(2,1)S(1)} %get-tuple-element.39), channel_id=1, source_target_pairs={{0,8},{8,0},{16,24},{24,16},{1,9},{9,1},{17,25},{25,17},{2,10},{10... | collective-permute-start | bytes 811016 | tf_op jit(solution)/shard_map/ppermute | solution.py:226
  5.1 15.2 %collective-permute-start.4 = (bf16[528,256]{1,0:T(8,128)(2,1)S(1)}, bf16[528,256]{1,0:T(8,128)(2,1)S(1)}, u32[]{:S(2)}, u32[]{:S(2)}) collective-permute-start(bf16[528,256]{1,0:T(8,128)(2,1)S(1)} %get-tuple-element.40), channel_id=1, source_target_pairs={{0,16},{8,24},{16,0},{24,8},{1,17},{9,25},{17,1},{25,9},{2,18},{10... | collective-permute-start | bytes 811016 | tf_op jit(solution)/shard_map/ppermute | solution.py:226
  6.6 13.7 %collective-permute-start.5 = (bf16[528,256]{1,0:T(8,128)(2,1)S(1)}, bf16[528,256]{1,0:T(8,128)(2,1)S(1)}, u32[]{:S(2)}, u32[]{:S(2)}) collective-permute-start(bf16[528,256]{1,0:T(8,128)(2,1)S(1)} %get-tuple-element.41), channel_id=1, source_target_pairs={{0,24},{8,16},{16,8},{24,0},{1,25},{9,17},{17,9},{25,1},{2,26},{10... | collective-permute-start | bytes 811016 | tf_op jit(solution)/shard_map/ppermute | solution.py:226
  8.0 17.9 %collective-permute-start = (bf16[512,256]{1,0:T(8,128)(2,1)S(1)}, bf16[512,256]{1,0:T(8,128)(2,1)S(1)}, u32[]{:S(2)}, u32[]{:S(2)}) collective-permute-start(bf16[512,256]{1,0:T(8,128)(2,1)S(1)} %get-tuple-element.35), channel_id=1, source_target_pairs={{0,8},{8,0},{16,24},{24,16},{1,9},{9,1},{17,25},{25,17},{2,10},{10... | collective-permute-start | bytes 786440 | tf_op jit(solution)/shard_map/ppermute | solution.py:226
  10.1 20.4 %collective-permute-start.1 = (bf16[512,256]{1,0:T(8,128)(2,1)S(1)}, bf16[512,256]{1,0:T(8,128)(2,1)S(1)}, u32[]{:S(2)}, u32[]{:S(2)}) collective-permute-start(bf16[512,256]{1,0:T(8,128)(2,1)S(1)} %get-tuple-element.36), channel_id=1, source_target_pairs={{0,16},{8,24},{16,0},{24,8},{1,17},{9,25},{17,1},{25,9},{2,18},{10... | collective-permute-start | bytes 786440 | tf_op jit(solution)/shard_map/ppermute | solution.py:226
  12.4 18.6 %collective-permute-start.2 = (bf16[512,256]{1,0:T(8,128)(2,1)S(1)}, bf16[512,256]{1,0:T(8,128)(2,1)S(1)}, u32[]{:S(2)}, u32[]{:S(2)}) collective-permute-start(bf16[512,256]{1,0:T(8,128)(2,1)S(1)} %get-tuple-element.37), channel_id=1, source_target_pairs={{0,24},{8,16},{16,8},{24,0},{1,25},{9,17},{17,9},{25,1},{2,26},{10... | collective-permute-start | bytes 786440 | tf_op jit(solution)/shard_map/ppermute | solution.py:226
  23.8 14.3 %collective-permute-start.9 = (bf16[512,256]{1,0:T(8,128)(2,1)S(1)}, bf16[512,256]{1,0:T(8,128)(2,1)S(1)}, u32[]{:S(2)}, u32[]{:S(2)}) collective-permute-start(bf16[512,256]{1,0:T(8,128)(2,1)S(1)} %get-tuple-element.49), channel_id=1, source_target_pairs={{0,8},{8,0},{16,24},{24,16},{1,9},{9,1},{17,25},{25,17},{2,10},{10... | collective-permute-start | bytes 786440 | tf_op jit(solution)/shard_map/ppermute | solution.py:226
  24.9 14.7 %collective-permute-start.10 = (bf16[512,256]{1,0:T(8,128)(2,1)S(1)}, bf16[512,256]{1,0:T(8,128)(2,1)S(1)}, u32[]{:S(2)}, u32[]{:S(2)}) collective-permute-start(bf16[512,256]{1,0:T(8,128)(2,1)S(1)} %get-tuple-element.50), channel_id=1, source_target_pairs={{0,16},{8,24},{16,0},{24,8},{1,17},{9,25},{17,1},{25,9},{2,18},{10... | collective-permute-start | bytes 786440 | tf_op jit(solution)/shard_map/ppermute | solution.py:226
  34.6 16.2 %collective-permute-start.6 = (bf16[512,256]{1,0:T(8,128)(2,1)S(1)}, bf16[512,256]{1,0:T(8,128)(2,1)S(1)}, u32[]{:S(2)}, u32[]{:S(2)}) collective-permute-start(bf16[512,256]{1,0:T(8,128)(2,1)S(1)} %get-tuple-element.45), channel_id=1, source_target_pairs={{0,8},{8,0},{16,24},{24,16},{1,9},{9,1},{17,25},{25,17},{2,10},{10... | collective-permute-start | bytes 786440 | tf_op jit(solution)/shard_map/ppermute | solution.py:226
  36.1 13.6 %collective-permute-start.11 = (bf16[512,256]{1,0:T(8,128)(2,1)S(1)}, bf16[512,256]{1,0:T(8,128)(2,1)S(1)}, u32[]{:S(2)}, u32[]{:S(2)}) collective-permute-start(bf16[512,256]{1,0:T(8,128)(2,1)S(1)} %get-tuple-element.51), channel_id=1, source_target_pairs={{0,24},{8,16},{16,8},{24,0},{1,25},{9,17},{17,9},{25,1},{2,26},{10... | collective-permute-start | bytes 786440 | tf_op jit(solution)/shard_map/ppermute | solution.py:226
  37.9 15.8 %collective-permute-start.7 = (bf16[512,256]{1,0:T(8,128)(2,1)S(1)}, bf16[512,256]{1,0:T(8,128)(2,1)S(1)}, u32[]{:S(2)}, u32[]{:S(2)}) collective-permute-start(bf16[512,256]{1,0:T(8,128)(2,1)S(1)} %get-tuple-element.46), channel_id=1, source_target_pairs={{0,16},{8,24},{16,0},{24,8},{1,17},{9,25},{17,1},{25,9},{2,18},{10... | collective-permute-start | bytes 786440 | tf_op jit(solution)/shard_map/ppermute | solution.py:226
  38.1 15.6 %collective-permute-start.8 = (bf16[512,256]{1,0:T(8,128)(2,1)S(1)}, bf16[512,256]{1,0:T(8,128)(2,1)S(1)}, u32[]{:S(2)}, u32[]{:S(2)}) collective-permute-start(bf16[512,256]{1,0:T(8,128)(2,1)S(1)} %get-tuple-element.47), channel_id=1, source_target_pairs={{0,24},{8,16},{16,8},{24,0},{1,25},{9,17},{17,9},{25,1},{2,26},{10... | collective-permute-start | bytes 786440 | tf_op jit(solution)/shard_map/ppermute | solution.py:226
  40.2 14.6 %all-to-all-start = ((f32[32,2,128]{2,1,0:T(2,128)}), f32[32,2,128]{2,1,0:T(2,128)S(1)}, u32[]{:S(2)}, u32[]{:S(2)}) async-start(f32[32,2,128]{2,1,0:T(2,128)} %add_parts.1), calls=%async_computation | async-start | bytes 65536 | tf_op jit(solution)/shard_map/all_to_all | solution.py:279

commit v5 on v4

v5 whole, which is shorter than its diff:
```python
import functools

import jax
import jax.numpy as jnp
from jax import lax
from jax.experimental import pallas as pl
from jax.experimental.pallas import tpu as pltpu
from jax.sharding import PartitionSpec as P

HEAD_DIM = 128
EPS = 1e-06
TENSORS = 4
ID_ROWS = 16
LOG2_E = 1.4426950408889634
SCALE = HEAD_DIM ** (-0.5)
MIB = 1024 * 1024


def dot(a, b, contract):
    return lax.dot_general(
        a, b, ((contract[:1], contract[1:]), ((), ())), preferred_element_type=jnp.float32
    )


def normalize(rows, gain):
    floats = rows.astype(jnp.float32)
    inv_rms = lax.rsqrt(jnp.mean(floats * floats, axis=-1, keepdims=True) + EPS)
    normed = floats * inv_rms
    return normed, inv_rms, (normed * gain).astype(jnp.bfloat16)


def norm_back(grad_out, normed, inv_rms, gain):
    grad_normed = grad_out * gain
    inner_mean = jnp.mean(grad_normed * normed, axis=-1, keepdims=True)
    grad_rows = (inv_rms * (grad_normed - normed * inner_mean)).astype(jnp.bfloat16)
    return grad_rows, jnp.sum(grad_out * normed, axis=0, keepdims=True)


def pack_kernel(shifts, local, chunk, width, with_ids, gain_count, *refs):
    tensors, rest = refs[:TENSORS], refs[TENSORS:]
    if with_ids:
        ids_ref, rest = rest[0], rest[1:]
    gain_refs, rest = rest[:gain_count], rest[gain_count:]
    outs, rest = rest[: len(shifts)], rest[len(shifts) :]
    gain_outs, rest = rest[:gain_count], rest[gain_count:]
    sems = rest[0]
    rows = tensors[0].shape[1]
    pairs = [(ids_ref, rest[1])] if with_ids else []
    for out, shift in zip(outs, shifts):
        owner = jnp.bitwise_xor(lax.axis_index("seq"), shift)
        start = pl.multiple_of(owner * local + chunk * width, HEAD_DIM)
        for t in range(TENSORS):
            pairs.append((
                tensors[t].at[0, :, pl.ds(start, width)],
                out.at[pl.ds(t * rows, rows), :],
            ))
    pairs.extend(zip(gain_refs, gain_outs))
    started = [
        pltpu.make_async_copy(source, target, sems.at[i])
        for i, (source, target) in enumerate(pairs)
    ]
    for copy in started:
        copy.start()
    if with_ids:
        started[0].wait()
        ids = jnp.broadcast_to(rest[1][...].astype(jnp.float32), (ID_ROWS, rows))
        for out in outs:
            for column in range(0, width, rows):
                out[TENSORS * rows :, column : column + rows] = ids.astype(jnp.bfloat16)
    for copy in started[1 if with_ids else 0 :]:
        copy.wait()


def pack(arrays, slice_ids, gains, shifts, local, chunk, width, label):
    rows = arrays[0].shape[1]
    with_ids = slice_ids is not None
    height = TENSORS * rows + (ID_ROWS if with_ids else 0)
    vmem_spec = pl.BlockSpec(memory_space=pltpu.VMEM)
    operands = tuple(
        pltpu.with_memory_space_constraint(x, pltpu.HBM)
        for x in (*arrays, *([slice_ids] if with_ids else []), *gains)
    )
    count = TENSORS * len(shifts) + len(gains) + (1 if with_ids else 0)
    outs = pl.pallas_call(
        functools.partial(
            pack_kernel, tuple(shifts), local, chunk, width, with_ids, len(gains)
        ),
        out_shape=[jax.ShapeDtypeStruct((height, width), jnp.bfloat16)] * len(shifts)
        + [jax.ShapeDtypeStruct((1, HEAD_DIM), jnp.float32)] * len(gains),
        in_specs=[pl.BlockSpec(memory_space=pltpu.HBM)] * len(operands),
        out_specs=[vmem_spec] * (len(shifts) + len(gains)),
        scratch_shapes=[pltpu.SemaphoreType.DMA((count,))]
        + ([pltpu.VMEM((1, rows), jnp.int32)] if with_ids else []),
        compiler_params=pltpu.CompilerParams(vmem_limit_bytes=8 * MIB),
        name=label,
    )(*operands)
    return dict(zip(shifts, outs)), outs[len(shifts) :]


def unpack_kernel(places, count, local, width, aliased, with_gains, *refs):
    pieces, rest = refs[:count], refs[count:]
    if with_gains:
        gain_ref, rest = rest[0], rest[1:]
    if aliased:
        rest = rest[TENSORS:]
    outs, rest = rest[:TENSORS], rest[TENSORS:]
    if with_gains:
        gain_outs, totals, rest = rest[:2], rest[2], rest[3:]
    sems = rest[0]
    rows = outs[0].shape[1]
    started = []
    for operand, shift, chunk in places:
        owner = jnp.bitwise_xor(lax.axis_index("seq"), shift)
        start = pl.multiple_of(owner * local + chunk * width, HEAD_DIM)
        for t in range(TENSORS):
            started.append(
                pltpu.make_async_copy(
                    pieces[operand].at[pl.ds(t * rows, rows), :],
                    outs[t].at[0, :, pl.ds(start, width)],
                    sems.at[len(started)],
                )
            )
    for copy in started:
        copy.start()
    if with_gains:
        totals[...] = jnp.sum(gain_ref[...], axis=0)
        for i, out in enumerate(gain_outs):
            started.append(
                pltpu.make_async_copy(totals.at[i], out.at[0], sems.at[len(started)])
            )
            started[-1].start()
    for copy in started:
        copy.wait()


def unpack(entries, gain_sums, previous, shape, local, width, label):
    pieces = [piece for piece, _, _ in entries]
    places = [(i, shift, chunk) for i, (_, shift, chunk) in enumerate(entries)]
    count, aliased, with_gains = len(pieces), previous is not None, gain_sums is not None
    hbm_spec = pl.BlockSpec(memory_space=pltpu.HBM)
    vmem_spec = pl.BlockSpec(memory_space=pltpu.VMEM)
    read = (*pieces, *([gain_sums] if with_gains else []))
    operands = (*read, *(previous if aliased else ()))
    gain_outs = 2 if with_gains else 0
    return pl.pallas_call(
        functools.partial(unpack_kernel, places, count, local, width, aliased, with_gains),
        out_shape=[jax.ShapeDtypeStruct(shape, jnp.bfloat16)] * TENSORS
        + [jax.ShapeDtypeStruct((1, HEAD_DIM), jnp.float32)] * gain_outs,
        in_specs=[vmem_spec] * len(read) + [hbm_spec] * (len(operands) - len(read)),
        out_specs=[hbm_spec] * (TENSORS + gain_outs),
        scratch_shapes=[pltpu.VMEM((2, HEAD_DIM), jnp.float32)] * (1 if with_gains else 0)
        + [pltpu.SemaphoreType.DMA((count * TENSORS + gain_outs,))],
        input_output_aliases={len(read) + t: t for t in range(TENSORS)} if aliased else {},
        compiler_params=pltpu.CompilerParams(vmem_limit_bytes=8 * MIB),
        name=label,
    )(*operands)


def attend_kernel(groups, rows, heads, block, *refs):
    pieces, ids, rest = refs[:groups], refs[groups : 2 * groups], refs[2 * groups :]
    gain_refs, outs, gain_out = rest[:2], rest[2 : 2 + groups], rest[2 + groups]
    length = groups * rows
    query_gain, key_gain = gain_refs[0][...], gain_refs[1][...]
    ids_row = jnp.concatenate([ref[0:1, 0:rows].astype(jnp.float32) for ref in ids], axis=1)
    ids_col = jnp.broadcast_to(ids_row, (HEAD_DIM, length)).T
    lane = lax.broadcasted_iota(jnp.int32, (length, HEAD_DIM), 1)
    of_slice = jnp.where(lane == 0, ids_col, jnp.where(lane == 1, 1.0 - ids_col, 0.0))
    not_slice = jnp.where(lane == 0, 1.0 - ids_col, jnp.where(lane == 1, ids_col, 0.0))
    q_marks = (64.0 * of_slice).astype(jnp.bfloat16)
    k_marks = (-64.0 * not_slice).astype(jnp.bfloat16)
    gain_parts = [jnp.zeros((1, HEAD_DIM), jnp.float32)] * 2
    for head in range(heads):
        cols = slice(head * HEAD_DIM, (head + 1) * HEAD_DIM)

        def gather(t):
            return jnp.concatenate(
                [ref[t * rows : (t + 1) * rows, cols] for ref in pieces], axis=0
            )

        q_normed, q_inv, q_ready = normalize(gather(0), query_gain)
        k_normed, k_inv, k_ready = normalize(gather(1), key_gain)
        values, cotangent = gather(2), gather(3)
        k_marked = jnp.concatenate([k_ready, k_marks], axis=1)
        value_acc = key_acc = None
        attended_parts, query_parts = [], []
        for start in range(0, length, block):
            part = slice(start, start + block)
            q_block, grad_block = q_ready[part], cotangent[part]
            scores = dot(jnp.concatenate([q_block, q_marks[part]], axis=1), k_marked, (1, 1)) * (SCALE * LOG2_E)
            weights = jnp.exp2(scores)
            probs = weights * (1.0 / jnp.sum(weights, axis=1, keepdims=True))
            probs_low = probs.astype(jnp.bfloat16)
            attended = dot(probs_low, values, (1, 0)).astype(jnp.bfloat16)
            row_inner = jnp.sum(
                grad_block.astype(jnp.float32) * attended.astype(jnp.float32),
                axis=1,
                keepdims=True,
            )
            grad_probs = dot(grad_block, values, (1, 1))
            grad_scores = (probs * (grad_probs - row_inner)).astype(jnp.bfloat16)
            value_part = dot(grad_block, probs_low, (0, 0))
            key_part = dot(q_block, grad_scores, (0, 0))
            value_acc = value_part if value_acc is None else value_acc + value_part
            key_acc = key_part if key_acc is None else key_acc + key_part
            attended_parts.append(attended)
            query_parts.append(dot(grad_scores, k_ready, (1, 0)))
        value_acc, key_acc = value_acc.T, key_acc.T
        attended = jnp.concatenate(attended_parts, axis=0)
        query_acc = jnp.concatenate(query_parts, axis=0) * SCALE
        query_grad, query_sum = norm_back(query_acc, q_normed, q_inv, query_gain)
        key_grad, key_sum = norm_back(key_acc * SCALE, k_normed, k_inv, key_gain)
        gain_parts = [gain_parts[0] + query_sum, gain_parts[1] + key_sum]
        results = (attended, query_grad, key_grad, value_acc.astype(jnp.bfloat16))
        for i, out in enumerate(outs):
            for t in range(TENSORS):
                out[t * rows : (t + 1) * rows, cols] = results[t][i * rows : (i + 1) * rows]
    gain_out[0:1, :] = gain_parts[0]
    gain_out[1:2, :] = gain_parts[1]


def attend(pieces, id_holders, query_gain, key_gain, rows, heads, chunk):
    groups = len(pieces)
    width = heads * HEAD_DIM
    length = groups * rows
    height = TENSORS * rows
    block = min(length, 512 if length <= 512 else 256)
    piece_spec = pl.BlockSpec((height, width), lambda i: (0, 0))
    ids_spec = pl.BlockSpec((ID_ROWS, HEAD_DIM), lambda i: (height // ID_ROWS, 0))
    gain_spec = pl.BlockSpec((1, HEAD_DIM), lambda i: (0, 0))
    area = length * length * heads
    outs = pl.pallas_call(
        functools.partial(attend_kernel, groups, rows, heads, block),
        grid=(1,),
        out_shape=[jax.ShapeDtypeStruct((height, width), jnp.bfloat16)] * groups
        + [jax.ShapeDtypeStruct((2, HEAD_DIM), jnp.float32)],
        in_specs=[piece_spec] * groups + [ids_spec] * groups + [gain_spec] * 2,
        out_specs=[piece_spec] * groups + [pl.BlockSpec((2, HEAD_DIM), lambda i: (0, 0))],
        compiler_params=pltpu.CompilerParams(vmem_limit_bytes=(24 if length <= 512 else 48) * MIB),
        cost_estimate=pl.CostEstimate(
            flops=12 * area * HEAD_DIM,
            bytes_accessed=4 * groups * height * width,
            transcendentals=area,
        ),
        name=f"attend{chunk}",
    )(*pieces, *id_holders, query_gain, key_gain)
    return list(outs[:groups]), outs[groups]


def permute(value, axis, size, shift):
    return lax.ppermute(value, axis, [(i, i ^ shift) for i in range(size)])


def add_parts_kernel(*refs):
    *parts, out = refs
    total = parts[0][...]
    for part in parts[1:]:
        total = total + part[...]
    out[...] = jnp.broadcast_to(total[None], out.shape)


def add_parts(parts, copies):
    vmem_spec = pl.BlockSpec(memory_space=pltpu.VMEM)
    return pl.pallas_call(
        add_parts_kernel,
        out_shape=jax.ShapeDtypeStruct((copies, *parts[0].shape), jnp.float32),
        in_specs=[vmem_spec] * len(parts),
        out_specs=vmem_spec,
        compiler_params=pltpu.CompilerParams(vmem_limit_bytes=4 * MIB),
        name="add_parts",
    )(*parts)


def per_device(queries, key_rows, values, cotangent, slice_ids, query_gain, key_gain):
    rows, width = queries.shape[1], queries.shape[2]
    groups, batches = lax.axis_size("seq"), lax.axis_size("dp")
    local = width // groups
    chunks = 2 if local >= 2 * HEAD_DIM else 1
    chunk_width = local // chunks
    heads = chunk_width // HEAD_DIM
    arrays = (queries, key_rows, values, cotangent)
    gains = (query_gain.reshape(1, HEAD_DIM), key_gain.reshape(1, HEAD_DIM))

    peers = list(range(1, groups))
    every = list(range(chunks))
    received = []
    for chunk in every:
        if chunk == 0:
            payloads, _ = pack(
                arrays, slice_ids, (), peers[-1:], local, chunk, chunk_width, "pack_far"
            )
            rest, gains = pack(
                arrays, slice_ids, gains, peers[:-1] + [0], local, chunk, chunk_width, "pack"
            )
            payloads.update(rest)
        else:
            payloads, _ = pack(
                arrays, None, (), peers + [0], local, chunk, chunk_width, "pack_next"
            )
        received.append(
            [payloads[0]] + [permute(payloads[shift], "seq", groups, shift) for shift in peers]
        )
    returned, gain_parts = [], []
    for chunk in range(chunks):
        results, gain_part = attend(
            received[chunk], received[0], gains[0], gains[1], rows, heads, chunk
        )
        gain_parts.append(gain_part)
        returned.append(
            [results[0]] + [permute(results[shift], "seq", groups, shift) for shift in peers]
        )
    gain_sums = lax.all_to_all(
        add_parts(gain_parts, batches * groups),
        ("dp", "seq"),
        split_axis=0,
        concat_axis=0,
        tiled=True,
    )
    early = [(returned[chunk][0], 0, chunk) for chunk in every]
    early += [(returned[chunk][s], s, chunk) for chunk in every[:-1] for s in peers]
    late = [(returned[-1][s], s, chunks - 1) for s in peers]
    outputs = unpack(early, None, None, queries.shape, local, chunk_width, "unpack")
    *outputs, query_total, key_total = unpack(
        late, gain_sums, outputs, queries.shape, local, chunk_width, "unpack_last"
    )
    return (*outputs, query_total.reshape(HEAD_DIM), key_total.reshape(HEAD_DIM))


def solution(mesh):
    rows = P("dp", "seq", None)
    return jax.shard_map(
        per_device,
        mesh=mesh,
        in_specs=(rows, rows, rows, rows, P("dp", "seq"), P(), P()),
        out_specs=(rows, rows, rows, rows, P(), P()),
        check_vma=False,
    )
```

time: 55.7 us -> 53.7 us (0.964)
  waiting for transfers between devices: 17.9 us -> 16.3 us
  starting transfers between devices: 23.5 us -> 24.5 us
  Pallas kernels: 12.7 us -> 11.8 us
    ppermute x12, waiting for transfers between devices: 17.9 us -> 8.47 us  [permute(): return lax.ppermute(value, axis, [(i, i ^ shift) for i in range(size)])]
    all_to_all x1, waiting for transfers between devices: 0.01 us -> 7.82 us  [per_device(): lax.all_to_all(add_parts(gain_parts, batches * groups), ('dp', 'seq'), sp...]
    pallas_call x2, Pallas kernels: 7.02 us -> 5.29 us  [attend(): pl.pallas_call(functools.partial(attend_kernel, groups, rows, heads, bloc...]
    ppermute x12, starting transfers between devices: 18.2 us -> 19.5 us  [permute(): return lax.ppermute(value, axis, [(i, i ^ shift) for i in range(size)])]
    pallas_call x5 -> x6, Pallas kernels: 5.65 us -> 6.54 us  [the longest x3 3.69 us: pack(): pl.pallas_call(functools.partial(pack_kernel, tuple(shifts), local, chunk...]
  transfers between devices with their start and end apart: 13 -> 13, of which waited for: 6 -> 5; matrix products, arithmetic and copies ran while one was open for 0% -> 0% of each run, Pallas kernels for 20% -> 18%
where the time goes in v5:
time: 53.7 us; the launch traced here: 53.3 us
  starting transfers between devices  24.5 us (46%)
  waiting for transfers between devices  16.3 us (30%)
  Pallas kernels  11.8 us (22%)
  between operations  0.71 us (1%)
    ppermute x12, starting transfers between devices, permute(): return lax.ppermute(value, axis, [(i, i ^ shift) for i in range(size)])  19.5 us
    ppermute x12, waiting for transfers between devices, permute(): return lax.ppermute(value, axis, [(i, i ^ shift) for i in range(size)])  8.47 us
    all_to_all x1, waiting for transfers between devices, per_device(): lax.all_to_all(add_parts(gain_parts, batches * groups), ('dp', 'seq'), sp...  7.82 us
    pallas_call x2, Pallas kernels, attend(): pl.pallas_call(functools.partial(attend_kernel, groups, rows, heads, bloc...  5.29 us
    all_to_all x1, starting transfers between devices, per_device(): lax.all_to_all(add_parts(gain_parts, batches * groups), ('dp', 'seq'), sp...  4.97 us
    pallas_call x3, Pallas kernels, pack(): pl.pallas_call(functools.partial(pack_kernel, tuple(shifts), local, chunk...  3.69 us
    pallas_call x2, Pallas kernels, unpack(): pl.pallas_call(functools.partial(unpack_kernel, places, count, local, wid...  2.23 us
  transfers between devices with their start and end apart: 13, of which 5 were waited for; matrix products, arithmetic and copies ran while one was open for 0% of the time, Pallas kernels for 18%

profile of v5, /device:TPU:0, one launch (start us, length us, event | category | flops | bytes accessed | tf_op | source)
XLA Modules:
  0.0 53.3 jit_solution(11286428717885217592)
XLA Ops:
  0.6 1.0 %pack_far.1 = bf16[528,256]{1,0:T(8,128)(2,1)S(1)} custom-call(bf16[1,128,2048]{2,1,0:T(8,128)(2,1)} %refs_0_.5, bf16[1,128,2048]{2,1,0:T(8,128)(2,1)} %refs_1_.5, bf16[1,128,2048]{2,1,0:T(8,128)(2,1)} %refs_2_.5, bf16[1,128,2048]{2,1,0:T(8,128)(2,1)} %refs_3_.5, s32[1,128]{1,0:T(1,128)} %refs_4_.3), custom_call_target="tpu_custom_call" | custom-call | tf_op jit(solution)/shard_map/pack_far/pallas_call | solution.py:84
  1.6 4.0 %collective-permute-start.5 = (bf16[528,256]{1,0:T(8,128)(2,1)S(1)}, bf16[528,256]{1,0:T(8,128)(2,1)S(1)}, u32[]{:S(2)}, u32[]{:S(2)}) collective-permute-start(bf16[528,256]{1,0:T(8,128)(2,1)S(1)} %pack_far.1), channel_id=1, source_target_pairs={{0,24},{8,16},{16,8},{24,0},{1,25},{9,17},{17,9},{25,1},{2,26},{10... | collective-permute-start | bytes 811016 | tf_op jit(solution)/shard_map/ppermute | solution.py:250
  5.6 1.3 %pack.1 = (bf16[528,256]{1,0:T(8,128)(2,1)S(1)}, bf16[528,256]{1,0:T(8,128)(2,1)S(1)}, bf16[528,256]{1,0:T(8,128)(2,1)S(1)}, f32[1,128]{1,0:T(1,128)S(1)}, f32[1,128]{1,0:T(1,128)S(1)}) custom-call(bf16[1,128,2048]{2,1,0:T(8,128)(2,1)} %refs_0_.5, bf16[1,128,2048]{2,1,0:T(8,128)(2,1)} %refs_1_.5, bf16[1,128,2048]{2,1,0:T(8,128)(2,1)} %refs_2_.5, ...), custom_call_target="tpu_custom_call" | custom-call | tf_op jit(solution)/shard_map/pack/pallas_call | solution.py:84
  6.9 0.6 %collective-permute-start.3 = (bf16[528,256]{1,0:T(8,128)(2,1)S(1)}, bf16[528,256]{1,0:T(8,128)(2,1)S(1)}, u32[]{:S(2)}, u32[]{:S(2)}) collective-permute-start(bf16[528,256]{1,0:T(8,128)(2,1)S(1)} %get-tuple-element.40), channel_id=1, source_target_pairs={{0,8},{8,0},{16,24},{24,16},{1,9},{9,1},{17,25},{25,17},{2,10},{10... | collective-permute-start | bytes 811016 | tf_op jit(solution)/shard_map/ppermute | solution.py:250
  7.5 0.1 collective-permute-start.4
  7.6 1.4 %pack_next.1 = (bf16[512,256]{1,0:T(8,128)(2,1)S(1)}, bf16[512,256]{1,0:T(8,128)(2,1)S(1)}, bf16[512,256]{1,0:T(8,128)(2,1)S(1)}, bf16[512,256]{1,0:T(8,128)(2,1)S(1)}) custom-call(bf16[1,128,2048]{2,1,0:T(8,128)(2,1)} %refs_0_.5, bf16[1,128,2048]{2,1,0:T(8,128)(2,1)} %refs_1_.5, bf16[1,128,2048]{2,1,0:T(8,128)(2,1)} %refs_2_.5, bf16[1,128,2048]{2,1,0:T(8,128)(2,1)} %refs_3_.5), custom_call_target="tpu_custom_call" | custom-call | tf_op jit(solution)/shard_map/pack_next/pallas_call | solution.py:84
  9.0 2.0 %collective-permute-start = (bf16[512,256]{1,0:T(8,128)(2,1)S(1)}, bf16[512,256]{1,0:T(8,128)(2,1)S(1)}, u32[]{:S(2)}, u32[]{:S(2)}) collective-permute-start(bf16[512,256]{1,0:T(8,128)(2,1)S(1)} %get-tuple-element.36), channel_id=1, source_target_pairs={{0,8},{8,0},{16,24},{24,16},{1,9},{9,1},{17,25},{25,17},{2,10},{10... | collective-permute-start | bytes 786440 | tf_op jit(solution)/shard_map/ppermute | solution.py:250
  11.0 1.5 %collective-permute-start.1 = (bf16[512,256]{1,0:T(8,128)(2,1)S(1)}, bf16[512,256]{1,0:T(8,128)(2,1)S(1)}, u32[]{:S(2)}, u32[]{:S(2)}) collective-permute-start(bf16[512,256]{1,0:T(8,128)(2,1)S(1)} %get-tuple-element.37), channel_id=1, source_target_pairs={{0,16},{8,24},{16,0},{24,8},{1,17},{9,25},{17,1},{25,9},{2,18},{10... | collective-permute-start | bytes 786440 | tf_op jit(solution)/shard_map/ppermute | solution.py:250
  12.5 0.5 collective-permute-done.5.refs_7_.refs_3_
  13.0 3.0 %collective-permute-start.2 = (bf16[512,256]{1,0:T(8,128)(2,1)S(1)}, bf16[512,256]{1,0:T(8,128)(2,1)S(1)}, u32[]{:S(2)}, u32[]{:S(2)}) collective-permute-start(bf16[512,256]{1,0:T(8,128)(2,1)S(1)} %get-tuple-element.38), channel_id=1, source_target_pairs={{0,24},{8,16},{16,8},{24,0},{1,25},{9,17},{17,9},{25,1},{2,26},{10... | collective-permute-start | bytes 786440 | tf_op jit(solution)/shard_map/ppermute | solution.py:250
  15.9 3.4 %collective-permute-done.3.refs_5_.refs_1_ = bf16[528,256]{1,0:T(8,128)(2,1)S(1)} collective-permute-done((bf16[528,256]{1,0:T(8,128)(2,1)S(1)}, bf16[528,256]{1,0:T(8,128)(2,1)S(1)}, u32[]{:S(2)}, u32[]{:S(2)}) %collective-permute-start.3) | collective-permute-done | bytes 270368 | tf_op jit(solution)/shard_map/ppermute | solution.py:250
  19.3 0.0 collective-permute-done.4.refs_6_.refs_2_
  19.3 2.6 %attend0.1 = (bf16[512,256]{1,0:T(8,128)(2,1)S(1)}, bf16[512,256]{1,0:T(8,128)(2,1)S(1)}, bf16[512,256]{1,0:T(8,128)(2,1)S(1)}, bf16[512,256]{1,0:T(8,128)(2,1)S(1)}, f32[2,128]{1,0:T(2,128)S(1)}) custom-call(bf16[528,256]{1,0:T(8,128)(2,1)S(1)} %get-tuple-element.39.refs_4_.refs_0_, bf16[528,256]{1,0:T(8,128)(2,1)S(1)} %collective-permute-done.3.refs_5_.refs_1_, ...), custom_call_target="tpu_custom_call" | custom-call | flops 805306368 | bytes 2097152 | tf_op jit(solution)/shard_map/attend0/pallas_call | solution.py:231
  22.0 1.6 %collective-permute-start.9 = (bf16[512,256]{1,0:T(8,128)(2,1)S(1)}, bf16[512,256]{1,0:T(8,128)(2,1)S(1)}, u32[]{:S(2)}, u32[]{:S(2)}) collective-permute-start(bf16[512,256]{1,0:T(8,128)(2,1)S(1)} %get-tuple-element.51), channel_id=1, source_target_pairs={{0,8},{8,0},{16,24},{24,16},{1,9},{9,1},{17,25},{25,17},{2,10},{10... | collective-permute-start | bytes 786440 | tf_op jit(solution)/shard_map/ppermute | solution.py:250
  23.5 0.5 collective-permute-start.10
  24.0 0.9 %collective-permute-done.refs_1_ = bf16[512,256]{1,0:T(8,128)(2,1)S(1)} collective-permute-done((bf16[512,256]{1,0:T(8,128)(2,1)S(1)}, bf16[512,256]{1,0:T(8,128)(2,1)S(1)}, u32[]{:S(2)}, u32[]{:S(2)}) %collective-permute-start) | collective-permute-done | bytes 262176 | tf_op jit(solution)/shard_map/ppermute | solution.py:250
  24.9 1.4 %collective-permute-start.11 = (bf16[512,256]{1,0:T(8,128)(2,1)S(1)}, bf16[512,256]{1,0:T(8,128)(2,1)S(1)}, u32[]{:S(2)}, u32[]{:S(2)}) collective-permute-start(bf16[512,256]{1,0:T(8,128)(2,1)S(1)} %get-tuple-element.53), channel_id=1, source_target_pairs={{0,24},{8,16},{16,8},{24,0},{1,25},{9,17},{17,9},{25,1},{2,26},{10... | collective-permute-start | bytes 786440 | tf_op jit(solution)/shard_map/ppermute | solution.py:250
  26.3 0.0 collective-permute-done.1.refs_2_
  26.3 3.7 %collective-permute-done.2.refs_3_ = bf16[512,256]{1,0:T(8,128)(2,1)S(1)} collective-permute-done((bf16[512,256]{1,0:T(8,128)(2,1)S(1)}, bf16[512,256]{1,0:T(8,128)(2,1)S(1)}, u32[]{:S(2)}, u32[]{:S(2)}) %collective-permute-start.2) | collective-permute-done | bytes 262176 | tf_op jit(solution)/shard_map/ppermute | solution.py:250
  30.0 2.6 %attend1.1 = (bf16[512,256]{1,0:T(8,128)(2,1)S(1)}, bf16[512,256]{1,0:T(8,128)(2,1)S(1)}, bf16[512,256]{1,0:T(8,128)(2,1)S(1)}, bf16[512,256]{1,0:T(8,128)(2,1)S(1)}, f32[2,128]{1,0:T(2,128)S(1)}) custom-call(bf16[512,256]{1,0:T(8,128)(2,1)S(1)} %get-tuple-element.35.refs_0_, bf16[512,256]{1,0:T(8,128)(2,1)S(1)} %collective-permute-done.refs_1_, ...), custom_call_target="tpu_custom_call" | custom-call | flops 805306368 | bytes 2097152 | tf_op jit(solution)/shard_map/attend1/pallas_call | solution.py:231
  32.7 2.1 %collective-permute-start.6 = (bf16[512,256]{1,0:T(8,128)(2,1)S(1)}, bf16[512,256]{1,0:T(8,128)(2,1)S(1)}, u32[]{:S(2)}, u32[]{:S(2)}) collective-permute-start(bf16[512,256]{1,0:T(8,128)(2,1)S(1)} %get-tuple-element.44), channel_id=1, source_target_pairs={{0,8},{8,0},{16,24},{24,16},{1,9},{9,1},{17,25},{25,17},{2,10},{10... | collective-permute-start | bytes 786440 | tf_op jit(solution)/shard_map/ppermute | solution.py:250
  34.7 1.5 %collective-permute-start.7 = (bf16[512,256]{1,0:T(8,128)(2,1)S(1)}, bf16[512,256]{1,0:T(8,128)(2,1)S(1)}, u32[]{:S(2)}, u32[]{:S(2)}) collective-permute-start(bf16[512,256]{1,0:T(8,128)(2,1)S(1)} %get-tuple-element.45), channel_id=1, source_target_pairs={{0,16},{8,24},{16,0},{24,8},{1,17},{9,25},{17,1},{25,9},{2,18},{10... | collective-permute-start | bytes 786440 | tf_op jit(solution)/shard_map/ppermute | solution.py:250
  36.3 1.4 %collective-permute-start.8 = (bf16[512,256]{1,0:T(8,128)(2,1)S(1)}, bf16[512,256]{1,0:T(8,128)(2,1)S(1)}, u32[]{:S(2)}, u32[]{:S(2)}) collective-permute-start(bf16[512,256]{1,0:T(8,128)(2,1)S(1)} %get-tuple-element.46), channel_id=1, source_target_pairs={{0,24},{8,16},{16,8},{24,0},{1,25},{9,17},{17,9},{25,1},{2,26},{10... | collective-permute-start | bytes 786440 | tf_op jit(solution)/shard_map/ppermute | solution.py:250
  37.6 0.6 %add_parts.1 = f32[32,2,128]{2,1,0:T(2,128)} custom-call(f32[2,128]{1,0:T(2,128)S(1)} %get-tuple-element.47.refs_0_, f32[2,128]{1,0:T(2,128)S(1)} %get-tuple-element.48.refs_1_), custom_call_target="tpu_custom_call" | custom-call | tf_op jit(solution)/shard_map/add_parts/pallas_call | solution.py:263
  38.2 5.0 %all-to-all-start = ((f32[32,2,128]{2,1,0:T(2,128)}), f32[32,2,128]{2,1,0:T(2,128)S(1)}, u32[]{:S(2)}, u32[]{:S(2)}) async-start(f32[32,2,128]{2,1,0:T(2,128)} %add_parts.1), calls=%async_computation | async-start | bytes 65536 | tf_op jit(solution)/shard_map/all_to_all | solution.py:311
  43.2 0.0 collective-permute-done.10.refs_3_
  43.2 1.2 %unpack.1 = (bf16[1,128,2048]{2,1,0:T(8,128)(2,1)}, bf16[1,128,2048]{2,1,0:T(8,128)(2,1)}, bf16[1,128,2048]{2,1,0:T(8,128)(2,1)}, bf16[1,128,2048]{2,1,0:T(8,128)(2,1)}) custom-call(bf16[512,256]{1,0:T(8,128)(2,1)S(1)} %get-tuple-element.49.refs_0_, bf16[512,256]{1,0:T(8,128)(2,1)S(1)} %get-tuple-element.50.refs_1_, ...), custom_call_target="tpu_custom_call" | custom-call | tf_op jit(solution)/shard_map/unpack/pallas_call | solution.py:145
  44.5 7.8 %all-to-all-done.refs_3_ = f32[32,2,128]{2,1,0:T(2,128)S(1)} async-done(((f32[32,2,128]{2,1,0:T(2,128)}), f32[32,2,128]{2,1,0:T(2,128)S(1)}, u32[]{:S(2)}, u32[]{:S(2)}) %all-to-all-start) | async-done | bytes 32800 | tf_op jit(solution)/shard_map/all_to_all | solution.py:311
  52.3 0.0 collective-permute-done.6.refs_0_
  52.3 0.0 collective-permute-done.7.refs_1_
  52.3 0.0 collective-permute-done.8.refs_2_
  52.3 1.0 %unpack_last.1 = (bf16[1,128,2048]{2,1,0:T(8,128)(2,1)}, bf16[1,128,2048]{2,1,0:T(8,128)(2,1)}, bf16[1,128,2048]{2,1,0:T(8,128)(2,1)}, bf16[1,128,2048]{2,1,0:T(...) custom-call(bf16[512,256]{1,0:T(8,128)(2,1)S(1)} %collective-permute, ...), custom_call_target="tpu_custom_call", output_to_operand_aliasing={{0}: (4, {}), {1}: (5, {}), {2}: (6, {}), {3}: (7, {})} | custom-call | tf_op jit(solution)/shard_map/unpack_last/pallas_call | solution.py:145
  (2 shorter events, 0.0 us)
Async XLA Ops:
  1.6 11.3 %collective-permute-start.5 = (bf16[528,256]{1,0:T(8,128)(2,1)S(1)}, bf16[528,256]{1,0:T(8,128)(2,1)S(1)}, u32[]{:S(2)}, u32[]{:S(2)}) collective-permute-start(bf16[528,256]{1,0:T(8,128)(2,1)S(1)} %pack_far.1), channel_id=1, source_target_pairs={{0,24},{8,16},{16,8},{24,0},{1,25},{9,17},{17,9},{25,1},{2,26},{10... | collective-permute-start | bytes 811016 | tf_op jit(solution)/shard_map/ppermute | solution.py:250
  6.9 12.4 %collective-permute-start.3 = (bf16[528,256]{1,0:T(8,128)(2,1)S(1)}, bf16[528,256]{1,0:T(8,128)(2,1)S(1)}, u32[]{:S(2)}, u32[]{:S(2)}) collective-permute-start(bf16[528,256]{1,0:T(8,128)(2,1)S(1)} %get-tuple-element.40), channel_id=1, source_target_pairs={{0,8},{8,0},{16,24},{24,16},{1,9},{9,1},{17,25},{25,17},{2,10},{10... | collective-permute-start | bytes 811016 | tf_op jit(solution)/shard_map/ppermute | solution.py:250
  7.5 11.8 %collective-permute-start.4 = (bf16[528,256]{1,0:T(8,128)(2,1)S(1)}, bf16[528,256]{1,0:T(8,128)(2,1)S(1)}, u32[]{:S(2)}, u32[]{:S(2)}) collective-permute-start(bf16[528,256]{1,0:T(8,128)(2,1)S(1)} %get-tuple-element.41), channel_id=1, source_target_pairs={{0,16},{8,24},{16,0},{24,8},{1,17},{9,25},{17,1},{25,9},{2,18},{10... | collective-permute-start | bytes 811016 | tf_op jit(solution)/shard_map/ppermute | solution.py:250
  9.0 16.0 %collective-permute-start = (bf16[512,256]{1,0:T(8,128)(2,1)S(1)}, bf16[512,256]{1,0:T(8,128)(2,1)S(1)}, u32[]{:S(2)}, u32[]{:S(2)}) collective-permute-start(bf16[512,256]{1,0:T(8,128)(2,1)S(1)} %get-tuple-element.36), channel_id=1, source_target_pairs={{0,8},{8,0},{16,24},{24,16},{1,9},{9,1},{17,25},{25,17},{2,10},{10... | collective-permute-start | bytes 786440 | tf_op jit(solution)/shard_map/ppermute | solution.py:250
  11.0 15.4 %collective-permute-start.1 = (bf16[512,256]{1,0:T(8,128)(2,1)S(1)}, bf16[512,256]{1,0:T(8,128)(2,1)S(1)}, u32[]{:S(2)}, u32[]{:S(2)}) collective-permute-start(bf16[512,256]{1,0:T(8,128)(2,1)S(1)} %get-tuple-element.37), channel_id=1, source_target_pairs={{0,16},{8,24},{16,0},{24,8},{1,17},{9,25},{17,1},{25,9},{2,18},{10... | collective-permute-start | bytes 786440 | tf_op jit(solution)/shard_map/ppermute | solution.py:250
  13.0 17.1 %collective-permute-start.2 = (bf16[512,256]{1,0:T(8,128)(2,1)S(1)}, bf16[512,256]{1,0:T(8,128)(2,1)S(1)}, u32[]{:S(2)}, u32[]{:S(2)}) collective-permute-start(bf16[512,256]{1,0:T(8,128)(2,1)S(1)} %get-tuple-element.38), channel_id=1, source_target_pairs={{0,24},{8,16},{16,8},{24,0},{1,25},{9,17},{17,9},{25,1},{2,26},{10... | collective-permute-start | bytes 786440 | tf_op jit(solution)/shard_map/ppermute | solution.py:250
  22.0 14.3 %collective-permute-start.9 = (bf16[512,256]{1,0:T(8,128)(2,1)S(1)}, bf16[512,256]{1,0:T(8,128)(2,1)S(1)}, u32[]{:S(2)}, u32[]{:S(2)}) collective-permute-start(bf16[512,256]{1,0:T(8,128)(2,1)S(1)} %get-tuple-element.51), channel_id=1, source_target_pairs={{0,8},{8,0},{16,24},{24,16},{1,9},{9,1},{17,25},{25,17},{2,10},{10... | collective-permute-start | bytes 786440 | tf_op jit(solution)/shard_map/ppermute | solution.py:250
  23.5 19.7 %collective-permute-start.10 = (bf16[512,256]{1,0:T(8,128)(2,1)S(1)}, bf16[512,256]{1,0:T(8,128)(2,1)S(1)}, u32[]{:S(2)}, u32[]{:S(2)}) collective-permute-start(bf16[512,256]{1,0:T(8,128)(2,1)S(1)} %get-tuple-element.52), channel_id=1, source_target_pairs={{0,16},{8,24},{16,0},{24,8},{1,17},{9,25},{17,1},{25,9},{2,18},{10... | collective-permute-start | bytes 786440 | tf_op jit(solution)/shard_map/ppermute | solution.py:250
  24.9 18.3 %collective-permute-start.11 = (bf16[512,256]{1,0:T(8,128)(2,1)S(1)}, bf16[512,256]{1,0:T(8,128)(2,1)S(1)}, u32[]{:S(2)}, u32[]{:S(2)}) collective-permute-start(bf16[512,256]{1,0:T(8,128)(2,1)S(1)} %get-tuple-element.53), channel_id=1, source_target_pairs={{0,24},{8,16},{16,8},{24,0},{1,25},{9,17},{17,9},{25,1},{2,26},{10... | collective-permute-start | bytes 786440 | tf_op jit(solution)/shard_map/ppermute | solution.py:250
  32.7 19.6 %collective-permute-start.6 = (bf16[512,256]{1,0:T(8,128)(2,1)S(1)}, bf16[512,256]{1,0:T(8,128)(2,1)S(1)}, u32[]{:S(2)}, u32[]{:S(2)}) collective-permute-start(bf16[512,256]{1,0:T(8,128)(2,1)S(1)} %get-tuple-element.44), channel_id=1, source_target_pairs={{0,8},{8,0},{16,24},{24,16},{1,9},{9,1},{17,25},{25,17},{2,10},{10... | collective-permute-start | bytes 786440 | tf_op jit(solution)/shard_map/ppermute | solution.py:250
  34.7 17.6 %collective-permute-start.7 = (bf16[512,256]{1,0:T(8,128)(2,1)S(1)}, bf16[512,256]{1,0:T(8,128)(2,1)S(1)}, u32[]{:S(2)}, u32[]{:S(2)}) collective-permute-start(bf16[512,256]{1,0:T(8,128)(2,1)S(1)} %get-tuple-element.45), channel_id=1, source_target_pairs={{0,16},{8,24},{16,0},{24,8},{1,17},{9,25},{17,1},{25,9},{2,18},{10... | collective-permute-start | bytes 786440 | tf_op jit(solution)/shard_map/ppermute | solution.py:250
  36.3 16.0 %collective-permute-start.8 = (bf16[512,256]{1,0:T(8,128)(2,1)S(1)}, bf16[512,256]{1,0:T(8,128)(2,1)S(1)}, u32[]{:S(2)}, u32[]{:S(2)}) collective-permute-start(bf16[512,256]{1,0:T(8,128)(2,1)S(1)} %get-tuple-element.46), channel_id=1, source_target_pairs={{0,24},{8,16},{16,8},{24,0},{1,25},{9,17},{17,9},{25,1},{2,26},{10... | collective-permute-start | bytes 786440 | tf_op jit(solution)/shard_map/ppermute | solution.py:250
  38.2 14.0 %all-to-all-start = ((f32[32,2,128]{2,1,0:T(2,128)}), f32[32,2,128]{2,1,0:T(2,128)S(1)}, u32[]{:S(2)}, u32[]{:S(2)}) async-start(f32[32,2,128]{2,1,0:T(2,128)} %add_parts.1), calls=%async_computation | async-start | bytes 65536 | tf_op jit(solution)/shard_map/all_to_all | solution.py:311

commit v6 on v5

--- a/solution.py
+++ b/solution.py
@@ -197,7 +197,7 @@
                 keepdims=True,
             )
             grad_probs = dot(grad_block, values, (1, 1))
-            grad_scores = (probs * (grad_probs - row_inner)).astype(jnp.bfloat16)
+            grad_scores = (probs * (grad_probs - row_inner) * SCALE).astype(jnp.bfloat16)
             value_part = dot(grad_block, probs_low, (0, 0))
             key_part = dot(q_block, grad_scores, (0, 0))
             value_acc = value_part if value_acc is None else value_acc + value_part
@@ -206,9 +206,9 @@
             query_parts.append(dot(grad_scores, k_ready, (1, 0)))
         value_acc, key_acc = value_acc.T, key_acc.T
         attended = jnp.concatenate(attended_parts, axis=0)
-        query_acc = jnp.concatenate(query_parts, axis=0) * SCALE
+        query_acc = jnp.concatenate(query_parts, axis=0)
         query_grad, query_sum = norm_back(query_acc, q_normed, q_inv, query_gain)
-        key_grad, key_sum = norm_back(key_acc * SCALE, k_normed, k_inv, key_gain)
+        key_grad, key_sum = norm_back(key_acc, k_normed, k_inv, key_gain)
         gain_parts = [gain_parts[0] + query_sum, gain_parts[1] + key_sum]
         results = (attended, query_grad, key_grad, value_acc.astype(jnp.bfloat16))
         for i, out in enumerate(outs):

time: 53.7 us -> 53.7 us (level)
  transfers between devices with their start and end apart: 13 -> 13, of which waited for: 5 -> 5; matrix products, arithmetic and copies ran while one was open for 0% -> 0% of each run, Pallas kernels for 18% -> 19%
where the time goes in v6:
time: 53.7 us; the launch traced here: 53.3 us
  starting transfers between devices  24.5 us (46%)
  waiting for transfers between devices  16.2 us (30%)
  Pallas kernels  11.9 us (22%)
  between operations  0.71 us (1%)
    ppermute x12, starting transfers between devices, permute(): return lax.ppermute(value, axis, [(i, i ^ shift) for i in range(size)])  19.5 us
    ppermute x12, waiting for transfers between devices, permute(): return lax.ppermute(value, axis, [(i, i ^ shift) for i in range(size)])  8.43 us
    all_to_all x1, waiting for transfers between devices, per_device(): lax.all_to_all(add_parts(gain_parts, batches * groups), ('dp', 'seq'), sp...  7.79 us
    pallas_call x2, Pallas kernels, attend(): pl.pallas_call(functools.partial(attend_kernel, groups, rows, heads, bloc...  5.36 us
    all_to_all x1, starting transfers between devices, per_device(): lax.all_to_all(add_parts(gain_parts, batches * groups), ('dp', 'seq'), sp...  5 us
    pallas_call x3, Pallas kernels, pack(): pl.pallas_call(functools.partial(pack_kernel, tuple(shifts), local, chunk...  3.69 us
    pallas_call x2, Pallas kernels, unpack(): pl.pallas_call(functools.partial(unpack_kernel, places, count, local, wid...  2.23 us
  transfers between devices with their start and end apart: 13, of which 5 were waited for; matrix products, arithmetic and copies ran while one was open for 0% of the time, Pallas kernels for 19%

profile of v6, /device:TPU:0, one launch (start us, length us, event | category | flops | bytes accessed | tf_op | source)
XLA Modules:
  0.0 53.3 jit_solution(18336987143126187517)
XLA Ops:
  0.6 1.0 %pack_far.1 = bf16[528,256]{1,0:T(8,128)(2,1)S(1)} custom-call(bf16[1,128,2048]{2,1,0:T(8,128)(2,1)} %refs_0_.5, bf16[1,128,2048]{2,1,0:T(8,128)(2,1)} %refs_1_.5, bf16[1,128,2048]{2,1,0:T(8,128)(2,1)} %refs_2_.5, bf16[1,128,2048]{2,1,0:T(8,128)(2,1)} %refs_3_.5, s32[1,128]{1,0:T(1,128)} %refs_4_.3), custom_call_target="tpu_custom_call" | custom-call | tf_op jit(solution)/shard_map/pack_far/pallas_call | solution.py:84
  1.6 4.0 %collective-permute-start.5 = (bf16[528,256]{1,0:T(8,128)(2,1)S(1)}, bf16[528,256]{1,0:T(8,128)(2,1)S(1)}, u32[]{:S(2)}, u32[]{:S(2)}) collective-permute-start(bf16[528,256]{1,0:T(8,128)(2,1)S(1)} %pack_far.1), channel_id=1, source_target_pairs={{0,24},{8,16},{16,8},{24,0},{1,25},{9,17},{17,9},{25,1},{2,26},{10... | collective-permute-start | bytes 811016 | tf_op jit(solution)/shard_map/ppermute | solution.py:250
  5.6 1.3 %pack.1 = (bf16[528,256]{1,0:T(8,128)(2,1)S(1)}, bf16[528,256]{1,0:T(8,128)(2,1)S(1)}, bf16[528,256]{1,0:T(8,128)(2,1)S(1)}, f32[1,128]{1,0:T(1,128)S(1)}, f32[1,128]{1,0:T(1,128)S(1)}) custom-call(bf16[1,128,2048]{2,1,0:T(8,128)(2,1)} %refs_0_.5, bf16[1,128,2048]{2,1,0:T(8,128)(2,1)} %refs_1_.5, bf16[1,128,2048]{2,1,0:T(8,128)(2,1)} %refs_2_.5, ...), custom_call_target="tpu_custom_call" | custom-call | tf_op jit(solution)/shard_map/pack/pallas_call | solution.py:84
  6.9 0.6 %collective-permute-start.3 = (bf16[528,256]{1,0:T(8,128)(2,1)S(1)}, bf16[528,256]{1,0:T(8,128)(2,1)S(1)}, u32[]{:S(2)}, u32[]{:S(2)}) collective-permute-start(bf16[528,256]{1,0:T(8,128)(2,1)S(1)} %get-tuple-element.40), channel_id=1, source_target_pairs={{0,8},{8,0},{16,24},{24,16},{1,9},{9,1},{17,25},{25,17},{2,10},{10... | collective-permute-start | bytes 811016 | tf_op jit(solution)/shard_map/ppermute | solution.py:250
  7.5 0.1 collective-permute-start.4
  7.6 1.4 %pack_next.1 = (bf16[512,256]{1,0:T(8,128)(2,1)S(1)}, bf16[512,256]{1,0:T(8,128)(2,1)S(1)}, bf16[512,256]{1,0:T(8,128)(2,1)S(1)}, bf16[512,256]{1,0:T(8,128)(2,1)S(1)}) custom-call(bf16[1,128,2048]{2,1,0:T(8,128)(2,1)} %refs_0_.5, bf16[1,128,2048]{2,1,0:T(8,128)(2,1)} %refs_1_.5, bf16[1,128,2048]{2,1,0:T(8,128)(2,1)} %refs_2_.5, bf16[1,128,2048]{2,1,0:T(8,128)(2,1)} %refs_3_.5), custom_call_target="tpu_custom_call" | custom-call | tf_op jit(solution)/shard_map/pack_next/pallas_call | solution.py:84
  9.0 2.0 %collective-permute-start = (bf16[512,256]{1,0:T(8,128)(2,1)S(1)}, bf16[512,256]{1,0:T(8,128)(2,1)S(1)}, u32[]{:S(2)}, u32[]{:S(2)}) collective-permute-start(bf16[512,256]{1,0:T(8,128)(2,1)S(1)} %get-tuple-element.36), channel_id=1, source_target_pairs={{0,8},{8,0},{16,24},{24,16},{1,9},{9,1},{17,25},{25,17},{2,10},{10... | collective-permute-start | bytes 786440 | tf_op jit(solution)/shard_map/ppermute | solution.py:250
  11.0 1.5 %collective-permute-start.1 = (bf16[512,256]{1,0:T(8,128)(2,1)S(1)}, bf16[512,256]{1,0:T(8,128)(2,1)S(1)}, u32[]{:S(2)}, u32[]{:S(2)}) collective-permute-start(bf16[512,256]{1,0:T(8,128)(2,1)S(1)} %get-tuple-element.37), channel_id=1, source_target_pairs={{0,16},{8,24},{16,0},{24,8},{1,17},{9,25},{17,1},{25,9},{2,18},{10... | collective-permute-start | bytes 786440 | tf_op jit(solution)/shard_map/ppermute | solution.py:250
  12.5 0.5 collective-permute-done.5.refs_7_.refs_3_
  13.0 3.0 %collective-permute-start.2 = (bf16[512,256]{1,0:T(8,128)(2,1)S(1)}, bf16[512,256]{1,0:T(8,128)(2,1)S(1)}, u32[]{:S(2)}, u32[]{:S(2)}) collective-permute-start(bf16[512,256]{1,0:T(8,128)(2,1)S(1)} %get-tuple-element.38), channel_id=1, source_target_pairs={{0,24},{8,16},{16,8},{24,0},{1,25},{9,17},{17,9},{25,1},{2,26},{10... | collective-permute-start | bytes 786440 | tf_op jit(solution)/shard_map/ppermute | solution.py:250
  15.9 3.4 %collective-permute-done.3.refs_5_.refs_1_ = bf16[528,256]{1,0:T(8,128)(2,1)S(1)} collective-permute-done((bf16[528,256]{1,0:T(8,128)(2,1)S(1)}, bf16[528,256]{1,0:T(8,128)(2,1)S(1)}, u32[]{:S(2)}, u32[]{:S(2)}) %collective-permute-start.3) | collective-permute-done | bytes 270368 | tf_op jit(solution)/shard_map/ppermute | solution.py:250
  19.3 2.7 %attend0.1 = (bf16[512,256]{1,0:T(8,128)(2,1)S(1)}, bf16[512,256]{1,0:T(8,128)(2,1)S(1)}, bf16[512,256]{1,0:T(8,128)(2,1)S(1)}, bf16[512,256]{1,0:T(8,128)(2,1)S(1)}, f32[2,128]{1,0:T(2,128)S(1)}) custom-call(bf16[528,256]{1,0:T(8,128)(2,1)S(1)} %get-tuple-element.39.refs_4_.refs_0_, bf16[528,256]{1,0:T(8,128)(2,1)S(1)} %collective-permute-done.3.refs_5_.refs_1_, ...), custom_call_target="tpu_custom_call" | custom-call | flops 805306368 | bytes 2097152 | tf_op jit(solution)/shard_map/attend0/pallas_call | solution.py:231
  22.0 1.6 %collective-permute-start.9 = (bf16[512,256]{1,0:T(8,128)(2,1)S(1)}, bf16[512,256]{1,0:T(8,128)(2,1)S(1)}, u32[]{:S(2)}, u32[]{:S(2)}) collective-permute-start(bf16[512,256]{1,0:T(8,128)(2,1)S(1)} %get-tuple-element.51), channel_id=1, source_target_pairs={{0,8},{8,0},{16,24},{24,16},{1,9},{9,1},{17,25},{25,17},{2,10},{10... | collective-permute-start | bytes 786440 | tf_op jit(solution)/shard_map/ppermute | solution.py:250
  23.6 0.5 collective-permute-start.10
  24.0 0.9 %collective-permute-done.refs_1_ = bf16[512,256]{1,0:T(8,128)(2,1)S(1)} collective-permute-done((bf16[512,256]{1,0:T(8,128)(2,1)S(1)}, bf16[512,256]{1,0:T(8,128)(2,1)S(1)}, u32[]{:S(2)}, u32[]{:S(2)}) %collective-permute-start) | collective-permute-done | bytes 262176 | tf_op jit(solution)/shard_map/ppermute | solution.py:250
  24.9 1.4 %collective-permute-start.11 = (bf16[512,256]{1,0:T(8,128)(2,1)S(1)}, bf16[512,256]{1,0:T(8,128)(2,1)S(1)}, u32[]{:S(2)}, u32[]{:S(2)}) collective-permute-start(bf16[512,256]{1,0:T(8,128)(2,1)S(1)} %get-tuple-element.53), channel_id=1, source_target_pairs={{0,24},{8,16},{16,8},{24,0},{1,25},{9,17},{17,9},{25,1},{2,26},{10... | collective-permute-start | bytes 786440 | tf_op jit(solution)/shard_map/ppermute | solution.py:250
  26.3 0.0 collective-permute-done.1.refs_2_
  26.3 3.7 %collective-permute-done.2.refs_3_ = bf16[512,256]{1,0:T(8,128)(2,1)S(1)} collective-permute-done((bf16[512,256]{1,0:T(8,128)(2,1)S(1)}, bf16[512,256]{1,0:T(8,128)(2,1)S(1)}, u32[]{:S(2)}, u32[]{:S(2)}) %collective-permute-start.2) | collective-permute-done | bytes 262176 | tf_op jit(solution)/shard_map/ppermute | solution.py:250
  30.0 2.7 %attend1.1 = (bf16[512,256]{1,0:T(8,128)(2,1)S(1)}, bf16[512,256]{1,0:T(8,128)(2,1)S(1)}, bf16[512,256]{1,0:T(8,128)(2,1)S(1)}, bf16[512,256]{1,0:T(8,128)(2,1)S(1)}, f32[2,128]{1,0:T(2,128)S(1)}) custom-call(bf16[512,256]{1,0:T(8,128)(2,1)S(1)} %get-tuple-element.35.refs_0_, bf16[512,256]{1,0:T(8,128)(2,1)S(1)} %collective-permute-done.refs_1_, ...), custom_call_target="tpu_custom_call" | custom-call | flops 805306368 | bytes 2097152 | tf_op jit(solution)/shard_map/attend1/pallas_call | solution.py:231
  32.7 2.1 %collective-permute-start.6 = (bf16[512,256]{1,0:T(8,128)(2,1)S(1)}, bf16[512,256]{1,0:T(8,128)(2,1)S(1)}, u32[]{:S(2)}, u32[]{:S(2)}) collective-permute-start(bf16[512,256]{1,0:T(8,128)(2,1)S(1)} %get-tuple-element.44), channel_id=1, source_target_pairs={{0,8},{8,0},{16,24},{24,16},{1,9},{9,1},{17,25},{25,17},{2,10},{10... | collective-permute-start | bytes 786440 | tf_op jit(solution)/shard_map/ppermute | solution.py:250
  34.8 1.5 %collective-permute-start.7 = (bf16[512,256]{1,0:T(8,128)(2,1)S(1)}, bf16[512,256]{1,0:T(8,128)(2,1)S(1)}, u32[]{:S(2)}, u32[]{:S(2)}) collective-permute-start(bf16[512,256]{1,0:T(8,128)(2,1)S(1)} %get-tuple-element.45), channel_id=1, source_target_pairs={{0,16},{8,24},{16,0},{24,8},{1,17},{9,25},{17,1},{25,9},{2,18},{10... | collective-permute-start | bytes 786440 | tf_op jit(solution)/shard_map/ppermute | solution.py:250
  36.3 0.0 collective-permute-done.9.refs_2_
  36.3 1.3 %collective-permute-start.8 = (bf16[512,256]{1,0:T(8,128)(2,1)S(1)}, bf16[512,256]{1,0:T(8,128)(2,1)S(1)}, u32[]{:S(2)}, u32[]{:S(2)}) collective-permute-start(bf16[512,256]{1,0:T(8,128)(2,1)S(1)} %get-tuple-element.46), channel_id=1, source_target_pairs={{0,24},{8,16},{16,8},{24,0},{1,25},{9,17},{17,9},{25,1},{2,26},{10... | collective-permute-start | bytes 786440 | tf_op jit(solution)/shard_map/ppermute | solution.py:250
  37.6 0.6 %add_parts.1 = f32[32,2,128]{2,1,0:T(2,128)} custom-call(f32[2,128]{1,0:T(2,128)S(1)} %get-tuple-element.47.refs_0_, f32[2,128]{1,0:T(2,128)S(1)} %get-tuple-element.48.refs_1_), custom_call_target="tpu_custom_call" | custom-call | tf_op jit(solution)/shard_map/add_parts/pallas_call | solution.py:263
  38.2 5.0 %all-to-all-start = ((f32[32,2,128]{2,1,0:T(2,128)}), f32[32,2,128]{2,1,0:T(2,128)S(1)}, u32[]{:S(2)}, u32[]{:S(2)}) async-start(f32[32,2,128]{2,1,0:T(2,128)} %add_parts.1), calls=%async_computation | async-start | bytes 65536 | tf_op jit(solution)/shard_map/all_to_all | solution.py:311
  43.3 0.0 collective-permute-done.11.refs_4_
  43.3 1.2 %unpack.1 = (bf16[1,128,2048]{2,1,0:T(8,128)(2,1)}, bf16[1,128,2048]{2,1,0:T(8,128)(2,1)}, bf16[1,128,2048]{2,1,0:T(8,128)(2,1)}, bf16[1,128,2048]{2,1,0:T(8,128)(2,1)}) custom-call(bf16[512,256]{1,0:T(8,128)(2,1)S(1)} %get-tuple-element.49.refs_0_, bf16[512,256]{1,0:T(8,128)(2,1)S(1)} %get-tuple-element.50.refs_1_, ...), custom_call_target="tpu_custom_call" | custom-call | tf_op jit(solution)/shard_map/unpack/pallas_call | solution.py:145
  44.5 7.8 %all-to-all-done.refs_3_ = f32[32,2,128]{2,1,0:T(2,128)S(1)} async-done(((f32[32,2,128]{2,1,0:T(2,128)}), f32[32,2,128]{2,1,0:T(2,128)S(1)}, u32[]{:S(2)}, u32[]{:S(2)}) %all-to-all-start) | async-done | bytes 32800 | tf_op jit(solution)/shard_map/all_to_all | solution.py:311
  52.3 0.0 collective-permute-done.6.refs_0_
  52.3 0.0 collective-permute-done.7.refs_1_
  52.3 0.0 collective-permute-done.8.refs_2_
  52.3 1.0 %unpack_last.1 = (bf16[1,128,2048]{2,1,0:T(8,128)(2,1)}, bf16[1,128,2048]{2,1,0:T(8,128)(2,1)}, bf16[1,128,2048]{2,1,0:T(8,128)(2,1)}, bf16[1,128,2048]{2,1,0:T(...) custom-call(bf16[512,256]{1,0:T(8,128)(2,1)S(1)} %collective-permute, ...), custom_call_target="tpu_custom_call", output_to_operand_aliasing={{0}: (4, {}), {1}: (5, {}), {2}: (6, {}), {3}: (7, {})} | custom-call | tf_op jit(solution)/shard_map/unpack_last/pallas_call | solution.py:145
  (2 shorter events, 0.0 us)
Async XLA Ops:
  1.6 11.3 %collective-permute-start.5 = (bf16[528,256]{1,0:T(8,128)(2,1)S(1)}, bf16[528,256]{1,0:T(8,128)(2,1)S(1)}, u32[]{:S(2)}, u32[]{:S(2)}) collective-permute-start(bf16[528,256]{1,0:T(8,128)(2,1)S(1)} %pack_far.1), channel_id=1, source_target_pairs={{0,24},{8,16},{16,8},{24,0},{1,25},{9,17},{17,9},{25,1},{2,26},{10... | collective-permute-start | bytes 811016 | tf_op jit(solution)/shard_map/ppermute | solution.py:250
  6.9 12.4 %collective-permute-start.3 = (bf16[528,256]{1,0:T(8,128)(2,1)S(1)}, bf16[528,256]{1,0:T(8,128)(2,1)S(1)}, u32[]{:S(2)}, u32[]{:S(2)}) collective-permute-start(bf16[528,256]{1,0:T(8,128)(2,1)S(1)} %get-tuple-element.40), channel_id=1, source_target_pairs={{0,8},{8,0},{16,24},{24,16},{1,9},{9,1},{17,25},{25,17},{2,10},{10... | collective-permute-start | bytes 811016 | tf_op jit(solution)/shard_map/ppermute | solution.py:250
  7.5 11.8 %collective-permute-start.4 = (bf16[528,256]{1,0:T(8,128)(2,1)S(1)}, bf16[528,256]{1,0:T(8,128)(2,1)S(1)}, u32[]{:S(2)}, u32[]{:S(2)}) collective-permute-start(bf16[528,256]{1,0:T(8,128)(2,1)S(1)} %get-tuple-element.41), channel_id=1, source_target_pairs={{0,16},{8,24},{16,0},{24,8},{1,17},{9,25},{17,1},{25,9},{2,18},{10... | collective-permute-start | bytes 811016 | tf_op jit(solution)/shard_map/ppermute | solution.py:250
  9.0 16.0 %collective-permute-start = (bf16[512,256]{1,0:T(8,128)(2,1)S(1)}, bf16[512,256]{1,0:T(8,128)(2,1)S(1)}, u32[]{:S(2)}, u32[]{:S(2)}) collective-permute-start(bf16[512,256]{1,0:T(8,128)(2,1)S(1)} %get-tuple-element.36), channel_id=1, source_target_pairs={{0,8},{8,0},{16,24},{24,16},{1,9},{9,1},{17,25},{25,17},{2,10},{10... | collective-permute-start | bytes 786440 | tf_op jit(solution)/shard_map/ppermute | solution.py:250
  11.0 15.4 %collective-permute-start.1 = (bf16[512,256]{1,0:T(8,128)(2,1)S(1)}, bf16[512,256]{1,0:T(8,128)(2,1)S(1)}, u32[]{:S(2)}, u32[]{:S(2)}) collective-permute-start(bf16[512,256]{1,0:T(8,128)(2,1)S(1)} %get-tuple-element.37), channel_id=1, source_target_pairs={{0,16},{8,24},{16,0},{24,8},{1,17},{9,25},{17,1},{25,9},{2,18},{10... | collective-permute-start | bytes 786440 | tf_op jit(solution)/shard_map/ppermute | solution.py:250
  13.0 17.1 %collective-permute-start.2 = (bf16[512,256]{1,0:T(8,128)(2,1)S(1)}, bf16[512,256]{1,0:T(8,128)(2,1)S(1)}, u32[]{:S(2)}, u32[]{:S(2)}) collective-permute-start(bf16[512,256]{1,0:T(8,128)(2,1)S(1)} %get-tuple-element.38), channel_id=1, source_target_pairs={{0,24},{8,16},{16,8},{24,0},{1,25},{9,17},{17,9},{25,1},{2,26},{10... | collective-permute-start | bytes 786440 | tf_op jit(solution)/shard_map/ppermute | solution.py:250
  22.0 14.3 %collective-permute-start.9 = (bf16[512,256]{1,0:T(8,128)(2,1)S(1)}, bf16[512,256]{1,0:T(8,128)(2,1)S(1)}, u32[]{:S(2)}, u32[]{:S(2)}) collective-permute-start(bf16[512,256]{1,0:T(8,128)(2,1)S(1)} %get-tuple-element.51), channel_id=1, source_target_pairs={{0,8},{8,0},{16,24},{24,16},{1,9},{9,1},{17,25},{25,17},{2,10},{10... | collective-permute-start | bytes 786440 | tf_op jit(solution)/shard_map/ppermute | solution.py:250
  23.6 19.7 %collective-permute-start.10 = (bf16[512,256]{1,0:T(8,128)(2,1)S(1)}, bf16[512,256]{1,0:T(8,128)(2,1)S(1)}, u32[]{:S(2)}, u32[]{:S(2)}) collective-permute-start(bf16[512,256]{1,0:T(8,128)(2,1)S(1)} %get-tuple-element.52), channel_id=1, source_target_pairs={{0,16},{8,24},{16,0},{24,8},{1,17},{9,25},{17,1},{25,9},{2,18},{10... | collective-permute-start | bytes 786440 | tf_op jit(solution)/shard_map/ppermute | solution.py:250
  24.9 18.3 %collective-permute-start.11 = (bf16[512,256]{1,0:T(8,128)(2,1)S(1)}, bf16[512,256]{1,0:T(8,128)(2,1)S(1)}, u32[]{:S(2)}, u32[]{:S(2)}) collective-permute-start(bf16[512,256]{1,0:T(8,128)(2,1)S(1)} %get-tuple-element.53), channel_id=1, source_target_pairs={{0,24},{8,16},{16,8},{24,0},{1,25},{9,17},{17,9},{25,1},{2,26},{10... | collective-permute-start | bytes 786440 | tf_op jit(solution)/shard_map/ppermute | solution.py:250
  32.7 19.6 %collective-permute-start.6 = (bf16[512,256]{1,0:T(8,128)(2,1)S(1)}, bf16[512,256]{1,0:T(8,128)(2,1)S(1)}, u32[]{:S(2)}, u32[]{:S(2)}) collective-permute-start(bf16[512,256]{1,0:T(8,128)(2,1)S(1)} %get-tuple-element.44), channel_id=1, source_target_pairs={{0,8},{8,0},{16,24},{24,16},{1,9},{9,1},{17,25},{25,17},{2,10},{10... | collective-permute-start | bytes 786440 | tf_op jit(solution)/shard_map/ppermute | solution.py:250
  34.8 17.5 %collective-permute-start.7 = (bf16[512,256]{1,0:T(8,128)(2,1)S(1)}, bf16[512,256]{1,0:T(8,128)(2,1)S(1)}, u32[]{:S(2)}, u32[]{:S(2)}) collective-permute-start(bf16[512,256]{1,0:T(8,128)(2,1)S(1)} %get-tuple-element.45), channel_id=1, source_target_pairs={{0,16},{8,24},{16,0},{24,8},{1,17},{9,25},{17,1},{25,9},{2,18},{10... | collective-permute-start | bytes 786440 | tf_op jit(solution)/shard_map/ppermute | solution.py:250
  36.3 16.0 %collective-permute-start.8 = (bf16[512,256]{1,0:T(8,128)(2,1)S(1)}, bf16[512,256]{1,0:T(8,128)(2,1)S(1)}, u32[]{:S(2)}, u32[]{:S(2)}) collective-permute-start(bf16[512,256]{1,0:T(8,128)(2,1)S(1)} %get-tuple-element.46), channel_id=1, source_target_pairs={{0,24},{8,16},{16,8},{24,0},{1,25},{9,17},{17,9},{25,1},{2,26},{10... | collective-permute-start | bytes 786440 | tf_op jit(solution)/shard_map/ppermute | solution.py:250
  38.2 14.0 %all-to-all-start = ((f32[32,2,128]{2,1,0:T(2,128)}), f32[32,2,128]{2,1,0:T(2,128)S(1)}, u32[]{:S(2)}, u32[]{:S(2)}) async-start(f32[32,2,128]{2,1,0:T(2,128)} %add_parts.1), calls=%async_computation | async-start | bytes 65536 | tf_op jit(solution)/shard_map/all_to_all | solution.py:311
